TPU v7x, 32 devices: a whole 2x2x4 slice. The times are simulated.
32 devices in a mesh: stretch: 4 (over x, core), stream: 8 (over z, y).
Axes of the slice: x: 2, y: 2, z: 4, core: 2. Of those that a mesh axis runs over, the one named last changes fastest.
Arguments:
- inputs: bfloat16 [2, 8, 1024, 2304], P(None, 'stream', 'stretch'), may hold values from -6 to 6
- weight: bfloat16 [4608, 6912], P('stream'), may hold values from -0.09375 to 0.09375
- bias: float32 [6912], replicated, may hold values from -6 to 10
- reset: int32 [2, 8, 1024], P(None, 'stream', 'stretch'), may hold values from 0 to 1
- cotangent: bfloat16 [2, 8, 1024, 2304], P(None, 'stream', 'stretch'), may hold values from -6 to 6
Outputs:
- hidden: bfloat16 [2, 8, 1024, 2304], P(None, 'stream', 'stretch')
- grad_inputs: float32 [2, 8, 1024, 2304], P(None, 'stream', 'stretch')
- grad_weight: float32 [4608, 6912], P('stream')
- grad_bias: float32 [6912], replicated
All inputs are finite; a program needn't handle non-finite values.
Results may differ from a plain program's by a relative error of at most 0.0029.
Values may be sent and summed in bfloat16 or wider, within the bound.
No kernel may reach another device: no remote copies, remote signals or barrier semaphores. Data moves between devices by JAX's collectives and lax.ppermute only.
A program may use at most 512 MiB of HBM per device.

v0:
```python
import jax
import jax.numpy as jnp
from jax import lax
from jax.sharding import PartitionSpec as P


def shifted(value, axis, steps):
    count = lax.axis_size(axis)
    first, last = (max(0, -steps), min(count, count - steps))
    return lax.ppermute(value, axis, [(source, source + steps) for source in range(first, last)])


def prefix(part, axis, combine, identity, reverse):
    count = lax.axis_size(axis)
    place = lax.axis_index(axis)
    ahead = count - 1 - place if reverse else place
    gathered = jax.tree.map(lambda a: lax.all_gather(a, axis), part)
    state = jax.tree.map(lambda a, e: jnp.zeros_like(a) + jnp.asarray(e, a.dtype), part, identity)

    def one(lap, state):
        source = count - 1 - lap if reverse else lap
        return combine(
            state, jax.tree.map(lambda a: lax.dynamic_index_in_dim(a, source, 0, False), gathered)
        )

    return lax.fori_loop(0, ahead, one, state)


def compose(first, second):
    return (first[0] * second[0], first[1] * second[0] + second[1])


def shards(inputs, weight, bias, reset, cotangent):
    batches, _, rows, width = inputs.shape
    tokens = inputs.reshape(batches, rows, width)
    gate_cols = weight.shape[1]
    count_rows = batches * rows
    rim_in = shifted(tokens[:, -1, :], "stretch", 1)
    before = jnp.concatenate([rim_in[:, None, :], tokens[:, :-1, :]], axis=1)
    stacked = jnp.concatenate([tokens, before], axis=2).reshape(count_rows, 2 * width)
    whole_weight = lax.all_gather(weight, "stream", axis=0, tiled=True)
    gates = jnp.dot(stacked, whole_weight, preferred_element_type=jnp.float32)
    gates = (gates + bias).reshape(batches, rows, gate_cols)
    cand = jnp.tanh(gates[..., :width])
    forget = jax.nn.sigmoid(gates[..., width : 2 * width])
    outgate = jax.nn.sigmoid(gates[..., 2 * width :])
    keep = 1.0 - reset.reshape(batches, rows).astype(jnp.float32)
    decay = forget * keep[..., None]
    inject = (1.0 - forget) * cand
    prod_all, local_state = lax.associative_scan(compose, (decay, inject), axis=1)
    ones_row = jnp.ones((batches, width), jnp.float32)
    zeros_row = jnp.zeros((batches, width), jnp.float32)
    entering = prefix(
        (prod_all[:, -1], local_state[:, -1]), "stretch", compose, (ones_row, zeros_row), False
    )
    state_in = entering[1]
    cell = local_state + prod_all * state_in[:, None, :]
    hidden = (outgate * cell).astype(jnp.bfloat16).reshape(inputs.shape)
    grad_h = cotangent.reshape(batches, rows, width).astype(jnp.float32)
    seed = grad_h * outgate
    next_decay = jnp.concatenate([decay[:, 1:], ones_row[:, None, :]], axis=1)
    prod_back, local_adj = lax.associative_scan(
        compose, (next_decay[:, ::-1], seed[:, ::-1]), axis=1
    )
    prod_back = prod_back[:, ::-1]
    local_adj = local_adj[:, ::-1]
    leaving = (decay[:, 0] * prod_back[:, 0], decay[:, 0] * local_adj[:, 0])
    incoming = prefix(leaving, "stretch", compose, (ones_row, zeros_row), True)
    adjoint = local_adj + prod_back * incoming[1][:, None, :]
    prev_cell = jnp.concatenate([state_in[:, None, :], cell[:, :-1]], axis=1)
    d_cand = adjoint * (1.0 - forget) * (1.0 - cand * cand)
    d_forget = adjoint * (keep[..., None] * prev_cell - cand) * forget * (1.0 - forget)
    d_out = grad_h * cell * outgate * (1.0 - outgate)
    d_gates = (
        jnp.concatenate([d_cand, d_forget, d_out], axis=2)
        .astype(jnp.bfloat16)
        .reshape(count_rows, gate_cols)
    )
    contract_cols = (((1,), (1,)), ((), ()))
    d_stacked = lax.dot_general(
        d_gates, whole_weight, contract_cols, preferred_element_type=jnp.float32
    )
    d_stacked = d_stacked.reshape(batches, rows, 2 * width)
    rim_back = shifted(d_stacked[:, 0, width:], "stretch", -1)
    later_tap = jnp.concatenate([d_stacked[:, 1:, width:], rim_back[:, None, :]], axis=1)
    grad_inputs = (d_stacked[..., :width] + later_tap).reshape(inputs.shape)
    contract_rows = (((0,), (0,)), ((), ()))
    grad_weight = lax.psum_scatter(
        lax.dot_general(stacked, d_gates, contract_rows, preferred_element_type=jnp.float32),
        "stream",
        scatter_dimension=0,
        tiled=True,
    )
    grad_weight = lax.psum(grad_weight, "stretch")
    bias_part = jnp.sum(d_gates, axis=0, dtype=jnp.float32)
    grad_bias = lax.psum(bias_part, ("stretch", "stream"))
    return (hidden, grad_inputs, grad_weight, grad_bias)


def solution(mesh):
    in_specs = (
        P(None, "stream", "stretch", None),
        P("stream", None),
        P(),
        P(None, "stream", "stretch"),
        P(None, "stream", "stretch", None),
    )
    out_specs = (
        P(None, "stream", "stretch", None),
        P(None, "stream", "stretch", None),
        P("stream", None),
        P(),
    )
    return jax.shard_map(shards, mesh=mesh, in_specs=in_specs, out_specs=out_specs, check_vma=False)
```

profile of v0, /device:TPU:0, one launch (start us, length us, event | category | flops | bytes accessed | tf_op | source)
XLA Modules:
  0.0 4263.2 jit_solution(12222642338597610584)
XLA Ops:
  22.8 1192.5 %all-gather.6.cloned.1.call-done = bf16[4608,6912]{1,0:T(8,128)(2,1)} async-done(((bf16[576,6912]{1,0:T(8,128)(2,1)}), bf16[4608,6912]{1,0:T(8,128)(2,1)}) %all-gather.6.cloned.1.call-update) | async-done | bytes 63701008 | tf_op jit(solution)/shard_map/all_gather | solution.py:41
  1215.3 43.7 %convolution_add_fusion = f32[512,6912]{1,0:T(8,128)} fusion(bf16[4608,6912]{1,0:T(8,128)(2,1)} %all-gather.6.cloned.1.call-done, f32[6912]{0:T(1024)} %param.11, bf16[512,2304]{1,0:T(8,128)(2,1)} %bitcast.85, bf16[512,2304]{1,0:T(8,128)(2,1)} %bitcast.84), kind=kOutput, calls=%fused_computation.8 | convolution fusion | flops 32627884032 | bytes 82603008 | tf_op jit(solution)/shard_map/dot_general | solution.py:42
  1267.8 10.2 slice.587
  1278.0 9.9 slice.532
  1288.0 9.9 slice.530
  1299.4 10.2 slice.586
  1309.6 9.9 slice.535
  1319.6 9.9 slice.531
  1430.7 10.6 pad.213
  1449.5 10.7 pad.228
  1474.0 13.2 fusion.4
  1490.0 9.9 slice.669
  1508.2 9.9 slice.606
  1523.3 9.9 slice.667
  1543.1 9.9 slice.609
  1553.1 18.7 slice.607
  1571.8 11.7 slice.612
  1583.5 18.9 slice.610
  1602.4 11.8 slice.616
  1693.7 11.9 slice.670
  1705.7 19.0 slice.668
  1773.4 10.5 pad.244
  1790.5 10.7 pad.261
  1819.9 36.6 rev.8
  1856.5 36.4 rev.9
  1904.7 16.2 multiply_convert_fusion
  1920.9 50.9 %convolution_bitcast_fusion = f32[4608,6912]{1,0:T(8,128)} fusion(bf16[2,255,2304]{1,2,0:T(8,128)(2,1)S(1)} %bitcast.80, bf16[2,1,2304]{1,2,0:T(8,128)(2,1)S(1)} %copy-done.32, bf16[2,256,2304]{1,2,0:T(8,128)(2,1)S(1)} %bitcast.79, bf16[2,256,2304]{2,1,0:T(8,128)(2,1)} %get-tuple-element.170, bf16[2,256,2304]{2,1,0:T(8,128)(2,1)} %get-tuple-element.173, ...), kind=kOutput, calls=%fused_computation.4 | convolution fusion | flops 32650297344 | bytes 139198464 | tf_op jit(solution)/shard_map/dot_general | solution.py:89
  1971.9 1995.8 %reduce-scatter.2.cloned.1.call-done = f32[576,6912]{1,0:T(8,128)} async-done(((f32[4608,6912]{1,0:T(8,128)}), f32[576,6912]{1,0:T(8,128)}) %reduce-scatter.2.cloned.1.call-update) | async-done | bytes 15925264 | tf_op jit(solution)/shard_map/reduce_scatter | solution.py:88
  3969.3 40.6 fusion
  4020.8 42.1 psum.15
  4070.0 175.4 %all-reduce.68.cloned.1.call-done = f32[576,6912]{1,0:T(8,128)} async-done(((f32[576,6912]{1,0:T(8,128)}), f32[576,6912]{1,0:T(8,128)}) %all-reduce.68.cloned.1.call-update) | async-done | bytes 15925264 | tf_op jit(solution)/shard_map/psum | solution.py:94
  4245.4 11.1 copy.114
  (433 shorter events, 358.8 us)
Async XLA Ops:
  7.2 1208.1 %all-gather.6.cloned.1.call-start = ((), (), s32[]{:S(2)}) async-start(), calls=%async_computation.1 | async-start | bytes 71663616 | tf_op jit(solution)/shard_map/all_gather | solution.py:41
  7.9 6.1 copy-start.73
  7.9 3959.8 %reduce-scatter.2.cloned.1.call-start = ((), (), s32[]{:S(2)}) async-start(), calls=%async_computation.2 | async-start | bytes 143327232 | tf_op jit(solution)/shard_map/reduce_scatter | solution.py:88
  10.8 7.1 copy-start.11
  11.6 3.2 collective-permute-start
  14.0 1244.9 %copy-start.71 = (f32[2,1,256]{2,0,1:T(2,128)}, f32[2,1,256]{2,0,1:T(2,128)S(1)}, u32[]{:S(2)}) copy-start(f32[2,1,256]{2,0,1:T(2,128)S(1)} %copy.44) | copy-start | bytes 6148
  1404.7 5.5 copy-start.29
  1430.7 17.2 copy-start.19
  1430.7 17.2 copy-start.49
  1449.5 10.7 copy-start.21
  1583.5 18.9 copy-start.24
  1627.2 7.3 copy-start.9
  1658.1 35.7 copy-start.23
  1705.7 19.1 copy-start.59
  1705.7 19.1 copy-start.60
  1705.7 19.2 copy-start.47
  1705.7 19.3 copy-start.46
  1705.7 19.3 copy-start.57
  1705.7 19.3 copy-start.58
  1705.7 19.5 copy-start.44
  1705.7 19.5 copy-start.45
  1705.7 19.6 copy-start.61
  1705.7 19.6 copy-start.62
  1790.5 10.8 copy-start.22
  1801.2 13.5 slice-start
  1807.9 6.9 slice-start.1
  1807.9 8.1 copy-start.8
  1856.5 48.2 %copy-start.72 = (f32[2,1,256]{2,0,1:T(2,128)S(1)}, f32[2,1,256]{2,0,1:T(2,128)}, u32[]{:S(2)}) copy-start(f32[2,1,256]{2,0,1:T(2,128)} %copy-done.71) | copy-start | bytes 6148
  1904.7 16.2 copy-start.12
  1904.7 16.2 copy-start.32
  1971.8 2273.6 %all-reduce.68.cloned.1.call-start = ((), (), s32[]{:S(2)}) async-start(), calls=%async_computation.3 | async-start | bytes 31850496 | tf_op jit(solution)/shard_map/psum | solution.py:94
  4010.9 52.1 %collective-permute-start.1 = (f32[2,2304]{1,0:T(2,128)S(1)}, f32[2,2304]{1,0:T(2,128)S(1)}, u32[]{:S(2)}, u32[]{:S(2)}) collective-permute-start(f32[2,2304]{1,0:T(2,128)S(1)} %bitcast.108), channel_id=1, source_target_pairs={{8,0},{16,8},{24,16},{9,1},{17,9},{25,17},{10,2},{18,10},{26,18},{... | collective-permute-start | bytes 55304 | tf_op jit(solution)/shard_map/ppermute | solution.py:10
  (49 other events, 97.9 us)
Sparse Core Ops, SparseCore 0:
  9.5 1205.6 all-gather.5
  1971.9 1995.6 reduce-scatter.1
  3970.3 275.0 all-reduce.67
where the time goes:
time: 4280 us; the launch traced here: 4260 us
  waiting for transfers between devices  3370 us (79%)
  local copies, waits for them, and re-layouts  553 us (13%)
  matrix products  135 us (3%)
  other arithmetic  127 us (3%)
  blocking collectives  63.2 us (1%)
    reduce_scatter x1, waiting for transfers between devices, shards(): lax.psum_scatter(lax.dot_general(stacked, d_gates, contract_rows, preferr...  2000 us
    all_gather x1, waiting for transfers between devices, shards(): whole_weight = lax.all_gather(weight, 'stream', axis=0, tiled=True)  1190 us
    slice x57, local copies, waits for them, and re-layouts, shards(): lax.associative_scan(compose, (next_decay[:, ::-1], seed[:, ::-1]), axis=1)  211 us
    psum x1, waiting for transfers between devices, shards(): grad_weight = lax.psum(grad_weight, 'stretch')  175 us
    slice x52, local copies, waits for them, and re-layouts, shards(): lax.associative_scan(compose, (decay, inject), axis=1)  99.9 us
  transfers between devices with their start and end apart: 5, of which 4 were waited for; matrix products, arithmetic and copies ran while one was open for 2% of the time, Pallas kernels for 0%

commit v1 on v0

v1 whole, which is shorter than its diff:
```python
import functools

import jax
import jax.numpy as jnp
from jax import lax
from jax.experimental import pallas as pl
from jax.experimental.pallas import tpu as pltpu
from jax.sharding import PartitionSpec as P

BF = jnp.bfloat16
F32 = jnp.float32
LANES = 128
VMEM_BYTES = 60 * 1024 * 1024


def any_spec():
    return pl.BlockSpec(memory_space=pl.ANY)


def vmem_spec():
    return pl.BlockSpec(memory_space=pltpu.VMEM)


def smem_spec():
    return pl.BlockSpec(memory_space=pltpu.SMEM)


def ring_order(count):
    inner = 1
    while (2 * inner) ** 2 <= count:
        inner *= 2
    outer = count // inner
    if inner == 1 or outer % 2:
        return list(range(count))
    order = [z * inner for z in range(outer)]
    for turn, z in enumerate(reversed(range(outer))):
        across = range(1, inner) if turn % 2 == 0 else reversed(range(1, inner))
        order += [z * inner + y for y in across]
    return order


def sigmoid(v):
    return 0.5 + 0.5 * jnp.tanh(0.5 * v)


def gates_kernel(rows, half, n_blocks, n_pieces, group, ids, *refs):
    x_refs = refs[:n_blocks]
    own_ref = refs[n_blocks]
    w_refs = refs[n_blocks + 1 : n_blocks + 1 + n_pieces]
    bias_ref, keep_ref, cot_ref = refs[n_blocks + 1 + n_pieces : n_blocks + 4 + n_pieces]
    hid_ref, dg_ref, db_ref = refs[n_blocks + 4 + n_pieces : n_blocks + 7 + n_pieces]
    x_buf, w_buf, gate_buf, cell_buf, adj_buf, x_sem, w_sem = refs[n_blocks + 7 + n_pieces :]
    time, width = x_buf.shape
    cols = gate_buf.shape[1]
    tile = w_buf.shape[2]
    batch = ids[0]

    def x_copy(i):
        start = pl.multiple_of(ids[1 + i] * rows, rows)
        return pltpu.make_async_copy(x_refs[i].at[batch], x_buf.at[pl.ds(start, rows), :], x_sem.at[i])

    def w_copies(col, size, slot):
        copies = []
        for i in range(n_pieces + 2):
            if i < 2:
                source = own_ref.at[i, :, pl.ds(col, size)]
                block = ids[1 + n_blocks] + i
            else:
                source = w_refs[i - 2].at[:, pl.ds(col, size)]
                block = ids[2 + n_blocks + i - 2]
            start = pl.multiple_of(block * half, half)
            copies.append(
                pltpu.make_async_copy(
                    source, w_buf.at[slot, pl.ds(start, half), pl.ds(0, size)], w_sem.at[slot, i]
                )
            )
        return copies

    full = cols // tile
    tail = cols - full * tile
    for i in range(n_blocks):
        x_copy(i).start()
    for copy in w_copies(0, tile, 0):
        copy.start()
    for i in range(n_blocks):
        x_copy(i).wait()
    row0 = lax.broadcasted_iota(jnp.int32, (time, 1), 0) == 0

    def product(slot, col, size):
        now = jnp.dot(x_buf[...], w_buf[slot, :width, :size], preferred_element_type=F32)
        prev = jnp.dot(x_buf[...], w_buf[slot, width:, :size], preferred_element_type=F32)
        prev = jnp.where(row0, 0.0, pltpu.roll(prev, 1, 0))
        gate_buf[:, pl.ds(col, size)] = now + prev + bias_ref[:, pl.ds(col, size)]

    @pl.loop(0, full)
    def _(n):
        slot = lax.rem(n, 2)

        @pl.when(n + 1 < full)
        def _():
            for copy in w_copies(pl.multiple_of((n + 1) * tile, tile), tile, 1 - slot):
                copy.start()

        if tail:

            @pl.when(n + 1 == full)
            def _():
                for copy in w_copies(full * tile, tail, 1 - slot):
                    copy.start()

        for copy in w_copies(pl.multiple_of(n * tile, tile), tile, slot):
            copy.wait()
        product(slot, pl.multiple_of(n * tile, tile), tile)

    if tail:
        for copy in w_copies(full * tile, tail, full % 2):
            copy.wait()
        product(full % 2, full * tile, tail)

    scan(time, group, gate_buf, keep_ref, cot_ref, cell_buf, adj_buf, hid_ref, dg_ref, db_ref)


STEP = 16


def scan(time, group, gate_buf, keep_ref, cot_ref, cell_buf, adj_buf, hid_ref, dg_ref, db_ref):
    steps = time // STEP
    sub = lax.broadcasted_iota(jnp.int32, (8, LANES), 0)
    zeros = jnp.zeros((8, LANES), F32)

    def down(a, d):
        return pltpu.roll(a, d, 0)

    def up(a, d):
        return pltpu.roll(a, 8 - d, 0)

    def spread(a, r):
        return jnp.broadcast_to(a[r : r + 1, :], (8, LANES))

    @pl.loop(0, group // LANES)
    def _(block):
        lane = pl.multiple_of(block * LANES, LANES)
        z_at = pl.ds(lane, LANES)
        f_at = pl.ds(pl.multiple_of(group + lane, LANES), LANES)
        o_at = pl.ds(pl.multiple_of(2 * group + lane, LANES), LANES)

        def forward(i, carry):
            at = pl.multiple_of(i * STEP, STEP)
            outs = []
            for h in range(STEP // 8):
                here = pl.ds(at + 8 * h, 8)
                cand = jnp.tanh(gate_buf[here, z_at])
                forget = sigmoid(gate_buf[here, f_at])
                outgate = sigmoid(gate_buf[here, o_at])
                a = forget * keep_ref[here, :]
                b = (1.0 - forget) * cand
                gate_buf[here, z_at] = cand
                gate_buf[here, f_at] = forget
                gate_buf[here, o_at] = outgate
                for d in (1, 2, 4):
                    inside = sub >= d
                    b = b + a * jnp.where(inside, down(b, d), 0.0)
                    a = a * jnp.where(inside, down(a, d), 1.0)
                cell = b + a * carry
                carry = spread(b, 7) + spread(a, 7) * carry
                cell_buf[here, :] = cell
                outs.append(outgate * cell)
            hid_ref[pl.ds(at, STEP), z_at] = jnp.concatenate(outs, axis=0).astype(BF)
            return carry

        lax.fori_loop(0, steps, forward, zeros, unroll=4)

        def backward(n, state):
            adj_in, decay_in, later, total = state
            i = steps - 1 - n
            at = pl.multiple_of(i * STEP, STEP)
            grads = cot_ref[pl.ds(at, STEP), z_at].astype(F32)
            parts = []
            for h in reversed(range(STEP // 8)):
                here = pl.ds(at + 8 * h, 8)
                cand = gate_buf[here, z_at]
                forget = gate_buf[here, f_at]
                outgate = gate_buf[here, o_at]
                keep = keep_ref[here, :]
                cell = cell_buf[here, :]
                first = at + 8 * h == 0
                before = cell_buf[pl.ds(jnp.maximum(at + 8 * h - 8, 0), 8), :]
                before = jnp.where(first, 0.0, before)
                prev = jnp.where(sub == 0, down(before, 1), down(cell, 1))
                g = grads[8 * h : 8 * h + 8]
                decay = forget * keep
                a = jnp.where(sub == 7, decay_in, up(decay, 1))
                b = g * outgate
                for d in (1, 2, 4):
                    inside = sub < 8 - d
                    b = b + a * jnp.where(inside, up(b, d), 0.0)
                    a = a * jnp.where(inside, up(a, d), 1.0)
                adj = b + a * adj_in
                adj_in = spread(b, 0) + spread(a, 0) * adj_in
                decay_in = spread(decay, 0)
                omf = 1.0 - forget
                scaled = adj * omf
                d_z = scaled * (1.0 - cand * cand)
                d_f = scaled * forget * (keep * prev - cand)
                d_o = g * cell * (outgate * (1.0 - outgate))
                parts.append((d_z, d_f, d_o))
            parts.reverse()
            new_later, new_total = [], []
            for gate, where in enumerate((z_at, f_at, o_at)):
                tiles = [part[gate].astype(BF) for part in parts]
                wide = [t.astype(F32) for t in tiles]
                dg_ref[0, pl.ds(at, STEP), where] = jnp.concatenate(tiles, axis=0)
                follow = wide[1:] + [None]
                moved = []
                for t, nxt in zip(wide, follow):
                    edge = later[gate] if nxt is None else spread(nxt, 0)
                    moved.append(jnp.where(sub == 7, edge, up(t, 1)))
                dg_ref[1, pl.ds(at, STEP), where] = jnp.concatenate(moved, axis=0).astype(BF)
                new_later.append(spread(wide[0], 0))
                new_total.append(total[gate] + functools.reduce(jnp.add, wide))
            return adj_in, decay_in, tuple(new_later), tuple(new_total)

        triple = (zeros, zeros, zeros)
        _, _, _, total = lax.fori_loop(0, steps, backward, (zeros, zeros, triple, triple), unroll=2)
        for gate, where in enumerate((z_at, f_at, o_at)):
            db_ref[:, where] = total[gate]


def gates_call(ids, blocks, own, pieces, bias, keep, cot, group):
    rows = blocks[0].shape[1]
    width = blocks[0].shape[2]
    half = own.shape[1]
    cols = own.shape[2]
    time = keep.shape[0]
    tile = min(256, cols)
    flops = 2 * time * 2 * width * cols
    kernel = functools.partial(gates_kernel, rows, half, len(blocks), len(pieces), group)
    return pl.pallas_call(
        kernel,
        out_shape=(
            jax.ShapeDtypeStruct((time, group), BF),
            jax.ShapeDtypeStruct((2, time, cols), BF),
            jax.ShapeDtypeStruct((8, cols), F32),
        ),
        in_specs=[smem_spec()]
        + [any_spec()] * (len(blocks) + 1 + len(pieces))
        + [vmem_spec()] * 3,
        out_specs=(vmem_spec(),) * 3,
        scratch_shapes=[
            pltpu.VMEM((time, width), BF),
            pltpu.VMEM((2, 2 * width, tile), BF),
            pltpu.VMEM((time, cols), F32),
            pltpu.VMEM((time, LANES), F32),
            pltpu.VMEM((time, LANES), F32),
            pltpu.SemaphoreType.DMA((len(blocks),)),
            pltpu.SemaphoreType.DMA((2, len(pieces) + 2)),
        ],
        compiler_params=pltpu.CompilerParams(vmem_limit_bytes=VMEM_BYTES),
        cost_estimate=pl.CostEstimate(
            flops=flops, bytes_accessed=2 * width * cols * 2 + time * width * 2 + time * cols * 6, transcendentals=0
        ),
        name="gates",
    )(ids, *blocks, own, *pieces, bias, keep, cot)


def inputs_kernel(half, n_pieces, chunk, groups, ids, *refs):
    dg_refs = refs[:groups]
    weights = [refs[groups + g * (n_pieces + 1) : groups + (g + 1) * (n_pieces + 1)] for g in range(groups)]
    mine_ref, all_ref = refs[groups + groups * (n_pieces + 1) : groups + groups * (n_pieces + 1) + 2]
    w_buf, acc, w_sem = refs[groups + groups * (n_pieces + 1) + 2 :]
    time, width = acc.shape

    def w_copies(g, col, size, slot):
        copies = []
        for i in range(n_pieces + 2):
            if i < 2:
                source = weights[g][0].at[i, :, pl.ds(col, size)]
                block = ids[1] + i
            else:
                source = weights[g][i - 1].at[:, pl.ds(col, size)]
                block = ids[2 + i - 2]
            start = pl.multiple_of(block * half, half)
            copies.append(
                pltpu.make_async_copy(
                    source, w_buf.at[slot, pl.ds(start, half), pl.ds(0, size)], w_sem.at[slot, i]
                )
            )
        return copies

    jobs = []
    for g in range(groups):
        cols = dg_refs[g].shape[2]
        col = 0
        while col < cols:
            size = min(chunk, cols - col)
            jobs.append((g, col, size))
            col += size
    step = 256 if width % 256 == 0 else LANES
    for copy in w_copies(*jobs[0], 0):
        copy.start()
    for n, (g, col, size) in enumerate(jobs):
        slot = n % 2
        if n + 1 < len(jobs):
            for copy in w_copies(*jobs[n + 1], 1 - slot):
                copy.start()
        for copy in w_copies(g, col, size, slot):
            copy.wait()

        @pl.loop(0, width // step)
        def _(k):
            at = pl.ds(pl.multiple_of(k * step, step), step)
            total = None if n == 0 else acc[:, at]
            for tap in range(2):
                rows = pl.ds(pl.multiple_of(tap * width + k * step, LANES), step)
                part = lax.dot_general(
                    dg_refs[g][tap, :, col : col + size],
                    w_buf[slot, rows, :size],
                    (((1,), (1,)), ((), ())),
                    preferred_element_type=F32,
                )
                total = part if total is None else total + part
            acc[:, at] = total

    own = mine_ref.shape[0]
    mine_ref[...] = acc[pl.ds(pl.multiple_of(ids[0] * own, own), own), :]
    all_ref[...] = acc[...].astype(BF)


def inputs_call(ids, dgs, weights, own_rows, width):
    groups = len(dgs)
    n_pieces = len(weights[0]) - 1
    half = weights[0][0].shape[1]
    time = dgs[0].shape[1]
    cols = sum(d.shape[2] for d in dgs)
    chunk = 512
    kernel = functools.partial(inputs_kernel, half, n_pieces, chunk, groups)
    flat = [w for group in weights for w in group]
    return pl.pallas_call(
        kernel,
        out_shape=(
            jax.ShapeDtypeStruct((own_rows, width), F32),
            jax.ShapeDtypeStruct((time, width), BF),
        ),
        in_specs=[smem_spec()] + [vmem_spec()] * groups + [any_spec()] * len(flat),
        out_specs=(vmem_spec(),) * 2,
        scratch_shapes=[
            pltpu.VMEM((2, 2 * width, chunk), BF),
            pltpu.VMEM((time, width), F32),
            pltpu.SemaphoreType.DMA((2, n_pieces + 2)),
        ],
        compiler_params=pltpu.CompilerParams(vmem_limit_bytes=VMEM_BYTES),
        cost_estimate=pl.CostEstimate(
            flops=2 * time * 2 * width * cols,
            bytes_accessed=2 * width * cols * 2 + time * cols * 4 + time * width * 4,
            transcendentals=0,
        ),
        name="grad_in",
    )(ids, *dgs, *flat)


def ring_kernel(n_received, ids, x_ref, mine_ref, other_ref, *refs):
    out_ref = refs[-1]
    total = jnp.dot(x_ref[0, 0], mine_ref[0], preferred_element_type=F32)
    total = total + jnp.dot(x_ref[1, 0], other_ref[0], preferred_element_type=F32)
    for ref in refs[:n_received]:
        total = total + ref[...].astype(F32)
    out_ref[...] = total.astype(out_ref.dtype)


def ring_call(ids, x_t, mine, other, received, tile, dtype):
    half, time = x_t.shape[2:]
    cols = mine.shape[2]
    flat = pl.BlockSpec((half, tile), lambda n, ids: (0, n))
    return pl.pallas_call(
        functools.partial(ring_kernel, len(received)),
        out_shape=jax.ShapeDtypeStruct((half, cols), dtype),
        grid_spec=pltpu.PrefetchScalarGridSpec(
            num_scalar_prefetch=1,
            grid=(cols // tile,),
            in_specs=[
                pl.BlockSpec((2, 1, half, time), lambda n, ids: (0, ids[0], 0, 0)),
                pl.BlockSpec((1, time, tile), lambda n, ids: (ids[1], 0, n)),
                pl.BlockSpec((1, time, tile), lambda n, ids: (ids[1], 0, n)),
            ]
            + [flat] * len(received),
            out_specs=flat,
        ),
        compiler_params=pltpu.CompilerParams(vmem_limit_bytes=VMEM_BYTES),
        cost_estimate=pl.CostEstimate(
            flops=4 * half * time * cols, bytes_accessed=4 * time * cols + 8 * half * cols, transcendentals=0
        ),
        name="grad_w",
    )(ids, x_t, mine, other, *received)


def shards(inputs, weight, bias, reset, cotangent):
    batches, _, rows, width = inputs.shape
    shard_rows, gate_cols = weight.shape
    n_stream = lax.axis_size("stream")
    n_stretch = lax.axis_size("stretch")
    n_x = n_stretch // 2
    time = rows * n_stretch
    half = shard_rows // 2
    per_tap = n_stream // 2
    feats = width // n_x
    s = lax.axis_index("stretch")
    p = lax.axis_index("stream")
    x, c = s // 2, lax.rem(s, 2)
    sign = 1 - 2 * c

    order = ring_order(n_stream)
    place_of = [order.index(i) for i in range(n_stream)]
    r = jnp.array(place_of, jnp.int32)[p]
    order_arr = jnp.array(order, jnp.int32)

    def owner(steps):
        return order_arr[lax.rem(r + sign * steps + n_stream, n_stream)]

    def ring_pairs(forward):
        pairs = []
        for st in range(n_stretch):
            up = (st % 2 == 0) == forward
            for i in range(n_stream):
                j = (place_of[i] + (1 if up else -1)) % n_stream
                pairs.append((st * n_stream + i, st * n_stream + order[j]))
        return pairs

    long_pairs, short_pairs = ring_pairs(True), ring_pairs(False)
    hops = n_stream // 2

    def ring(a, pairs):
        return lax.ppermute(a, ("stretch", "stream"), pairs)

    def to_core(a):
        return lax.ppermute(a, "stretch", [(i, i ^ 1) for i in range(n_stretch)])

    def to_x(a, k):
        return lax.ppermute(a, "stretch", [(i, i ^ (2 * k)) for i in range(n_stretch)])

    def by_x(options):
        out = options[0]
        for i in range(1, n_x):
            out = jnp.where(x == i, options[i], out)
        return out

    def by_core(first, second):
        return jnp.where(c == 0, first, second), jnp.where(c == 0, second, first)

    tiles = -(-feats // LANES)
    first = tiles // 2
    sizes = [first * LANES, (tiles - first) * LANES]
    starts = [0, first * LANES]

    def columns(a, start, size, gates=3):
        real = min(size, feats - start)
        options = []
        for i in range(n_x):
            parts = []
            for gate in range(gates):
                at = gate * width + i * feats + start
                part = a[..., at : at + real]
                if real < size:
                    part = jnp.pad(part, [(0, 0)] * (a.ndim - 1) + [(0, size - real)])
                parts.append(part)
            options.append(jnp.concatenate(parts, axis=-1) if gates > 1 else parts[0])
        return by_x(options)

    tokens = inputs.reshape(batches, rows, width)
    cots = cotangent.reshape(batches, rows, width)
    own_weights = [
        columns(weight, start, size).reshape(2, half, 3 * size) for start, size in zip(starts, sizes)
    ]
    from_x = [tokens] + [to_x(tokens, k) for k in range(1, n_x)]
    blocks = from_x + [to_core(b) for b in from_x]
    places = [(x ^ k) * 2 + c for k in range(n_x)] + [(x ^ k) * 2 + (1 - c) for k in range(n_x)]

    pieces, at_block = [], []
    for g, own in enumerate(own_weights):
        mine = lax.dynamic_index_in_dim(own, c, 0, False)
        forth = back = mine
        got = []
        for t in range(1, hops + 1):
            forth = ring(forth, long_pairs)
            got.append((forth, owner(-t), owner(t)))
            if t < hops:
                back = ring(back, short_pairs)
                got.append((back, owner(t), owner(-t)))
        group = []
        for piece, source, other in got:
            group += [piece, to_core(piece)]
            if g == 0:
                at_block += [2 * source + c, 2 * other + (1 - c)]
        pieces.append(group)

    cot_mine = lax.dynamic_index_in_dim(cots, c, 0, False)
    cot_other = to_core(lax.dynamic_index_in_dim(cots, 1 - c, 0, False))
    cot_pair = jnp.concatenate(by_core(cot_mine, cot_other), axis=0)
    cot_parts = [cot_pair[:, i * feats : (i + 1) * feats] for i in range(n_x)]
    cot_by_k = [by_x(cot_parts)]
    for k in range(1, n_x):
        cot_by_k.append(to_x(by_x([cot_parts[i ^ k] for i in range(n_x)]), k))
    cot_all = jnp.concatenate([by_x([cot_by_k[i ^ j] for j in range(n_x)]) for i in range(n_x)], axis=0)

    resets = lax.all_gather(reset.reshape(batches, rows).astype(F32), "stretch")
    keep = 1.0 - lax.dynamic_index_in_dim(resets, c, 1, False).reshape(time, 1)

    block_ids = jnp.stack([c] + places + [2 * p] + at_block).astype(jnp.int32)
    hiddens, dgs, biases = [], [], []
    for g, (start, size) in enumerate(zip(starts, sizes)):
        bias_g = columns(bias[None, :], start, size)
        real = min(size, feats - start)
        cot_g = cot_all[:, start : start + real]
        if real < size:
            cot_g = jnp.pad(cot_g, [(0, 0), (0, size - real)])
        hid, dg, db = gates_call(block_ids, blocks, own_weights[g], pieces[g], bias_g, keep, cot_g, size)
        hiddens.append(hid[:, :real])
        dgs.append(dg)
        biases.append(jnp.sum(db, axis=0).reshape(3, size)[:, :real])
    others = [to_core(dg) for dg in dgs]

    every = [None] * n_stretch
    whole = jnp.zeros((batches, time, width), BF)
    for block, place in zip(blocks, places):
        whole = lax.dynamic_update_slice(whole, block, (0, place * rows, 0))
    x_t = whole.transpose(0, 2, 1).reshape(batches, per_tap, 2, half, time)
    x_t = lax.dynamic_index_in_dim(x_t, c, 2, False)
    x_t = jnp.stack(by_core(x_t[0], x_t[1]))

    def ids_of(shard):
        return jnp.stack([lax.rem(shard, per_tap), shard // per_tap]).astype(jnp.int32)

    sums = []
    for dg, other, size in zip(dgs, others, sizes):
        forth, back = [], []
        for t in range(hops):
            forth = [ring(ring_call(ids_of(owner(hops - t)), x_t, dg, other, forth, size, BF), long_pairs)]
            if t < hops - 1:
                shard = owner(-(hops - 1 - t))
                back = [ring(ring_call(ids_of(shard), x_t, dg, other, back, size, BF), short_pairs)]
        sums.append(ring_call(ids_of(p), x_t, dg, other, forth + back, size, F32))

    in_ids = jnp.stack([x, 2 * p] + at_block).astype(jnp.int32)
    own_rows = time // n_x
    d_mine, d_all = inputs_call(
        in_ids, dgs, [[own_weights[g]] + pieces[g] for g in range(2)], own_rows, width
    )
    d_all = d_all.reshape(n_x, own_rows, width)
    for k in range(1, n_x):
        d_mine = d_mine + to_x(lax.dynamic_index_in_dim(d_all, x ^ k, 0, False), k).astype(F32)
    d_mine = d_mine.reshape(2, rows, width)
    keep_part = lax.dynamic_index_in_dim(d_mine, c, 0, False)
    send_part = to_core(lax.dynamic_index_in_dim(d_mine, 1 - c, 0, False))
    grad_inputs = jnp.stack(by_core(keep_part, send_part)).reshape(inputs.shape)

    hid = jnp.concatenate(hiddens, axis=1).reshape(n_x, own_rows, feats)
    hid_by_k = [lax.dynamic_index_in_dim(hid, x, 0, False)]
    for k in range(1, n_x):
        hid_by_k.append(to_x(lax.dynamic_index_in_dim(hid, x ^ k, 0, False), k))
    hid = jnp.concatenate([by_x([hid_by_k[i ^ j] for j in range(n_x)]) for i in range(n_x)], axis=1)
    hid = hid.reshape(2, rows, width)
    keep_part = lax.dynamic_index_in_dim(hid, c, 0, False)
    send_part = to_core(lax.dynamic_index_in_dim(hid, 1 - c, 0, False))
    hidden = jnp.stack(by_core(keep_part, send_part)).reshape(inputs.shape)

    parts = [[None] * n_x for _ in sizes]
    for g, (total, start, size) in enumerate(zip(sums, starts, sizes)):
        real = min(size, feats - start)
        got = [total] + [to_x(total, k) for k in range(1, n_x)]
        got = [jnp.concatenate(by_core(a, to_core(a)), axis=0) for a in got]
        for i in range(n_x):
            piece = by_x([got[i ^ j] for j in range(n_x)])
            parts[g][i] = piece.reshape(shard_rows, 3, size)[:, :, :real]
    pieces_out = []
    for gate in range(3):
        for i in range(n_x):
            for g in range(2):
                pieces_out.append(parts[g][i][:, gate])
    grad_weight = jnp.concatenate(pieces_out, axis=1)

    bias_part = jnp.concatenate(biases, axis=1)
    bias_part = lax.psum(bias_part, "stream")
    spread = jnp.zeros((3, n_x, feats), F32)
    spread = lax.dynamic_update_slice(spread, bias_part[:, None, :], (0, x, 0))
    grad_bias = lax.psum(spread.reshape(gate_cols), "stretch")
    return (hidden, grad_inputs, grad_weight, grad_bias)


def solution(mesh):
    in_specs = (
        P(None, "stream", "stretch", None),
        P("stream", None),
        P(),
        P(None, "stream", "stretch"),
        P(None, "stream", "stretch", None),
    )
    out_specs = (
        P(None, "stream", "stretch", None),
        P(None, "stream", "stretch", None),
        P("stream", None),
        P(),
    )
    return jax.shard_map(shards, mesh=mesh, in_specs=in_specs, out_specs=out_specs, check_vma=False)
```

time: 4280 us -> 757 us (0.18)
  waiting for transfers between devices: 3370 us -> 126 us
  local copies, waits for them, and re-layouts: 553 us -> 117 us
  Pallas kernels: 0 us -> 282 us
  matrix products: 135 us -> 0 us
  other arithmetic: 127 us -> 71.9 us
  starting transfers between devices: 3.76 us -> 51.5 us
    reduce_scatter x1 -> x0, waiting for transfers between devices: 2000 us -> none  [shards(): lax.psum_scatter(lax.dot_general(stacked, d_gates, contract_rows, preferr...]
    all_gather x1 -> x0, waiting for transfers between devices: 1190 us -> none  [shards(): whole_weight = lax.all_gather(weight, 'stream', axis=0, tiled=True)]
    slice x113 -> x7, local copies, waits for them, and re-layouts: 321 us -> 16.3 us  [the longest x3 10.7 us: shards(): pieces_out.append(parts[g][i][:, gate])]
    pallas_call x0 -> x19, Pallas kernels: none -> 282 us  [the longest x16 117 us: ring_call(): pl.pallas_call(functools.partial(ring_kernel, len(received)), out_shape=j...]
    psum x1 -> x0, waiting for transfers between devices: 175 us -> none  [shards(): grad_weight = lax.psum(grad_weight, 'stretch')]
    dot_general x3 -> x0, matrix products: 135 us -> none  [the longest x1 50.9 us: shards(): lax.dot_general(stacked, d_gates, contract_rows, preferred_element_type=j...]
    ppermute x2 -> x59, waiting for transfers between devices: 0.77 us -> 126 us  [the longest x28 100 us: ring(): return lax.ppermute(a, ('stretch', 'stream'), pairs)]
    pad x56 -> x0, local copies, waits for them, and re-layouts: 114 us -> none  [the longest x28 57.2 us: shards(): lax.associative_scan(compose, (decay, inject), axis=1)]
  transfers between devices with their start and end apart: 5 -> 59, of which waited for: 4 -> 14; matrix products, arithmetic and copies ran while one was open for 2% -> 18% of each run, Pallas kernels for 0% -> 38%
where the time goes in v1:
time: 757 us; the launch traced here: 749 us
  Pallas kernels  282 us (37%)
  waiting for transfers between devices  126 us (17%)
  local copies, waits for them, and re-layouts  117 us (15%)
  other arithmetic  71.9 us (9%)
  blocking collectives  68.9 us (9%)
  starting transfers between devices  51.5 us (7%)
  between operations  30.5 us (4%)
    pallas_call x16, Pallas kernels, ring_call(): pl.pallas_call(functools.partial(ring_kernel, len(received)), out_shape=j...  117 us
    pallas_call x2, Pallas kernels, gates_call(): pl.pallas_call(kernel, out_shape=(jax.ShapeDtypeStruct((time, group), BF)...  106 us
    ppermute x28, waiting for transfers between devices, ring(): return lax.ppermute(a, ('stretch', 'stream'), pairs)  100 us
    pallas_call x1, Pallas kernels, inputs_call(): pl.pallas_call(kernel, out_shape=(jax.ShapeDtypeStruct((own_rows, width),...  59.1 us
    psum x1, blocking collectives, shards(): bias_part = lax.psum(bias_part, 'stream')  41.3 us
    ppermute x28, starting transfers between devices, ring(): return lax.ppermute(a, ('stretch', 'stream'), pairs)  36.5 us
    unnamed x85, local copies, waits for them, and re-layouts  30.2 us
    concatenate x10, local copies, waits for them, and re-layouts, shards(): got = [jnp.concatenate(by_core(a, to_core(a)), axis=0) for a in got]  27.8 us
  transfers between devices with their start and end apart: 59, of which 14 were waited for; matrix products, arithmetic and copies ran while one was open for 18% of the time, Pallas kernels for 38%

profile of v1, /device:TPU:0, one launch (start us, length us, event | category | flops | bytes accessed | tf_op | source)
XLA Modules:
  0.0 748.5 jit_solution(2054204153073452342)
XLA Ops:
  21.5 23.6 %collective-permute-done.19.refs_5_.refs_18_ = bf16[288,1920]{1,0:T(8,128)(2,1)} collective-permute-done((bf16[288,1920]{1,0:T(8,128)(2,1)S(1)}, bf16[288,1920]{1,0:T(8,128)(2,1)}, u32[]{:S(2)}, u32[]{:S(2)}) %collective-permute-start.19) | collective-permute-done | bytes 1105952 | tf_op jit(solution)/shard_map/ppermute | solution.py:432
  45.1 7.1 collective-permute-done.5.refs_7_.refs_5_
  56.9 17.9 %collective-permute-done.7.refs_9_.refs_7_ = bf16[288,1536]{1,0:T(8,128)(2,1)S(1)} collective-permute-done((bf16[288,1536]{1,0:T(8,128)(2,1)}, bf16[288,1536]{1,0:T(8,128)(2,1)S(1)}, u32[]{:S(2)}, u32[]{:S(2)}) %collective-permute-start.7) | collective-permute-done | bytes 884768 | tf_op jit(solution)/shard_map/ppermute | solution.py:432
  92.9 16.2 %all-gather = f32[8,1,256]{2,1,0:T(1,128)S(1)} all-gather(f32[2,1,256]{2,1,0:T(1,128)S(1)} %convert_element_type.16), channel_id=2, replica_groups=mesh['stretch'=4,'stream'=8] {'stretch'}, dimensions={0}, use_global_device_ids=true | all-gather | bytes 10240 | tf_op jit(solution)/shard_map/all_gather | solution.py:504
  118.2 18.1 %collective-permute-done.23.refs_9_.refs_22_ = bf16[288,1920]{1,0:T(8,128)(2,1)} collective-permute-done((bf16[288,1920]{1,0:T(8,128)(2,1)}, bf16[288,1920]{1,0:T(8,128)(2,1)}, u32[]{:S(2)}, u32[]{:S(2)}) %collective-permute-start.23) | collective-permute-done | bytes 1105952 | tf_op jit(solution)/shard_map/ppermute | solution.py:432
  176.0 12.5 %collective-permute-done.13.refs_15_.refs_13_ = bf16[288,1536]{1,0:T(8,128)(2,1)} collective-permute-done((bf16[288,1536]{1,0:T(8,128)(2,1)}, bf16[288,1536]{1,0:T(8,128)(2,1)}, u32[]{:S(2)}, u32[]{:S(2)}) %collective-permute-start.13) | collective-permute-done | bytes 884768 | tf_op jit(solution)/shard_map/ppermute | solution.py:432
  209.9 46.9 %gates.2 = (bf16[1024,512]{1,0:T(8,128)(2,1)}, bf16[2,1024,1536]{2,1,0:T(8,128)(2,1)}, f32[8,1536]{1,0:T(8,128)}) custom-call(s32[20]{0:T(128)} %stack.223.ids, bf16[2,256,2304]{2,1,0:T(8,128)(2,1)} %bitcast.29.refs_0_, bf16[2,256,2304]{2,1,0:T(8,128)(2,1)} %collective-permute-done.refs_1_, bf16[2,256,2304]{2,1,0:T(8,128)(2,1)} %collective-permute-done.1.refs_2_, ...), custom_call_target="tpu_custom_call" | custom-call | flops 14495514624 | bytes 28311552 | tf_op jit(solution)/shard_map/gates/pallas_call | solution.py:238
  257.8 59.0 %gates.3 = (bf16[1024,640]{1,0:T(8,128)(2,1)}, bf16[2,1024,1920]{2,1,0:T(8,128)(2,1)}, f32[8,1920]{1,0:T(8,128)}) custom-call(s32[20]{0:T(128)} %stack.223.ids, bf16[2,256,2304]{2,1,0:T(8,128)(2,1)} %bitcast.29.refs_0_, bf16[2,256,2304]{2,1,0:T(8,128)(2,1)} %collective-permute-done.refs_1_, bf16[2,256,2304]{2,1,0:T(8,128)(2,1)} %collective-permute-done.1.refs_2_, ...), custom_call_target="tpu_custom_call" | custom-call | flops 18119393280 | bytes 34209792 | tf_op jit(solution)/shard_map/gates/pallas_call | solution.py:238
  330.9 59.1 %grad_in.1 = (f32[512,2304]{1,0:T(8,128)}, bf16[1024,2304]{1,0:T(8,128)(2,1)}) custom-call(s32[16]{0:T(128)} %stack.228.ids, bf16[2,1024,1536]{2,1,0:T(8,128)(2,1)} %get-tuple-element.14.refs_0_.mine_ref, bf16[2,1024,1920]{2,1,0:T(8,128)(2,1)} %get-tuple-element.15.refs_1_.mine_ref, bf16[2,288,1536]{2,1,0:T(8,128)(2,1)} %copy-done.18, ...), custom_call_target="tpu_custom_call" | custom-call | flops 32614907904 | bytes 55443456 | tf_op jit(solution)/shard_map/grad_in/pallas_call | solution.py:338
  395.6 6.7 grad_w.16
  404.7 41.3 %psum.14 = f32[3,1,1152]{2,1,0:T(1,128)S(1)} all-reduce(f32[3,1,1152]{2,1,0:T(1,128)} %broadcast_in_dim.16), channel_id=1, replica_groups=mesh['stretch'=4,'stream'=8] {'stream'}, use_global_device_ids=true, to_apply=%region_2.3 | all-reduce | flops 3456 | bytes 27648 | tf_op jit(solution)/shard_map/psum | solution.py:581
  449.5 11.4 %psum.15 = f32[6912]{0:T(1024)} all-reduce(f32[6912]{0:T(1024)} %reshape.314), channel_id=1, replica_groups=mesh['stretch'=4,'stream'=8] {'stretch'}, use_global_device_ids=true, to_apply=%region_3.4 | all-reduce | flops 6912 | bytes 55296 | tf_op jit(solution)/shard_map/psum | solution.py:584
  463.4 6.6 grad_w.20
  469.9 6.8 grad_w.17
  481.4 5.4 collective-permute-done.42.refs_0_
  486.7 6.8 grad_w.21
  493.5 6.8 grad_w.18
  502.3 7.6 %grad_w.24 = bf16[288,1920]{1,0:T(8,128)(2,1)} custom-call(s32[2]{0:T(128)} %get-tuple-element.95.ids, bf16[2,4,288,1024]{3,2,1,0:T(8,128)(2,1)} %pad_maximum_fusion.x_ref, bf16[2,1024,1920]{2,1,0:T(8,128)(2,1)} %get-tuple-element.15.refs_1_.mine_ref, bf16[2,1024,1920]{2,1,0:T(8,128)(2,1)} %collective-permute-done.48.other_ref), custom_call_target="tpu_custom_call" | custom-call | flops 2264924160 | bytes 12288000 | tf_op jit(solution)/shard_map/grad_w/pallas_call | solution.py:374
  516.4 6.8 grad_w.22
  525.2 7.6 %grad_w.28 = bf16[288,1920]{1,0:T(8,128)(2,1)} custom-call(s32[2]{0:T(128)} %get-tuple-element.96.ids, bf16[2,4,288,1024]{3,2,1,0:T(8,128)(2,1)} %pad_maximum_fusion.x_ref, bf16[2,1024,1920]{2,1,0:T(8,128)(2,1)} %get-tuple-element.15.refs_1_.mine_ref, bf16[2,1024,1920]{2,1,0:T(8,128)(2,1)} %collective-permute-done.48.other_ref), custom_call_target="tpu_custom_call" | custom-call | flops 2264924160 | bytes 12288000 | tf_op jit(solution)/shard_map/grad_w/pallas_call | solution.py:374
  532.8 6.8 grad_w.19
  542.0 7.8 %grad_w.25 = bf16[288,1920]{1,0:T(8,128)(2,1)} custom-call(s32[2]{0:T(128)} %pad_add_fusion.3.ids, bf16[2,4,288,1024]{3,2,1,0:T(8,128)(2,1)} %pad_maximum_fusion.x_ref, bf16[2,1024,1920]{2,1,0:T(8,128)(2,1)} %get-tuple-element.15.refs_1_.mine_ref, bf16[2,1024,1920]{2,1,0:T(8,128)(2,1)} %collective-permute-done.48.other_ref, ...), custom_call_target="tpu_custom_call" | custom-call | flops 2264924160 | bytes 12288000 | tf_op jit(solution)/shard_map/grad_w/pallas_call | solution.py:374
  557.6 7.3 grad_w.23
  568.8 7.9 %grad_w.29 = bf16[288,1920]{1,0:T(8,128)(2,1)} custom-call(s32[2]{0:T(128)} %pad_add_fusion.6.ids, bf16[2,4,288,1024]{3,2,1,0:T(8,128)(2,1)} %pad_maximum_fusion.x_ref, bf16[2,1024,1920]{2,1,0:T(8,128)(2,1)} %get-tuple-element.15.refs_1_.mine_ref, bf16[2,1024,1920]{2,1,0:T(8,128)(2,1)} %collective-permute-done.48.other_ref, ...), custom_call_target="tpu_custom_call" | custom-call | flops 2264924160 | bytes 12288000 | tf_op jit(solution)/shard_map/grad_w/pallas_call | solution.py:374
  578.5 7.8 %grad_w.26 = bf16[288,1920]{1,0:T(8,128)(2,1)} custom-call(s32[2]{0:T(128)} %pad_add_fusion.2.ids, bf16[2,4,288,1024]{3,2,1,0:T(8,128)(2,1)} %pad_maximum_fusion.x_ref, bf16[2,1024,1920]{2,1,0:T(8,128)(2,1)} %get-tuple-element.15.refs_1_.mine_ref, bf16[2,1024,1920]{2,1,0:T(8,128)(2,1)} %collective-permute-done.48.other_ref, ...), custom_call_target="tpu_custom_call" | custom-call | flops 2264924160 | bytes 12288000 | tf_op jit(solution)/shard_map/grad_w/pallas_call | solution.py:374
  595.5 7.8 %grad_w.30 = bf16[288,1920]{1,0:T(8,128)(2,1)} custom-call(s32[2]{0:T(128)} %pad_add_fusion.5.ids, bf16[2,4,288,1024]{3,2,1,0:T(8,128)(2,1)} %pad_maximum_fusion.x_ref, bf16[2,1024,1920]{2,1,0:T(8,128)(2,1)} %get-tuple-element.15.refs_1_.mine_ref, bf16[2,1024,1920]{2,1,0:T(8,128)(2,1)} %collective-permute-done.48.other_ref, ...), custom_call_target="tpu_custom_call" | custom-call | flops 2264924160 | bytes 12288000 | tf_op jit(solution)/shard_map/grad_w/pallas_call | solution.py:374
  606.8 7.8 %grad_w.27 = bf16[288,1920]{1,0:T(8,128)(2,1)} custom-call(s32[2]{0:T(128)} %pad_add_fusion.1.ids, bf16[2,4,288,1024]{3,2,1,0:T(8,128)(2,1)} %pad_maximum_fusion.x_ref, bf16[2,1024,1920]{2,1,0:T(8,128)(2,1)} %get-tuple-element.15.refs_1_.mine_ref, bf16[2,1024,1920]{2,1,0:T(8,128)(2,1)} %collective-permute-done.48.other_ref, ...), custom_call_target="tpu_custom_call" | custom-call | flops 2264924160 | bytes 12288000 | tf_op jit(solution)/shard_map/grad_w/pallas_call | solution.py:374
  634.5 8.6 %grad_w.31 = f32[288,1920]{1,0:T(8,128)} custom-call(s32[2]{0:T(128)} %pad_add_fusion.ids, bf16[2,4,288,1024]{3,2,1,0:T(8,128)(2,1)} %pad_maximum_fusion.x_ref, bf16[2,1024,1920]{2,1,0:T(8,128)(2,1)} %get-tuple-element.15.refs_1_.mine_ref, bf16[2,1024,1920]{2,1,0:T(8,128)(2,1)} %collective-permute-done.48.other_ref, ...), custom_call_target="tpu_custom_call" | custom-call | flops 2264924160 | bytes 12288000 | tf_op jit(solution)/shard_map/grad_w/pallas_call | solution.py:374
  661.9 5.4 broadcast_select_fusion
  670.9 24.0 %collective-permute-done.56 = f32[288,1920]{1,0:T(8,128)} collective-permute-done((f32[288,1920]{1,0:T(8,128)}, f32[288,1920]{1,0:T(8,128)}, u32[]{:S(2)}, u32[]{:S(2)}) %collective-permute-start.56) | collective-permute-done | bytes 2211872 | tf_op jit(solution)/shard_map/ppermute | solution.py:438
  719.1 6.8 copy_select_fusion.1
  725.9 6.0 copy_select_fusion
  (279 shorter events, 240.0 us)
Async XLA Ops:
  15.0 40.0 %collective-permute-start.17 = (bf16[256,2304]{1,0:T(8,128)(2,1)S(1)}, bf16[256,2304]{1,0:T(8,128)(2,1)}, u32[]{:S(2)}, u32[]{:S(2)}) collective-permute-start(bf16[256,2304]{1,0:T(8,128)(2,1)S(1)} %dynamic-slice_bitcast_fusion.6), channel_id=1, source_target_pairs={{0,8},{8,0},{16,24},{24,16},{1,9},{9,1},{17,25},{25,17},{2,10},{10... | collective-permute-start | bytes 3538952 | tf_op jit(solution)/shard_map/ppermute | solution.py:435
  15.1 37.8 %collective-permute-start.21 = (bf16[288,1920]{1,0:T(8,128)(2,1)S(1)}, bf16[288,1920]{1,0:T(8,128)(2,1)}, u32[]{:S(2)}, u32[]{:S(2)}) collective-permute-start(bf16[288,1920]{1,0:T(8,128)(2,1)S(1)} %dynamic-slice_bitcast_fusion.7), channel_id=1, source_target_pairs={{0,1},{1,3},{2,0},{3,5},{4,2},{5,7},{6,4},{7,6},{8,10},{9,8},{10,1... | collective-permute-start | bytes 3317768 | tf_op jit(solution)/shard_map/ppermute | solution.py:432
  15.9 36.4 %collective-permute-start.5 = (bf16[288,1536]{1,0:T(8,128)(2,1)}, bf16[288,1536]{1,0:T(8,128)(2,1)}, u32[]{:S(2)}, u32[]{:S(2)}) collective-permute-start(bf16[288,1536]{1,0:T(8,128)(2,1)} %dynamic-slice_bitcast_fusion.8), channel_id=1, source_target_pairs={{0,1},{1,3},{2,0},{3,5},{4,2},{5,7},{6,4},{7,6},{8,10},{9,8},{10,1... | collective-permute-start | bytes 2654216 | tf_op jit(solution)/shard_map/ppermute | solution.py:432
  21.5 33.4 %collective-permute-start.4 = (bf16[288,1536]{1,0:T(8,128)(2,1)}, bf16[288,1536]{1,0:T(8,128)(2,1)}, u32[]{:S(2)}, u32[]{:S(2)}) collective-permute-start(bf16[288,1536]{1,0:T(8,128)(2,1)} %collective-permute-done.3.refs_5_.refs_3_), channel_id=1, source_target_pairs={{0,8},{8,0},{16,24},{24,16},{1,9},{9,1},{17,25},{25,17},{2,10},{10... | collective-permute-start | bytes 2654216 | tf_op jit(solution)/shard_map/ppermute | solution.py:435
  45.1 65.9 %collective-permute-start.20 = (bf16[288,1920]{1,0:T(8,128)(2,1)}, bf16[288,1920]{1,0:T(8,128)(2,1)}, u32[]{:S(2)}, u32[]{:S(2)}) collective-permute-start(bf16[288,1920]{1,0:T(8,128)(2,1)} %collective-permute-done.19.refs_5_.refs_18_), channel_id=1, source_target_pairs={{0,8},{8,0},{16,24},{24,16},{1,9},{9,1},{17,25},{25,17},{2,10},{10... | collective-permute-start | bytes 3317768 | tf_op jit(solution)/shard_map/ppermute | solution.py:435
  55.0 54.3 %collective-permute-start.9 = (bf16[288,1536]{1,0:T(8,128)(2,1)}, bf16[288,1536]{1,0:T(8,128)(2,1)}, u32[]{:S(2)}, u32[]{:S(2)}) collective-permute-start(bf16[288,1536]{1,0:T(8,128)(2,1)} %collective-permute-done.5.refs_7_.refs_5_), channel_id=1, source_target_pairs={{0,1},{1,3},{2,0},{3,5},{4,2},{5,7},{6,4},{7,6},{8,10},{9,8},{10,1... | collective-permute-start | bytes 2654216 | tf_op jit(solution)/shard_map/ppermute | solution.py:432
  55.0 83.1 %collective-permute-start = (bf16[2,256,2304]{2,1,0:T(8,128)(2,1)}, bf16[2,256,2304]{2,1,0:T(8,128)(2,1)}, u32[]{:S(2)}, u32[]{:S(2)}) collective-permute-start(bf16[2,256,2304]{2,1,0:T(8,128)(2,1)} %bitcast.29.refs_0_), channel_id=1, source_target_pairs={{0,16},{8,24},{16,0},{24,8},{1,17},{9,25},{17,1},{25,9},{2,18},{10... | collective-permute-start | bytes 7077896 | tf_op jit(solution)/shard_map/ppermute | solution.py:438
  56.9 82.1 %collective-permute-start.1 = (bf16[2,256,2304]{2,1,0:T(8,128)(2,1)}, bf16[2,256,2304]{2,1,0:T(8,128)(2,1)}, u32[]{:S(2)}, u32[]{:S(2)}) collective-permute-start(bf16[2,256,2304]{2,1,0:T(8,128)(2,1)} %bitcast.29.refs_0_), channel_id=1, source_target_pairs={{0,8},{8,0},{16,24},{24,16},{1,9},{9,1},{17,25},{25,17},{2,10},{10... | collective-permute-start | bytes 7077896 | tf_op jit(solution)/shard_map/ppermute | solution.py:435
  74.9 39.2 %collective-permute-start.22 = (bf16[288,1920]{1,0:T(8,128)(2,1)}, bf16[288,1920]{1,0:T(8,128)(2,1)}, u32[]{:S(2)}, u32[]{:S(2)}) collective-permute-start(bf16[288,1920]{1,0:T(8,128)(2,1)} %collective-permute-done.21.refs_7_.refs_20_), channel_id=1, source_target_pairs={{0,8},{8,0},{16,24},{24,16},{1,9},{9,1},{17,25},{25,17},{2,10},{10... | collective-permute-start | bytes 3317768 | tf_op jit(solution)/shard_map/ppermute | solution.py:435
  139.0 49.5 %collective-permute-start.27 = (bf16[288,1920]{1,0:T(8,128)(2,1)}, bf16[288,1920]{1,0:T(8,128)(2,1)}, u32[]{:S(2)}, u32[]{:S(2)}) collective-permute-start(bf16[288,1920]{1,0:T(8,128)(2,1)} %collective-permute-done.23.refs_9_.refs_22_), channel_id=1, source_target_pairs={{0,2},{1,0},{2,4},{3,1},{4,6},{5,3},{6,7},{7,5},{8,9},{9,11},{10,8... | collective-permute-start | bytes 3317768 | tf_op jit(solution)/shard_map/ppermute | solution.py:432
  141.9 47.1 %collective-permute-start.29 = (bf16[288,1920]{1,0:T(8,128)(2,1)}, bf16[288,1920]{1,0:T(8,128)(2,1)}, u32[]{:S(2)}, u32[]{:S(2)}) collective-permute-start(bf16[288,1920]{1,0:T(8,128)(2,1)} %collective-permute-done.25.refs_11_.refs_24_), channel_id=1, source_target_pairs={{0,1},{1,3},{2,0},{3,5},{4,2},{5,7},{6,4},{7,6},{8,10},{9,8},{10,1... | collective-permute-start | bytes 3317768 | tf_op jit(solution)/shard_map/ppermute | solution.py:432
  152.6 35.9 %collective-permute-start.13 = (bf16[288,1536]{1,0:T(8,128)(2,1)}, bf16[288,1536]{1,0:T(8,128)(2,1)}, u32[]{:S(2)}, u32[]{:S(2)}) collective-permute-start(bf16[288,1536]{1,0:T(8,128)(2,1)} %collective-permute-done.9.refs_11_.refs_9_), channel_id=1, source_target_pairs={{0,1},{1,3},{2,0},{3,5},{4,2},{5,7},{6,4},{7,6},{8,10},{9,8},{10,1... | collective-permute-start | bytes 2654216 | tf_op jit(solution)/shard_map/ppermute | solution.py:432
  154.2 55.3 %collective-permute-start.2 = (bf16[2,256,2304]{2,1,0:T(8,128)(2,1)}, bf16[2,256,2304]{2,1,0:T(8,128)(2,1)}, u32[]{:S(2)}, u32[]{:S(2)}) collective-permute-start(bf16[2,256,2304]{2,1,0:T(8,128)(2,1)} %collective-permute-done.refs_1_), channel_id=1, source_target_pairs={{0,8},{8,0},{16,24},{24,16},{1,9},{9,1},{17,25},{25,17},{2,10},{10... | collective-permute-start | bytes 7077896 | tf_op jit(solution)/shard_map/ppermute | solution.py:435
  155.2 36.9 %collective-permute-start.15 = (bf16[288,1536]{1,0:T(8,128)(2,1)}, bf16[288,1536]{1,0:T(8,128)(2,1)}, u32[]{:S(2)}, u32[]{:S(2)}) collective-permute-start(bf16[288,1536]{1,0:T(8,128)(2,1)} %collective-permute-done.11.refs_13_.refs_11_), channel_id=1, source_target_pairs={{0,2},{1,0},{2,4},{3,1},{4,6},{5,3},{6,7},{7,5},{8,9},{9,11},{10,8... | collective-permute-start | bytes 2654216 | tf_op jit(solution)/shard_map/ppermute | solution.py:432
  208.4 48.4 %collective-permute-start.24 = (bf16[288,1920]{1,0:T(8,128)(2,1)}, bf16[288,1920]{1,0:T(8,128)(2,1)S(1)}, u32[]{:S(2)}, u32[]{:S(2)}) collective-permute-start(bf16[288,1920]{1,0:T(8,128)(2,1)} %collective-permute-done.23.refs_9_.refs_22_), channel_id=1, source_target_pairs={{0,8},{8,0},{16,24},{24,16},{1,9},{9,1},{17,25},{25,17},{2,10},{10... | collective-permute-start | bytes 3317768 | tf_op jit(solution)/shard_map/ppermute | solution.py:435
  208.9 48.1 %collective-permute-start.26 = (bf16[288,1920]{1,0:T(8,128)(2,1)}, bf16[288,1920]{1,0:T(8,128)(2,1)}, u32[]{:S(2)}, u32[]{:S(2)}) collective-permute-start(bf16[288,1920]{1,0:T(8,128)(2,1)} %collective-permute-done.25.refs_11_.refs_24_), channel_id=1, source_target_pairs={{0,8},{8,0},{16,24},{24,16},{1,9},{9,1},{17,25},{25,17},{2,10},{10... | collective-permute-start | bytes 3317768 | tf_op jit(solution)/shard_map/ppermute | solution.py:435
  209.0 48.0 %collective-permute-start.28 = (bf16[288,1920]{1,0:T(8,128)(2,1)}, bf16[288,1920]{1,0:T(8,128)(2,1)}, u32[]{:S(2)}, u32[]{:S(2)}) collective-permute-start(bf16[288,1920]{1,0:T(8,128)(2,1)} %collective-permute-done.27.refs_13_.refs_26_), channel_id=1, source_target_pairs={{0,8},{8,0},{16,24},{24,16},{1,9},{9,1},{17,25},{25,17},{2,10},{10... | collective-permute-start | bytes 3317768 | tf_op jit(solution)/shard_map/ppermute | solution.py:435
  209.4 47.6 %collective-permute-start.30 = (bf16[288,1920]{1,0:T(8,128)(2,1)}, bf16[288,1920]{1,0:T(8,128)(2,1)}, u32[]{:S(2)}, u32[]{:S(2)}) collective-permute-start(bf16[288,1920]{1,0:T(8,128)(2,1)} %collective-permute-done.29.refs_15_.refs_28_), channel_id=1, source_target_pairs={{0,8},{8,0},{16,24},{24,16},{1,9},{9,1},{17,25},{25,17},{2,10},{10... | collective-permute-start | bytes 3317768 | tf_op jit(solution)/shard_map/ppermute | solution.py:435
  209.5 47.5 %collective-permute-start.32 = (bf16[288,1920]{1,0:T(8,128)(2,1)}, bf16[288,1920]{1,0:T(8,128)(2,1)}, u32[]{:S(2)}, u32[]{:S(2)}) collective-permute-start(bf16[288,1920]{1,0:T(8,128)(2,1)} %collective-permute-done.31.refs_17_.refs_30_), channel_id=1, source_target_pairs={{0,8},{8,0},{16,24},{24,16},{1,9},{9,1},{17,25},{25,17},{2,10},{10... | collective-permute-start | bytes 3317768 | tf_op jit(solution)/shard_map/ppermute | solution.py:435
  256.8 138.8 %collective-permute-start.37 = (bf16[2,1024,1536]{2,1,0:T(8,128)(2,1)}, bf16[2,1024,1536]{2,1,0:T(8,128)(2,1)}, u32[]{:S(2)}, u32[]{:S(2)}) collective-permute-start(bf16[2,1024,1536]{2,1,0:T(8,128)(2,1)} %get-tuple-element.14.refs_0_.mine_ref), channel_id=1, source_target_pairs={{0,8},{8,0},{16,24},{24,16},{1,9},{9,1},{17,25},{25,17},{2,10},{10... | collective-permute-start | bytes 18874376 | tf_op jit(solution)/shard_map/ppermute | solution.py:435
  316.8 185.5 %collective-permute-start.48 = (bf16[2,1024,1920]{2,1,0:T(8,128)(2,1)}, bf16[2,1024,1920]{2,1,0:T(8,128)(2,1)}, u32[]{:S(2)}, u32[]{:S(2)}) collective-permute-start(bf16[2,1024,1920]{2,1,0:T(8,128)(2,1)} %get-tuple-element.15.refs_1_.mine_ref), channel_id=1, source_target_pairs={{0,8},{8,0},{16,24},{24,16},{1,9},{9,1},{17,25},{25,17},{2,10},{10... | collective-permute-start | bytes 23592968 | tf_op jit(solution)/shard_map/ppermute | solution.py:435
  329.1 131.8 %collective-permute-start.33 = (bf16[512,1152]{1,0:T(8,128)(2,1)S(1)}, bf16[512,1152]{1,0:T(8,128)(2,1)}, u32[]{:S(2)}, u32[]{:S(2)}) collective-permute-start(bf16[512,1152]{1,0:T(8,128)(2,1)S(1)} %dynamic-slice_bitcast_fusion.5), channel_id=1, source_target_pairs={{0,16},{8,24},{16,0},{24,8},{1,17},{9,25},{17,1},{25,9},{2,18},{10... | collective-permute-start | bytes 3538952 | tf_op jit(solution)/shard_map/ppermute | solution.py:438
  393.2 116.7 %collective-permute-start.35 = (bf16[512,2304]{1,0:T(8,128)(2,1)}, bf16[512,2304]{1,0:T(8,128)(2,1)}, u32[]{:S(2)}, u32[]{:S(2)}) collective-permute-start(bf16[512,2304]{1,0:T(8,128)(2,1)} %dynamic-slice_bitcast_fusion.3), channel_id=1, source_target_pairs={{0,16},{8,24},{16,0},{24,8},{1,17},{9,25},{17,1},{25,9},{2,18},{10... | collective-permute-start | bytes 7077896 | tf_op jit(solution)/shard_map/ppermute | solution.py:438
  402.4 67.6 %collective-permute-start.38 = (bf16[288,1536]{1,0:T(8,128)(2,1)}, bf16[288,1536]{1,0:T(8,128)(2,1)}, u32[]{:S(2)}, u32[]{:S(2)}) collective-permute-start(bf16[288,1536]{1,0:T(8,128)(2,1)} %grad_w.16), channel_id=1, source_target_pairs={{0,2},{1,0},{2,4},{3,1},{4,6},{5,3},{6,7},{7,5},{8,9},{9,11},{10,8... | collective-permute-start | bytes 2654216 | tf_op jit(solution)/shard_map/ppermute | solution.py:432
  481.4 68.4 %collective-permute-start.34 = (bf16[256,2304]{1,0:T(8,128)(2,1)}, bf16[256,2304]{1,0:T(8,128)(2,1)S(1)}, u32[]{:S(2)}, u32[]{:S(2)}) collective-permute-start(bf16[256,2304]{1,0:T(8,128)(2,1)} %dynamic-slice_bitcast_fusion.4), channel_id=1, source_target_pairs={{0,8},{8,0},{16,24},{24,16},{1,9},{9,1},{17,25},{25,17},{2,10},{10... | collective-permute-start | bytes 3538952 | tf_op jit(solution)/shard_map/ppermute | solution.py:435
  516.3 70.2 %collective-permute-start.36 = (f32[256,2304]{1,0:T(8,128)}, f32[256,2304]{1,0:T(8,128)}, u32[]{:S(2)}, u32[]{:S(2)}) collective-permute-start(f32[256,2304]{1,0:T(8,128)} %dynamic-slice_bitcast_fusion.2), channel_id=1, source_target_pairs={{0,8},{8,0},{16,24},{24,16},{1,9},{9,1},{17,25},{25,17},{2,10},{10... | collective-permute-start | bytes 7077896 | tf_op jit(solution)/shard_map/ppermute | solution.py:435
  532.7 36.1 %collective-permute-start.53 = (bf16[288,1920]{1,0:T(8,128)(2,1)}, bf16[288,1920]{1,0:T(8,128)(2,1)}, u32[]{:S(2)}, u32[]{:S(2)}) collective-permute-start(bf16[288,1920]{1,0:T(8,128)(2,1)} %grad_w.28), channel_id=1, source_target_pairs={{0,1},{1,3},{2,0},{3,5},{4,2},{5,7},{6,4},{7,6},{8,10},{9,8},{10,1... | collective-permute-start | bytes 3317768 | tf_op jit(solution)/shard_map/ppermute | solution.py:432
  565.0 41.2 %collective-permute-start.45 = (f32[288,1536]{1,0:T(8,128)}, f32[288,1536]{1,0:T(8,128)}, u32[]{:S(2)}, u32[]{:S(2)}) collective-permute-start(f32[288,1536]{1,0:T(8,128)} %grad_w.23), channel_id=1, source_target_pairs={{0,16},{8,24},{16,0},{24,8},{1,17},{9,25},{17,1},{25,9},{2,18},{10... | collective-permute-start | bytes 5308424 | tf_op jit(solution)/shard_map/ppermute | solution.py:438
  578.5 40.8 %collective-permute-start.47 = (f32[288,1536]{1,0:T(8,128)S(1)}, f32[288,1536]{1,0:T(8,128)}, u32[]{:S(2)}, u32[]{:S(2)}) collective-permute-start(f32[288,1536]{1,0:T(8,128)S(1)} %copy-done.10), channel_id=1, source_target_pairs={{0,8},{8,0},{16,24},{24,16},{1,9},{9,1},{17,25},{25,17},{2,10},{10... | collective-permute-start | bytes 5308424 | tf_op jit(solution)/shard_map/ppermute | solution.py:435
  606.2 40.1 %collective-permute-start.46 = (f32[288,1536]{1,0:T(8,128)}, f32[288,1536]{1,0:T(8,128)}, u32[]{:S(2)}, u32[]{:S(2)}) collective-permute-start(f32[288,1536]{1,0:T(8,128)} %collective-permute-done.45), channel_id=1, source_target_pairs={{0,8},{8,0},{16,24},{24,16},{1,9},{9,1},{17,25},{25,17},{2,10},{10... | collective-permute-start | bytes 5308424 | tf_op jit(solution)/shard_map/ppermute | solution.py:435
  643.1 57.0 %collective-permute-start.58 = (f32[288,1920]{1,0:T(8,128)}, f32[288,1920]{1,0:T(8,128)}, u32[]{:S(2)}, u32[]{:S(2)}) collective-permute-start(f32[288,1920]{1,0:T(8,128)} %grad_w.31), channel_id=1, source_target_pairs={{0,8},{8,0},{16,24},{24,16},{1,9},{9,1},{17,25},{25,17},{2,10},{10... | collective-permute-start | bytes 6635528 | tf_op jit(solution)/shard_map/ppermute | solution.py:435
  644.6 50.3 %collective-permute-start.56 = (f32[288,1920]{1,0:T(8,128)}, f32[288,1920]{1,0:T(8,128)}, u32[]{:S(2)}, u32[]{:S(2)}) collective-permute-start(f32[288,1920]{1,0:T(8,128)} %grad_w.31), channel_id=1, source_target_pairs={{0,16},{8,24},{16,0},{24,8},{1,17},{9,25},{17,1},{25,9},{2,18},{10... | collective-permute-start | bytes 6635528 | tf_op jit(solution)/shard_map/ppermute | solution.py:438
  (61 other events, 1104.0 us)

commit v2 on v1

v2 whole, which is shorter than its diff:
```python
import functools

import jax
import jax.numpy as jnp
import numpy as np
from jax import lax
from jax.experimental import pallas as pl
from jax.experimental.pallas import tpu as pltpu
from jax.sharding import PartitionSpec as P

BF = jnp.bfloat16
F32 = jnp.float32
LANES = 128
VMEM_BYTES = 60 * 1024 * 1024


def cost(flops):
    return pl.CostEstimate(flops=int(1.6 * flops), bytes_accessed=10**6, transcendentals=0)


def any_spec():
    return pl.BlockSpec(memory_space=pl.ANY)


def vmem_spec():
    return pl.BlockSpec(memory_space=pltpu.VMEM)


def smem_spec():
    return pl.BlockSpec(memory_space=pltpu.SMEM)


def ring_order(count):
    inner = 1
    while (2 * inner) ** 2 <= count:
        inner *= 2
    outer = count // inner
    if inner == 1 or outer % 2:
        return list(range(count))
    order = [z * inner for z in range(outer)]
    for turn, z in enumerate(reversed(range(outer))):
        across = range(1, inner) if turn % 2 == 0 else reversed(range(1, inner))
        order += [z * inner + y for y in across]
    return order


def sigmoid(v):
    return 0.5 + 0.5 * jnp.tanh(0.5 * v)


def gates_kernel(at, rows, half, n_blocks, n_pieces, group, offset, ids, *refs):
    x_refs = refs[:n_blocks]
    own_ref = refs[n_blocks]
    w_refs = refs[n_blocks + 1 : n_blocks + 1 + n_pieces]
    bias_ref, keep_ref, cot_ref = refs[n_blocks + 1 + n_pieces : n_blocks + 4 + n_pieces]
    hid_ref, dg_ref, db_ref = refs[n_blocks + 4 + n_pieces : n_blocks + 7 + n_pieces]
    x_buf, w_buf, gate_buf, cell_buf, hid_buf, dg_buf, x_sem, w_sem, out_sem = refs[n_blocks + 7 + n_pieces :]
    time, width = x_buf.shape
    cols = gate_buf.shape[1]
    tile = w_buf.shape[2]
    batch = ids[at["core"]]

    def x_copy(i):
        start = pl.multiple_of(ids[at["time"] + i] * rows, rows)
        return pltpu.make_async_copy(x_refs[i].at[batch], x_buf.at[pl.ds(start, rows), :], x_sem.at[i])

    def w_copies(col, size, slot):
        copies = []
        for i in range(n_pieces + 2):
            if i < 2:
                source = own_ref.at[i, :, pl.ds(offset + col, size)]
                block = ids[at["pieces"]] + i
            else:
                source = w_refs[i - 2].at[:, pl.ds(offset + col, size)]
                block = ids[at["pieces"] + i - 1]
            start = pl.multiple_of(block * half, half)
            copies.append(
                pltpu.make_async_copy(
                    source, w_buf.at[slot, pl.ds(start, half), pl.ds(0, size)], w_sem.at[slot, i]
                )
            )
        return copies

    full = cols // tile
    tail = cols - full * tile
    for i in range(n_blocks):
        x_copy(i).start()
    for copy in w_copies(0, tile, 0):
        copy.start()
    for i in range(n_blocks):
        x_copy(i).wait()
    row0 = lax.broadcasted_iota(jnp.int32, (time, 1), 0) == 0

    def product(slot, col, size):
        now = jnp.dot(x_buf[...], w_buf[slot, :width, :size], preferred_element_type=F32)
        prev = jnp.dot(x_buf[...], w_buf[slot, width:, :size], preferred_element_type=F32)
        prev = jnp.where(row0, 0.0, pltpu.roll(prev, 1, 0))
        gate_buf[:, pl.ds(col, size)] = now + prev + bias_ref[:, pl.ds(col, size)]

    @pl.loop(0, full)
    def _(n):
        slot = lax.rem(n, 2)

        @pl.when(n + 1 < full)
        def _():
            for copy in w_copies(pl.multiple_of((n + 1) * tile, tile), tile, 1 - slot):
                copy.start()

        if tail:

            @pl.when(n + 1 == full)
            def _():
                for copy in w_copies(full * tile, tail, 1 - slot):
                    copy.start()

        for copy in w_copies(pl.multiple_of(n * tile, tile), tile, slot):
            copy.wait()
        product(slot, pl.multiple_of(n * tile, tile), tile)

    if tail:
        for copy in w_copies(full * tile, tail, full % 2):
            copy.wait()
        product(full % 2, full * tile, tail)

    def out_copies(block):
        lane = block * LANES
        if not isinstance(block, int):
            lane = pl.multiple_of(lane, LANES)
        copies = [pltpu.make_async_copy(hid_buf.at[block], hid_ref.at[:, pl.ds(lane, LANES)], out_sem.at[block, 0])]
        for gate in range(3):
            copies.append(
                pltpu.make_async_copy(
                    dg_buf.at[block, :, :, pl.ds(gate * LANES, LANES)],
                    dg_ref.at[:, :, pl.ds(gate * group + lane, LANES)],
                    out_sem.at[block, 1 + gate],
                )
            )
        return copies

    scan(time, group, gate_buf, keep_ref, cot_ref, cell_buf, hid_buf, dg_buf, db_ref, out_copies)
    for block in range(group // LANES):
        for copy in out_copies(block):
            copy.wait()


STEP = 16


def scan(time, group, gate_buf, keep_ref, cot_ref, cell_buf, hid_buf, dg_buf, db_ref, out_copies):
    steps = time // STEP
    sub = lax.broadcasted_iota(jnp.int32, (8, LANES), 0)
    zeros = jnp.zeros((8, LANES), F32)

    def down(a, d):
        return pltpu.roll(a, d, 0)

    def up(a, d):
        return pltpu.roll(a, 8 - d, 0)

    def spread(a, r):
        return jnp.broadcast_to(a[r : r + 1, :], (8, LANES))

    @pl.loop(0, group // LANES)
    def _(block):
        lane = pl.multiple_of(block * LANES, LANES)
        z_at = pl.ds(lane, LANES)
        f_at = pl.ds(pl.multiple_of(group + lane, LANES), LANES)
        o_at = pl.ds(pl.multiple_of(2 * group + lane, LANES), LANES)

        def forward(i, carry):
            at = pl.multiple_of(i * STEP, STEP)
            outs = []
            for h in range(STEP // 8):
                here = pl.ds(at + 8 * h, 8)
                cand = jnp.tanh(gate_buf[here, z_at])
                forget = sigmoid(gate_buf[here, f_at])
                outgate = sigmoid(gate_buf[here, o_at])
                a = forget * keep_ref[here, :]
                b = (1.0 - forget) * cand
                gate_buf[here, z_at] = cand
                gate_buf[here, f_at] = forget
                gate_buf[here, o_at] = outgate
                for d in (1, 2, 4):
                    inside = sub >= d
                    b = b + a * jnp.where(inside, down(b, d), 0.0)
                    a = a * jnp.where(inside, down(a, d), 1.0)
                cell = b + a * carry
                carry = spread(b, 7) + spread(a, 7) * carry
                cell_buf[here, :] = cell
                outs.append(outgate * cell)
            hid_buf[block, pl.ds(at, STEP), :] = jnp.concatenate(outs, axis=0).astype(BF)
            return carry

        lax.fori_loop(0, steps, forward, zeros, unroll=16)

        def backward(n, state):
            adj_in, decay_in, later, total = state
            i = steps - 1 - n
            at = pl.multiple_of(i * STEP, STEP)
            grads = cot_ref[pl.ds(at, STEP), z_at].astype(F32)
            parts = []
            for h in reversed(range(STEP // 8)):
                here = pl.ds(at + 8 * h, 8)
                cand = gate_buf[here, z_at]
                forget = gate_buf[here, f_at]
                outgate = gate_buf[here, o_at]
                keep = keep_ref[here, :]
                cell = cell_buf[here, :]
                first = at + 8 * h == 0
                before = cell_buf[pl.ds(jnp.maximum(at + 8 * h - 8, 0), 8), :]
                before = jnp.where(first, 0.0, before)
                prev = jnp.where(sub == 0, down(before, 1), down(cell, 1))
                g = grads[8 * h : 8 * h + 8]
                decay = forget * keep
                a = jnp.where(sub == 7, decay_in, up(decay, 1))
                b = g * outgate
                for d in (1, 2, 4):
                    inside = sub < 8 - d
                    b = b + a * jnp.where(inside, up(b, d), 0.0)
                    a = a * jnp.where(inside, up(a, d), 1.0)
                adj = b + a * adj_in
                adj_in = spread(b, 0) + spread(a, 0) * adj_in
                decay_in = spread(decay, 0)
                omf = 1.0 - forget
                scaled = adj * omf
                d_z = scaled * (1.0 - cand * cand)
                d_f = scaled * forget * (keep * prev - cand)
                d_o = g * cell * (outgate * (1.0 - outgate))
                parts.append((d_z, d_f, d_o))
            parts.reverse()
            new_later, new_total = [], []
            for gate, where in enumerate((z_at, f_at, o_at)):
                tiles = [part[gate].astype(BF) for part in parts]
                wide = [t.astype(F32) for t in tiles]
                dg_buf[block, 0, pl.ds(at, STEP), gate * LANES : (gate + 1) * LANES] = jnp.concatenate(tiles, axis=0)
                follow = wide[1:] + [None]
                moved = []
                for t, nxt in zip(wide, follow):
                    edge = later[gate] if nxt is None else spread(nxt, 0)
                    moved.append(jnp.where(sub == 7, edge, up(t, 1)))
                dg_buf[block, 1, pl.ds(at, STEP), gate * LANES : (gate + 1) * LANES] = jnp.concatenate(moved, axis=0).astype(BF)
                new_later.append(spread(wide[0], 0))
                new_total.append(total[gate] + functools.reduce(jnp.add, wide))
            return adj_in, decay_in, tuple(new_later), tuple(new_total)

        triple = (zeros, zeros, zeros)
        _, _, _, total = lax.fori_loop(0, steps, backward, (zeros, zeros, triple, triple), unroll=8)
        for gate, where in enumerate((z_at, f_at, o_at)):
            db_ref[:, where] = total[gate]
        for copy in out_copies(block):
            copy.start()


def gates_call(at, ids, blocks, own, pieces, offset, bias, keep, cot, group):
    rows = blocks[0].shape[1]
    width = blocks[0].shape[2]
    half = own.shape[1]
    cols = 3 * group
    time = keep.shape[0]
    tile = min(256, cols)
    kernel = functools.partial(gates_kernel, at, rows, half, len(blocks), len(pieces), group, offset)
    return pl.pallas_call(
        kernel,
        out_shape=(
            jax.ShapeDtypeStruct((time, group), BF),
            jax.ShapeDtypeStruct((2, time, cols), BF),
            jax.ShapeDtypeStruct((8, cols), F32),
        ),
        in_specs=[smem_spec()]
        + [any_spec()] * (len(blocks) + 1 + len(pieces))
        + [vmem_spec()] * 3,
        out_specs=(any_spec(), any_spec(), vmem_spec()),
        scratch_shapes=[
            pltpu.VMEM((time, width), BF),
            pltpu.VMEM((2, 2 * width, tile), BF),
            pltpu.VMEM((time, cols), F32),
            pltpu.VMEM((time, LANES), F32),
            pltpu.VMEM((group // LANES, time, LANES), BF),
            pltpu.VMEM((group // LANES, 2, time, 3 * LANES), BF),
            pltpu.SemaphoreType.DMA((len(blocks),)),
            pltpu.SemaphoreType.DMA((2, len(pieces) + 2)),
            pltpu.SemaphoreType.DMA((group // LANES, 4)),
        ],
        compiler_params=pltpu.CompilerParams(vmem_limit_bytes=VMEM_BYTES),
        cost_estimate=cost(2 * time * 2 * width * cols * 1.5),
        name="gates",
    )(ids, *blocks, own, *pieces, bias, keep, cot)


def inputs_kernel(at_id, k, half, n_pieces, chunk, units, ids, *refs):
    dg_refs = refs[: len(units)]
    groups = 1 + max(g for g, _ in units)
    at = len(units) + groups * (n_pieces + 1)
    weights = [refs[len(units) + g * (n_pieces + 1) : len(units) + (g + 1) * (n_pieces + 1)] for g in range(groups)]
    out_ref = refs[at]
    w_buf, dg_buf, acc, w_sem, dg_sem = refs[at + 1 :]
    rows, width = acc.shape
    row = pl.multiple_of(ids[at_id["far"] + k] * rows, rows)

    def w_copies(g, col, size, slot):
        copies = []
        for i in range(n_pieces + 2):
            if i < 2:
                source = weights[g][0].at[i, :, pl.ds(col, size)]
                block = ids[at_id["pieces"]] + i
            else:
                source = weights[g][i - 1].at[:, pl.ds(col, size)]
                block = ids[at_id["pieces"] + i - 1]
            start = pl.multiple_of(block * half, half)
            copies.append(
                pltpu.make_async_copy(
                    source, w_buf.at[slot, pl.ds(start, half), pl.ds(0, size)], w_sem.at[slot, i]
                )
            )
        return copies

    firsts = [sum(ref.shape[2] for ref in dg_refs[:u]) for u in range(len(units))]

    def dg_copy(u):
        cols = dg_refs[u].shape[2]
        return pltpu.make_async_copy(
            dg_refs[u].at[:, pl.ds(row, rows), :], dg_buf.at[:, :, pl.ds(firsts[u], cols)], dg_sem.at[u]
        )

    jobs = []
    for u, (g, offset) in enumerate(units):
        cols = dg_refs[u].shape[2]
        for col in range(0, cols, chunk):
            jobs.append((u, col, (g, offset + col, min(chunk, cols - col))))
    step = 768 if width % 768 == 0 else LANES
    dg_copy(0).start()
    for copy in w_copies(*jobs[0][2], 0):
        copy.start()
    for u in range(1, len(units)):
        dg_copy(u).start()
    for n, (u, col, job) in enumerate(jobs):
        slot, size = n % 2, job[2]
        if n + 1 < len(jobs):
            for copy in w_copies(*jobs[n + 1][2], 1 - slot):
                copy.start()
        if col == 0:
            dg_copy(u).wait()
        for copy in w_copies(*job, slot):
            copy.wait()
        here = slice(firsts[u] + col, firsts[u] + col + size)

        @pl.loop(0, width // step)
        def _(k):
            at = pl.ds(pl.multiple_of(k * step, step), step)
            total = None if n == 0 else acc[:, at]
            for tap in range(2):
                feats = pl.ds(pl.multiple_of(tap * width + k * step, LANES), step)
                part = lax.dot_general(
                    dg_buf[tap, :, here],
                    w_buf[slot, feats, :size],
                    (((1,), (1,)), ((), ())),
                    preferred_element_type=F32,
                )
                total = part if total is None else total + part
            if n + 1 < len(jobs):
                acc[:, at] = total
            else:
                out_ref[:, at] = total.astype(out_ref.dtype)


def inputs_call(at, ids, k, dgs, weights, units, rows, width, dtype):
    n_pieces = len(weights[0]) - 1
    half = weights[0][0].shape[1]
    cols = sum(d.shape[2] for d in dgs)
    chunk = 768
    flat = [w for group in weights for w in group]
    return pl.pallas_call(
        functools.partial(inputs_kernel, at, k, half, n_pieces, chunk, units),
        out_shape=jax.ShapeDtypeStruct((rows, width), dtype),
        in_specs=[smem_spec()] + [any_spec()] * (len(dgs) + len(flat)),
        out_specs=vmem_spec(),
        scratch_shapes=[
            pltpu.VMEM((2, 2 * width, chunk), BF),
            pltpu.VMEM((2, rows, cols), BF),
            pltpu.VMEM((rows, width), F32),
            pltpu.SemaphoreType.DMA((2, n_pieces + 2)),
            pltpu.SemaphoreType.DMA((len(dgs),)),
        ],
        compiler_params=pltpu.CompilerParams(vmem_limit_bytes=VMEM_BYTES),
        cost_estimate=cost(2 * rows * 2 * width * cols),
        name="grad_in",
    )(ids, *dgs, *flat)


def turn_kernel(at, n_blocks, half, ids, *refs):
    x_refs, out_ref = refs[:n_blocks], refs[n_blocks]
    x_buf, t_buf, sem = refs[n_blocks + 1 :]
    rows = x_buf.shape[1]
    core = ids[at["core"]]
    jobs = [(i, m) for i in range(n_blocks) for m in range(2)]

    def load(n):
        i, m = jobs[n]
        batch = core if m == 0 else 1 - core
        return pltpu.make_async_copy(x_refs[i].at[batch], x_buf.at[n % 2], sem.at[n % 2])

    load(0).start()
    for n, (i, m) in enumerate(jobs):
        if n + 1 < len(jobs):
            load(n + 1).start()
        load(n).wait()
        t_buf[...] = x_buf[n % 2].T
        column = pl.ds(pl.multiple_of(ids[at["time"] + i] * rows, rows), rows)
        for q in range(out_ref.shape[1]):
            start = pl.multiple_of(q * 2 * half + core * half, 16)
            out_ref[m, q, :, column] = t_buf[pl.ds(start, half), :]


def turn_call(at, ids, blocks, per_tap, half, time):
    _, rows, width = blocks[0].shape
    return pl.pallas_call(
        functools.partial(turn_kernel, at, len(blocks), half),
        out_shape=jax.ShapeDtypeStruct((2, per_tap, half, time), BF),
        in_specs=[smem_spec()] + [any_spec()] * len(blocks),
        out_specs=vmem_spec(),
        scratch_shapes=[
            pltpu.VMEM((2, rows, width), BF),
            pltpu.VMEM((width, rows), BF),
            pltpu.SemaphoreType.DMA((2,)),
        ],
        compiler_params=pltpu.CompilerParams(vmem_limit_bytes=VMEM_BYTES),
        cost_estimate=cost(7 * 10**9),
        name="turn",
    )(ids, *blocks)


def weight_kernel(count, x_ref, *refs):
    mine_refs, other_refs, out_ref = refs[:count], refs[count : 2 * count], refs[2 * count]
    x_buf, dg_buf, out_buf, x_sem, in_sem, out_sem = refs[2 * count + 1 :]
    pieces, half, time = x_ref.shape[1:]
    jobs, col = [], 0
    for u in range(count):
        for tap in range(2):
            jobs.append((u, tap, col))
        col += mine_refs[u].shape[2]

    def x_copy(m):
        return pltpu.make_async_copy(x_ref.at[m], x_buf.at[m], x_sem.at[m])

    def dg_copies(n):
        u, tap, _ = jobs[n]
        size = mine_refs[u].shape[2]
        return [
            pltpu.make_async_copy(ref.at[tap], dg_buf.at[n % 2, m, :, pl.ds(0, size)], in_sem.at[n % 2, m])
            for m, ref in enumerate((mine_refs[u], other_refs[u]))
        ]

    def out_copy(n):
        u, tap, first = jobs[n]
        size = mine_refs[u].shape[2]
        return pltpu.make_async_copy(
            out_buf.at[n % 2, :, :, pl.ds(0, size)], out_ref.at[tap, :, :, pl.ds(first, size)], out_sem.at[n % 2]
        )

    x_copy(0).start()
    for copy in dg_copies(0):
        copy.start()
    x_copy(1).start()
    for n, (u, tap, first) in enumerate(jobs):
        size = mine_refs[u].shape[2]
        slot = n % 2
        if n + 1 < len(jobs):
            for copy in dg_copies(n + 1):
                copy.start()
        if n == 0:
            x_copy(0).wait()
            x_copy(1).wait()
        for copy in dg_copies(n):
            copy.wait()
        if n >= 2:
            out_copy(n - 2).wait()
        tile = 256 if size % 256 == 0 else LANES

        @pl.loop(0, size // tile)
        def _(k):
            at = pl.ds(pl.multiple_of(k * tile, tile), tile)
            total = None
            for m in range(2):
                part = jnp.dot(
                    x_buf[m].reshape(pieces * half, time), dg_buf[slot, m, :, at], preferred_element_type=F32
                )
                total = part if total is None else total + part
            out_buf[slot, :, :, at] = total.reshape(pieces, half, tile)

        out_copy(n).start()
    for n in range(max(0, len(jobs) - 2), len(jobs)):
        out_copy(n).wait()


def weight_call(x_t, mine, other):
    _, pieces, half, time = x_t.shape
    cols = sum(d.shape[2] for d in mine)
    most = max(d.shape[2] for d in mine)
    return pl.pallas_call(
        functools.partial(weight_kernel, len(mine)),
        out_shape=jax.ShapeDtypeStruct((2, pieces, half, cols), F32),
        in_specs=[any_spec()] * (1 + 2 * len(mine)),
        out_specs=any_spec(),
        scratch_shapes=[
            pltpu.VMEM(x_t.shape, BF),
            pltpu.VMEM((2, 2, time, most), BF),
            pltpu.VMEM((2, pieces, half, most), F32),
            pltpu.SemaphoreType.DMA((2,)),
            pltpu.SemaphoreType.DMA((2, 2)),
            pltpu.SemaphoreType.DMA((2,)),
        ],
        compiler_params=pltpu.CompilerParams(vmem_limit_bytes=VMEM_BYTES),
        cost_estimate=cost(8 * pieces * half * time * cols),
        name="grad_w",
    )(x_t, *mine, *other)


def place_kernel(at_id, count, spans, feats, width, ids, *refs):
    parts, out_ref = refs[:count], refs[-4]
    buf, in_sem, out_sem = refs[-3:]
    half = buf.shape[1]
    loads = [pltpu.make_async_copy(parts[i], buf.at[i], in_sem.at[i]) for i in range(count)]
    for copy in loads:
        copy.start()
    stores = []
    for i in range(count):
        loads[i].wait()
        row = pl.multiple_of(ids[at_id["place"] + 2 * i] * half, half)
        col = 0
        for start, size in spans:
            for gate in range(3):
                at = pl.multiple_of(gate * width + ids[at_id["place"] + 2 * i + 1] * feats + start, LANES)
                stores.append(
                    pltpu.make_async_copy(
                        buf.at[i, :, pl.ds(col, size)],
                        out_ref.at[pl.ds(row, half), pl.ds(at, size)],
                        out_sem.at[len(stores)],
                    )
                )
                stores[-1].start()
                col += size
    for copy in stores:
        copy.wait()


def place_call(at, ids, parts, out, spans, feats, rows, width):
    half, cols = parts[0].shape
    extra = [] if out is None else [out]
    return pl.pallas_call(
        functools.partial(place_kernel, at, len(parts), spans, feats, width),
        out_shape=jax.ShapeDtypeStruct((rows, 3 * width), F32),
        in_specs=[smem_spec()] + [any_spec()] * (len(parts) + len(extra)),
        out_specs=any_spec(),
        scratch_shapes=[
            pltpu.VMEM((len(parts), half, cols), F32),
            pltpu.SemaphoreType.DMA((len(parts),)),
            pltpu.SemaphoreType.DMA((3 * len(spans) * len(parts),)),
        ],
        input_output_aliases={1 + len(parts): 0} if extra else {},
        compiler_params=pltpu.CompilerParams(vmem_limit_bytes=VMEM_BYTES),
        cost_estimate=cost(5 * 10**9),
        name="place",
    )(ids, *parts, *extra)


def after(a, *others):
    return lax.optimization_barrier((a,) + others)[0] if others else a


class Links:
    def __init__(self):
        self.n_stream = lax.axis_size("stream")
        self.n_stretch = lax.axis_size("stretch")
        self.n_x = self.n_stretch // 2
        self.hops = self.n_stream // 2
        self.order = ring_order(self.n_stream)
        self.place_of = [self.order.index(i) for i in range(self.n_stream)]
        self.pairs = [self.ring_pairs(True), self.ring_pairs(False)]
        table = [self.numbers(s, p) for s in range(self.n_stretch) for p in range(self.n_stream)]
        self.at, total = {}, 0
        for name, numbers in table[0].items():
            self.at[name] = total
            total += len(numbers)
        flat = jnp.array(np.array([sum(row.values(), []) for row in table], np.int32))
        me = lax.axis_index("stretch") * self.n_stream + lax.axis_index("stream")
        self.ids = lax.dynamic_index_in_dim(flat, me, 0, False)
        self.x, self.c, self.p = (self.number(name) for name in ("x", "core", "stream"))

    def numbers(self, s, p):
        n, hops = self.n_stream, self.hops
        x, c, r = s // 2, s % 2, self.place_of[p]
        sign = 1 - 2 * c

        def owner(steps):
            return self.order[(r + sign * steps) % n]

        pieces = [2 * p]
        for t in range(1, hops + 1):
            pieces += [2 * owner(-t) + c, 2 * owner(t) + (1 - c)]
            if t < hops:
                pieces += [2 * owner(t) + c, 2 * owner(-t) + (1 - c)]
        far = [x ^ k for k in range(self.n_x)]
        return {
            "x": [x],
            "core": [c],
            "stream": [p],
            "time": [i * 2 + c for i in far] + [i * 2 + 1 - c for i in far],
            "pieces": pieces,
            "far": far,
            "place": [v for core in (c, 1 - c) for i in far for v in (core, i)],
            "forth": [owner(hops - t) for t in range(hops)],
            "back": [owner(t + 1 - hops) for t in range(hops - 1)],
        }

    def number(self, name, i=0):
        return self.ids[self.at[name] + i]

    def ring_pairs(self, forward):
        pairs = []
        for st in range(self.n_stretch):
            up = (st % 2 == 0) == forward
            for i in range(self.n_stream):
                j = (self.place_of[i] + (1 if up else -1)) % self.n_stream
                pairs.append((st * self.n_stream + i, st * self.n_stream + self.order[j]))
        return pairs

    def long(self, a):
        return lax.ppermute(a, ("stretch", "stream"), self.pairs[0])

    def short(self, a):
        return lax.ppermute(a, ("stretch", "stream"), self.pairs[1])

    def to_core(self, a):
        return lax.ppermute(a, "stretch", [(i, i ^ 1) for i in range(self.n_stretch)])

    def to_x(self, a, k):
        return lax.ppermute(a, "stretch", [(i, i ^ (2 * k)) for i in range(self.n_stretch)])

    def by_x(self, options):
        out = options[0]
        for i in range(1, self.n_x):
            out = jnp.where(self.x == i, options[i], out)
        return out

    def in_x_order(self, by_k):
        return [self.by_x([by_k[i ^ j] for j in range(self.n_x)]) for i in range(self.n_x)]

    def by_core(self, mine, other):
        return jnp.where(self.c == 0, mine, other), jnp.where(self.c == 0, other, mine)


class Gather:
    def __init__(self, links, mine):
        self.links = links
        self.forth = self.back = mine
        self.step = 0
        self.waiting, self.crossed, self.group, self.marks = [], [], [], []

    def cross(self):
        self.crossed = []
        for piece in self.waiting:
            self.crossed.append(self.links.to_core(piece))
            self.group += [piece, self.crossed[-1]]
        self.waiting = []

    def hop(self, *deps):
        links = self.links
        deps = tuple(self.crossed) + deps
        self.step += 1
        forth = links.long(after(self.forth, *deps))
        arriving = [forth]
        if self.step < links.hops:
            self.back = links.short(after(self.back, *deps))
            arriving.append(self.back)
            self.marks = arriving
        self.forth = forth
        self.cross()
        self.waiting = arriving

    def hops_until(self, last, *deps):
        while self.step < last:
            self.hop(*deps)
            deps = ()


class Reduce:
    def __init__(self, links, local):
        self.links, self.local = links, local
        self.forth = self.back = None
        self.step = 0

    def part(self, shard, incoming, deps):
        part = lax.dynamic_index_in_dim(self.local, shard, 0, False)
        part = part if incoming is None else part + incoming.astype(F32)
        return after(part.astype(BF), *deps)

    def hop(self, *deps):
        links, t = self.links, self.step
        self.step += 1
        sent = [self.part(links.number("forth", t), self.forth, deps)]
        self.forth = links.long(sent[0])
        if t < links.hops - 1:
            sent.append(self.part(links.number("back", t), self.back, deps))
            self.back = links.short(sent[1])
        return sent

    def hops_until(self, last, *deps):
        sent = []
        while self.step < last:
            sent = self.hop(*deps)
            deps = ()
        return sent

    def total(self, *deps):
        own = lax.dynamic_index_in_dim(self.local, self.links.p, 0, False)
        return own + after(self.forth, *deps).astype(F32) + self.back.astype(F32)


def shards(inputs, weight, bias, reset, cotangent):
    batches, _, rows, width = inputs.shape
    shard_rows, gate_cols = weight.shape
    links = Links()
    n_x, hops, x, c = links.n_x, links.hops, links.x, links.c
    at, ids = links.at, links.ids
    others_x = range(1, n_x)
    time = rows * links.n_stretch
    half = shard_rows // 2
    per_tap = links.n_stream // 2
    feats = width // n_x
    own_rows = time // n_x

    tiles = -(-feats // LANES)
    counts = [tiles // 5 + (1 if u in (0, 1, 3, 4)[: tiles % 5] else 0) for u in range(5)]
    sizes = [count * LANES for count in counts]
    starts = [sum(sizes[:u]) for u in range(5)]
    reals = [min(size, feats - start) for start, size in zip(starts, sizes)]
    members = [[0], [1, 2], [3, 4]]
    place_in_group = [(0, 0), (1, 0), (1, 3 * sizes[1]), (2, 0), (2, 3 * sizes[3])]
    grad_members = [[0, 1, 2], [3, 4]]

    def columns(a, u):
        options = []
        for i in range(n_x):
            parts = []
            for gate in range(3):
                first_col = gate * width + i * feats + starts[u]
                part = a[..., first_col : first_col + reals[u]]
                if reals[u] < sizes[u]:
                    part = jnp.pad(part, [(0, 0)] * (a.ndim - 1) + [(0, sizes[u] - reals[u])])
                parts.append(part)
            options.append(jnp.concatenate(parts, axis=-1))
        return links.by_x(options)

    def halves(g):
        parts = [columns(weight, u) for u in members[g]]
        return jnp.concatenate(parts, axis=1).reshape(2, half, -1)

    def mine_of(own, *deps):
        return after(lax.dynamic_index_in_dim(own, c, 0, False), *deps)

    tokens = inputs.reshape(batches, rows, width)
    cots = cotangent.reshape(batches, rows, width)
    mid = batches // 2

    own_weights = [halves(0)]
    first = Gather(links, mine_of(own_weights[0]))
    first.hop()
    core_tokens = links.to_core(tokens)
    x_first = [links.to_x(tokens[:mid], k) for k in others_x]
    cot_mine = lax.dynamic_index_in_dim(cots, c, 0, False)
    cot_other = links.to_core(lax.dynamic_index_in_dim(cots, 1 - c, 0, False))
    reset_mine = reset.reshape(batches, rows).astype(F32)
    reset_pair = jnp.stack(links.by_core(reset_mine, links.to_core(reset_mine)), axis=1)
    own_weights += [halves(1), halves(2)]
    first.hop(core_tokens, cot_other, reset_pair)
    first.hops_until(hops - 1)
    first.hop(*x_first)
    second = Gather(links, mine_of(own_weights[1], *first.marks))
    x_second = [links.to_x(after(tokens[mid:], *x_first), k) for k in others_x]

    cot_pair = jnp.concatenate(links.by_core(cot_mine, cot_other), axis=0)

    def cot_unit(u, *deps):
        parts = []
        for i in range(n_x):
            first_col = i * feats + starts[u]
            part = cot_pair[:, first_col : first_col + reals[u]]
            if reals[u] < sizes[u]:
                part = jnp.pad(part, [(0, 0), (0, sizes[u] - reals[u])])
            parts.append(part)
        by_k = [links.by_x(parts)]
        for k in others_x:
            leaving = links.by_x([parts[i ^ k] for i in range(n_x)])
            by_k.append(links.to_x(after(leaving, *deps), k))
        return jnp.concatenate(links.in_x_order(by_k), axis=0), by_k[1:]

    cot_units, cot_marks = [None] * 5, [None] * 5
    cot_units[0], cot_marks[0] = cot_unit(0, *x_first)
    reset_parts = [reset_pair] + [links.to_x(after(reset_pair, *x_first), k) for k in others_x]
    keep = jnp.stack(links.in_x_order(reset_parts), axis=1)
    keep = 1.0 - lax.dynamic_index_in_dim(keep, c, 0, False).reshape(time, 1)
    second.hop()
    first.cross()
    core_first = [links.to_core(a) for a in x_first]
    second.hop(*first.crossed, *core_first)
    second.hops_until(hops - 1, *x_second, *cot_marks[0], *reset_parts[1:])
    core_second = [links.to_core(a) for a in x_second]
    from_x = [jnp.concatenate(pair, axis=0) for pair in zip(x_first, x_second)]
    from_both = [jnp.concatenate(pair, axis=0) for pair in zip(core_first, core_second)]
    blocks = [tokens] + from_x + [core_tokens] + from_both
    for u in range(1, 5):
        cot_units[u], cot_marks[u] = cot_unit(u, *x_second)

    hiddens, dgs, others, biases = [], [], [], []

    def gates(u, gather, *deps):
        g, offset = place_in_group[u]
        bias_u = after(columns(bias[None, :], u), *deps)
        hid, dg, db = gates_call(
            at, ids, blocks, own_weights[g], gather.group, offset, bias_u, keep, cot_units[u], sizes[u]
        )
        hiddens.append(hid[:, : reals[u]])
        dgs.append(dg)
        others.append(links.to_core(dg))
        biases.append(jnp.sum(db, axis=0).reshape(3, sizes[u])[:, : reals[u]])
        return db

    def local_gradient(units):
        local = weight_call(x_t, [dgs[u] for u in units], [others[u] for u in units])
        return local.reshape(links.n_stream, half, -1)

    done = gates(0, first)
    second.hop(done)
    third = Gather(links, mine_of(own_weights[2], done, *second.marks))
    third.hop(*cot_marks[1], *cot_marks[2])
    second.cross()

    if half % 16 == 0 and rows % LANES == 0:
        x_t = turn_call(at, ids, blocks, per_tap, half, time)
    else:
        whole = jnp.zeros((batches, time, width), BF)
        for i, block in enumerate(blocks):
            whole = lax.dynamic_update_slice(whole, block, (0, links.number("time", i) * rows, 0))
        x_t = whole.transpose(0, 2, 1).reshape(batches, per_tap, 2, half, time)
        x_t = lax.dynamic_index_in_dim(x_t, c, 2, False)
        x_t = jnp.stack(links.by_core(x_t[0], x_t[1]))

    third.hop(x_t, *second.crossed)
    done = gates(1, second)
    third.hops_until(hops - 1, done, *cot_marks[3], *cot_marks[4])
    done = gates(2, second)
    third.hop(done)
    third.cross()

    red_first = Reduce(links, local_gradient(grad_members[0]))
    sent = red_first.hop()
    done = gates(3, third, *sent)
    sent = red_first.hop(done)
    done = gates(4, third, *sent)
    sent = red_first.hops_until(hops - 1, done)

    hid = jnp.concatenate(hiddens, axis=1).reshape(n_x, own_rows, feats)
    hid_by_k = [lax.dynamic_index_in_dim(hid, x, 0, False)]
    for k in others_x:
        hid_by_k.append(links.to_x(lax.dynamic_index_in_dim(hid, links.number("far", k), 0, False), k))
    hid = jnp.concatenate(links.in_x_order(hid_by_k), axis=1).reshape(2, rows, width)
    hid_mine = lax.dynamic_index_in_dim(hid, c, 0, False)
    hid_other = links.to_core(lax.dynamic_index_in_dim(hid, 1 - c, 0, False))
    hidden = jnp.stack(links.by_core(hid_mine, hid_other)).reshape(inputs.shape)

    pieces = [[own] + gather.group for own, gather in zip(own_weights, (first, second, third))]

    def d_inputs(k, dtype, *deps):
        now = [after(dgs[0], *deps)] + dgs[1:]
        return inputs_call(at, ids, k, now, pieces, place_in_group, own_rows, width, dtype)

    red_last = Reduce(links, local_gradient(grad_members[1]))
    sent = red_first.hop(red_last.local[0, 0, :1], *hid_by_k[1:])
    sent = red_last.hop(*sent)
    d_others = [d_inputs(k, BF, *sent) for k in others_x]
    d_received = [links.to_x(a, k) for a, k in zip(d_others, others_x)]

    bias_part = jnp.concatenate(biases, axis=1)
    bit = 1
    while bit < links.n_stream:
        swaps = [(i, i ^ bit) for i in range(links.n_stream)]
        bias_part = bias_part + lax.ppermute(bias_part, "stream", swaps)
        bit *= 2
    bias_part = bias_part + links.to_core(bias_part)
    bias_parts = [bias_part] + [links.to_x(bias_part, k) for k in others_x]
    grad_bias = jnp.stack(links.in_x_order(bias_parts), axis=1).reshape(gate_cols)

    aligned = feats % LANES == 0
    parts = [[None] * n_x for _ in sizes]

    def spread(total):
        scale = jnp.maximum(jnp.max(jnp.abs(total), axis=0, keepdims=True), 1e-30) * 2.0**-15
        coded, scale = lax.optimization_barrier(((total / scale).astype(jnp.float16), scale))
        scale = jnp.broadcast_to(scale, (8, scale.shape[1]))
        got = [(coded, scale)] + [(links.to_x(coded, k), links.to_x(scale, k)) for k in others_x]
        values = [a.astype(F32) * b[:1] for a, b in got]
        return values, [links.to_core(a) for a in values]

    def put(grad_weight, units, got, crossed):
        spans = [(starts[u], sizes[u]) for u in units]
        if aligned:
            return place_call(at, ids, got + crossed, grad_weight, spans, feats, shard_rows, width)
        got = [jnp.concatenate(links.by_core(a, b), axis=0) for a, b in zip(got, crossed)]
        col = 0
        ordered = links.in_x_order(got)
        for u in units:
            for i in range(n_x):
                piece = ordered[i][:, col : col + 3 * sizes[u]]
                parts[u][i] = piece.reshape(shard_rows, 3, sizes[u])[:, :, : reals[u]]
            col += 3 * sizes[u]
        return None

    got, crossed = spread(red_first.total(*d_others))
    sent = red_last.hop(*d_others)
    d_mine = d_inputs(0, F32, *sent)
    red_last.hops_until(hops - 1, d_mine, grad_bias, hidden, *got[1:])
    red_last.hop()
    grad_weight = put(None, grad_members[0], got, crossed)
    got, crossed = spread(red_last.total(*d_received))
    for a in d_received:
        d_mine = d_mine + a.astype(F32)
    d_mine = d_mine.reshape(2, rows, width)
    d_keep = lax.dynamic_index_in_dim(d_mine, c, 0, False)
    d_other = links.to_core(lax.dynamic_index_in_dim(d_mine, 1 - c, 0, False))
    grad_inputs = jnp.stack(links.by_core(d_keep, d_other)).reshape(inputs.shape)
    grad_weight = put(grad_weight, grad_members[1], got, crossed)
    if not aligned:
        grad_weight = jnp.concatenate(
            [parts[u][i][:, gate] for gate in range(3) for i in range(n_x) for u in range(5)], axis=1
        )
    return (hidden, grad_inputs, grad_weight, grad_bias)


def solution(mesh):
    in_specs = (
        P(None, "stream", "stretch", None),
        P("stream", None),
        P(),
        P(None, "stream", "stretch"),
        P(None, "stream", "stretch", None),
    )
    out_specs = (
        P(None, "stream", "stretch", None),
        P(None, "stream", "stretch", None),
        P("stream", None),
        P(),
    )
    return jax.shard_map(shards, mesh=mesh, in_specs=in_specs, out_specs=out_specs, check_vma=False)
```

time: 757 us -> 619 us (0.82)
  blocking collectives: 68.9 us -> 0 us
  local copies, waits for them, and re-layouts: 117 us -> 48.4 us
  Pallas kernels: 282 us -> 234 us
  waiting for transfers between devices: 126 us -> 163 us
  starting transfers between devices: 51.5 us -> 69.7 us
    psum x2 -> x0, blocking collectives: 52.7 us -> none  [the longest x1 41.3 us: shards(): bias_part = lax.psum(bias_part, 'stream')]
    pallas_call x17 -> x7, Pallas kernels: 176 us -> 130 us  [the longest x2 52.9 us: inputs_call(): pl.pallas_call(functools.partial(inputs_kernel, at, k, half, n_pieces, ch...]
    ppermute x59 -> x91, waiting for transfers between devices: 126 us -> 163 us  [the longest x20 90.3 us: long(): return lax.ppermute(a, ('stretch', 'stream'), self.pairs[0])]
    select_n x16 -> x15, other arithmetic: 43.9 us -> 11.7 us  [the longest x14 10.3 us: by_x(): out = jnp.where(self.x == i, options[i], out)]
    convert_element_type x1 -> x9, other arithmetic: 0.01 us -> 25.7 us  [the longest x6 21.1 us: part(): return after(part.astype(BF), *deps)]
    concatenate x11 -> x4, local copies, waits for them, and re-layouts: 29 us -> 4.36 us  [the longest x1 1.35 us: shards(): from_x = [jnp.concatenate(pair, axis=0) for pair in zip(x_first, x_second)]]
    ppermute x59 -> x91, starting transfers between devices: 51.5 us -> 69.7 us  [the longest x15 22 us: short(): return lax.ppermute(a, ('stretch', 'stream'), self.pairs[1])]
    all_gather x1 -> x0, blocking collectives: 16.2 us -> none  [shards(): resets = lax.all_gather(reset.reshape(batches, rows).astype(F32), 'stretch')]
  transfers between devices with their start and end apart: 59 -> 91, of which waited for: 14 -> 20; matrix products, arithmetic and copies ran while one was open for 18% -> 17% of each run, Pallas kernels for 38% -> 37%
where the time goes in v2:
time: 619 us; the launch traced here: 610 us
  Pallas kernels  234 us (38%)
  waiting for transfers between devices  163 us (26%)
  other arithmetic  70.2 us (11%)
  starting transfers between devices  69.7 us (11%)
  local copies, waits for them, and re-layouts  48.4 us (8%)
  between operations  24.4 us (4%)
    pallas_call x5, Pallas kernels, gates_call(): pl.pallas_call(kernel, out_shape=(jax.ShapeDtypeStruct((time, group), BF)...  103 us
    ppermute x20, waiting for transfers between devices, long(): return lax.ppermute(a, ('stretch', 'stream'), self.pairs[0])  90.3 us
    pallas_call x2, Pallas kernels, inputs_call(): pl.pallas_call(functools.partial(inputs_kernel, at, k, half, n_pieces, ch...  52.9 us
    pallas_call x2, Pallas kernels, weight_call(): pl.pallas_call(functools.partial(weight_kernel, len(mine)), out_shape=jax...  52.6 us
    ppermute x15, waiting for transfers between devices, to_x(): lax.ppermute(a, 'stretch', [(i, i ^ 2 * k) for i in range(self.n_stretch)])  48.1 us
    ppermute x15, starting transfers between devices, short(): return lax.ppermute(a, ('stretch', 'stream'), self.pairs[1])  22 us
    convert_element_type x6, other arithmetic, part(): return after(part.astype(BF), *deps)  21.1 us
    ppermute x20, starting transfers between devices, long(): return lax.ppermute(a, ('stretch', 'stream'), self.pairs[0])  18.1 us
  transfers between devices with their start and end apart: 91, of which 20 were waited for; matrix products, arithmetic and copies ran while one was open for 17% of the time, Pallas kernels for 37%

profile of v2, /device:TPU:0, one launch (start us, length us, event | category | flops | bytes accessed | tf_op | source)
XLA Modules:
  0.0 609.6 jit_solution(16440216251905796692)
XLA Ops:
  15.6 4.8 fusion.47
  29.7 6.6 %collective-permute-done.5.refs_5_.refs_6_ = bf16[288,768]{1,0:T(8,128)(2,1)S(1)} collective-permute-done((bf16[288,768]{1,0:T(8,128)(2,1)}, bf16[288,768]{1,0:T(8,128)(2,1)S(1)}, u32[]{:S(2)}, u32[]{:S(2)}) %collective-permute-start.5) | collective-permute-done | bytes 442400 | tf_op jit(solution)/shard_map/ppermute | solution.py:628
  43.5 5.7 collective-permute-done.11.refs_9_.refs_10_
  52.3 5.3 collective-permute-done.15.refs_13_.refs_14_
  64.2 6.2 %collective-permute-done.1 = bf16[1,256,2304]{2,1,0:T(8,128)(2,1)} collective-permute-done((bf16[1,256,2304]{2,1,0:T(8,128)(2,1)S(1)}, bf16[1,256,2304]{2,1,0:T(8,128)(2,1)}, u32[]{:S(2)}, u32[]{:S(2)}) %collective-permute-start.1) | collective-permute-done | bytes 1179680 | tf_op jit(solution)/shard_map/ppermute | solution.py:637
  75.7 12.2 %collective-permute-done.23.refs_5_.refs_21_ = bf16[288,1152]{1,0:T(8,128)(2,1)} collective-permute-done((bf16[288,1152]{1,0:T(8,128)(2,1)}, bf16[288,1152]{1,0:T(8,128)(2,1)}, u32[]{:S(2)}, u32[]{:S(2)}) %collective-permute-start.23) | collective-permute-done | bytes 663584 | tf_op jit(solution)/shard_map/ppermute | solution.py:628
  100.8 6.8 %collective-permute-done.27.refs_9_.refs_25_ = bf16[288,1152]{1,0:T(8,128)(2,1)} collective-permute-done((bf16[288,1152]{1,0:T(8,128)(2,1)}, bf16[288,1152]{1,0:T(8,128)(2,1)}, u32[]{:S(2)}, u32[]{:S(2)}) %collective-permute-start.27) | collective-permute-done | bytes 663584 | tf_op jit(solution)/shard_map/ppermute | solution.py:628
  113.9 22.1 %gates.5 = (bf16[1024,256]{1,0:T(8,128)(2,1)}, bf16[2,1024,768]{2,1,0:T(8,128)(2,1)}, f32[8,768]{1,0:T(8,128)}) custom-call(s32[39]{0:T(128)} %get-tuple-element.255.ids, bf16[2,256,2304]{2,1,0:T(8,128)(2,1)} %bitcast.206, bf16[2,256,2304]{2,1,0:T(8,128)(2,1)} %copy-done.26, bf16[2,256,2304]{2,1,0:T(8,128)(2,1)} %collective-permute-done.2.refs_2_, ...), custom_call_target="tpu_custom_call" | custom-call | flops 17394618368 | bytes 1000000 | tf_op jit(solution)/shard_map/gates/pallas_call | solution.py:262
  139.5 4.7 collective-permute-done.38
  153.4 7.2 %collective-permute-done.39.refs_5_.refs_36_ = bf16[288,1536]{1,0:T(8,128)(2,1)S(1)} collective-permute-done((bf16[288,1536]{1,0:T(8,128)(2,1)S(1)}, bf16[288,1536]{1,0:T(8,128)(2,1)S(1)}, u32[]{:S(2)}, u32[]{:S(2)}) %collective-permute-start.39) | collective-permute-done | bytes 884768 | tf_op jit(solution)/shard_map/ppermute | solution.py:628
  162.9 10.0 %turn.1.x_ref = bf16[2,4,288,1024]{3,2,1,0:T(8,128)(2,1)} custom-call(s32[39]{0:T(128)} %get-tuple-element.255.ids, bf16[2,256,2304]{2,1,0:T(8,128)(2,1)} %bitcast.207, bf16[2,256,2304]{2,1,0:T(8,128)(2,1)} %copy-done.26, bf16[2,256,2304]{2,1,0:T(8,128)(2,1)} %collective-permute-done.2.refs_2_, bf16[2,256,2304]{2,1,0:T(8,128)(2,1)} %copy-done.27), custom_call_target="tpu_custom_call" | custom-call | flops 11200000000 | bytes 1000000 | tf_op jit(solution)/shard_map/turn/pallas_call | solution.py:416
  176.3 22.0 %gates.6 = (bf16[1024,256]{1,0:T(8,128)(2,1)}, bf16[2,1024,768]{2,1,0:T(8,128)(2,1)}, f32[8,768]{1,0:T(8,128)}) custom-call(s32[39]{0:T(128)} %get-tuple-element.255.ids, bf16[2,256,2304]{2,1,0:T(8,128)(2,1)} %bitcast.208, bf16[2,256,2304]{2,1,0:T(8,128)(2,1)} %copy-done.26, bf16[2,256,2304]{2,1,0:T(8,128)(2,1)} %collective-permute-done.2.refs_2_, ...), custom_call_target="tpu_custom_call" | custom-call | flops 17394618368 | bytes 1000000 | tf_op jit(solution)/shard_map/gates/pallas_call | solution.py:262
  202.9 15.4 %gates.7 = (bf16[1024,128]{1,0:T(8,128)(2,1)}, bf16[2,1024,384]{2,1,0:T(8,128)(2,1)}, f32[8,384]{1,0:T(8,128)}) custom-call(s32[39]{0:T(128)} %get-tuple-element.255.ids, bf16[2,256,2304]{2,1,0:T(8,128)(2,1)} %bitcast.209, bf16[2,256,2304]{2,1,0:T(8,128)(2,1)} %copy-done.26, bf16[2,256,2304]{2,1,0:T(8,128)(2,1)} %collective-permute-done.2.refs_2_, ...), custom_call_target="tpu_custom_call" | custom-call | flops 8697309184 | bytes 1000000 | tf_op jit(solution)/shard_map/gates/pallas_call | solution.py:262
  235.8 16.3 %collective-permute-done.51.refs_15_.refs_46_ = bf16[288,1536]{1,0:T(8,128)(2,1)} collective-permute-done((bf16[288,1536]{1,0:T(8,128)(2,1)}, bf16[288,1536]{1,0:T(8,128)(2,1)}, u32[]{:S(2)}, u32[]{:S(2)}) %collective-permute-start.51) | collective-permute-done | bytes 884768 | tf_op jit(solution)/shard_map/ppermute | solution.py:631
  252.6 30.2 %grad_w.2 = f32[2,4,288,1920]{3,2,1,0:T(8,128)} custom-call(bf16[2,4,288,1024]{3,2,1,0:T(8,128)(2,1)} %turn.1.x_ref, bf16[2,1024,768]{2,1,0:T(8,128)(2,1)} %get-tuple-element.116.refs_0_, bf16[2,1024,768]{2,1,0:T(8,128)(2,1)} %get-tuple-element.97.refs_1_, bf16[2,1024,384]{2,1,0:T(8,128)(2,1)} %get-tuple-element.98.refs_2_, ...), custom_call_target="tpu_custom_call" | custom-call | flops 28991029248 | bytes 1000000 | tf_op jit(solution)/shard_map/grad_w/pallas_call | solution.py:499
  282.8 3.5 fusion.19
  288.4 22.0 %gates.8 = (bf16[1024,256]{1,0:T(8,128)(2,1)}, bf16[2,1024,768]{2,1,0:T(8,128)(2,1)}, f32[8,768]{1,0:T(8,128)}) custom-call(s32[39]{0:T(128)} %get-tuple-element.255.ids, bf16[2,256,2304]{2,1,0:T(8,128)(2,1)} %bitcast.210, bf16[2,256,2304]{2,1,0:T(8,128)(2,1)} %copy-done.26, bf16[2,256,2304]{2,1,0:T(8,128)(2,1)} %collective-permute-done.2.refs_2_, ...), custom_call_target="tpu_custom_call" | custom-call | flops 17394618368 | bytes 1000000 | tf_op jit(solution)/shard_map/gates/pallas_call | solution.py:262
  313.8 4.6 fusion.6
  320.6 22.0 %gates.9 = (bf16[1024,256]{1,0:T(8,128)(2,1)}, bf16[2,1024,768]{2,1,0:T(8,128)(2,1)}, f32[8,768]{1,0:T(8,128)}) custom-call(s32[39]{0:T(128)} %get-tuple-element.255.ids, bf16[2,256,2304]{2,1,0:T(8,128)(2,1)} %bitcast.211, bf16[2,256,2304]{2,1,0:T(8,128)(2,1)} %copy-done.26, bf16[2,256,2304]{2,1,0:T(8,128)(2,1)} %collective-permute-done.2.refs_2_, ...), custom_call_target="tpu_custom_call" | custom-call | flops 17394618368 | bytes 1000000 | tf_op jit(solution)/shard_map/gates/pallas_call | solution.py:262
  375.2 4.7 fusion.2
  384.6 20.1 %collective-permute-done.65 = bf16[288,1920]{1,0:T(8,128)(2,1)} collective-permute-done((bf16[288,1920]{1,0:T(8,128)(2,1)}, bf16[288,1920]{1,0:T(8,128)(2,1)}, u32[]{:S(2)}, u32[]{:S(2)}) %collective-permute-start.65) | collective-permute-done | bytes 1105952 | tf_op jit(solution)/shard_map/ppermute | solution.py:628
  404.7 3.2 fusion.5
  410.3 22.4 %grad_w.3 = f32[2,4,288,1536]{3,2,1,0:T(8,128)} custom-call(bf16[2,4,288,1024]{3,2,1,0:T(8,128)(2,1)} %turn.1.x_ref, bf16[2,1024,768]{2,1,0:T(8,128)(2,1)} %get-tuple-element.106.refs_0_.refs_3_, bf16[2,1024,768]{2,1,0:T(8,128)(2,1)} %get-tuple-element.107.refs_1_.refs_4_, bf16[2,1024,768]{2,1,0:T(8,128)(2,1)} %collective-permute-done.62.refs_2_, ...), custom_call_target="tpu_custom_call" | custom-call | flops 23192823808 | bytes 1000000 | tf_op jit(solution)/shard_map/grad_w/pallas_call | solution.py:499
  438.1 26.0 %grad_in.2 = bf16[512,2304]{1,0:T(8,128)(2,1)} custom-call(s32[39]{0:T(128)} %get-tuple-element.255.ids, bf16[2,1024,768]{2,1,0:T(8,128)(2,1)} %get-tuple-element.116.refs_0_, bf16[2,1024,768]{2,1,0:T(8,128)(2,1)} %get-tuple-element.97.refs_1_, bf16[2,1024,384]{2,1,0:T(8,128)(2,1)} %get-tuple-element.98.refs_2_, ...), custom_call_target="tpu_custom_call" | custom-call | flops 26091925504 | bytes 1000000 | tf_op jit(solution)/shard_map/grad_in/pallas_call | solution.py:372
  478.0 20.3 %collective-permute-done.80 = f32[8,1920]{1,0:T(8,128)S(1)} collective-permute-done((f32[8,1920]{1,0:T(8,128)S(1)}, f32[8,1920]{1,0:T(8,128)S(1)}, u32[]{:S(2)}, u32[]{:S(2)}) %collective-permute-start.80) | collective-permute-done | bytes 61472 | tf_op jit(solution)/shard_map/ppermute | solution.py:637
  501.2 4.0 fusion.9
  505.2 26.8 %grad_in.3 = f32[512,2304]{1,0:T(8,128)} custom-call(s32[39]{0:T(128)} %get-tuple-element.255.ids, bf16[2,1024,768]{2,1,0:T(8,128)(2,1)} %get-tuple-element.116.refs_0_, bf16[2,1024,768]{2,1,0:T(8,128)(2,1)} %get-tuple-element.97.refs_1_, bf16[2,1024,384]{2,1,0:T(8,128)(2,1)} %get-tuple-element.98.refs_2_, ...), custom_call_target="tpu_custom_call" | custom-call | flops 26091925504 | bytes 1000000 | tf_op jit(solution)/shard_map/grad_in/pallas_call | solution.py:372
  536.2 12.6 %collective-permute-done.81 = bf16[288,1536]{1,0:T(8,128)(2,1)S(1)} collective-permute-done((bf16[288,1536]{1,0:T(8,128)(2,1)}, bf16[288,1536]{1,0:T(8,128)(2,1)S(1)}, u32[]{:S(2)}, u32[]{:S(2)}) %collective-permute-start.81) | collective-permute-done | bytes 884768 | tf_op jit(solution)/shard_map/ppermute | solution.py:628
  556.9 9.8 %collective-permute-done.82 = bf16[288,1536]{1,0:T(8,128)(2,1)S(1)} collective-permute-done((bf16[288,1536]{1,0:T(8,128)(2,1)S(1)}, bf16[288,1536]{1,0:T(8,128)(2,1)S(1)}, u32[]{:S(2)}, u32[]{:S(2)}) %collective-permute-start.82) | collective-permute-done | bytes 884768 | tf_op jit(solution)/shard_map/ppermute | solution.py:628
  573.1 13.8 %collective-permute-done.86 = f32[8,1536]{1,0:T(8,128)S(1)} collective-permute-done((f32[8,1536]{1,0:T(8,128)S(1)}, f32[8,1536]{1,0:T(8,128)S(1)}, u32[]{:S(2)}, u32[]{:S(2)}) %collective-permute-start.86) | collective-permute-done | bytes 49184 | tf_op jit(solution)/shard_map/ppermute | solution.py:637
  589.0 8.3 %place.2.refs_4_ = f32[576,6912]{1,0:T(8,128)} custom-call(s32[39]{0:T(128)} %get-tuple-element.255.ids, f32[288,1920]{1,0:T(8,128)} %convert_multiply_fusion.refs_0_, f32[288,1920]{1,0:T(8,128)} %convert_multiply_fusion.1.refs_1_, f32[288,1920]{1,0:T(8,128)} %collective-permute-done.89.refs_2_, f32[288,1920]{1,0:T(8,128)} %collective-permute-done.90.refs_3_), custom_call_target="tpu_custom_call" | custom-call | flops 8000000000 | bytes 1000000 | tf_op jit(solution)/shard_map/place/pallas_call | solution.py:549
  602.5 6.7 %place.3 = f32[576,6912]{1,0:T(8,128)} custom-call(s32[39]{0:T(128)} %get-tuple-element.255.ids, f32[288,1536]{1,0:T(8,128)} %copy-done.5, f32[288,1536]{1,0:T(8,128)} %copy-done.6, f32[288,1536]{1,0:T(8,128)} %collective-permute-done.87.refs_2_, f32[288,1536]{1,0:T(8,128)} %collective-permute-done.88.refs_3_, ...), custom_call_target="tpu_custom_call", output_to_operand_aliasing={{}: (5, {})} | custom-call | flops 8000000000 | bytes 1000000 | tf_op jit(solution)/shard_map/place/pallas_call | solution.py:549
  (418 shorter events, 178.9 us)
Async XLA Ops:
  6.2 30.7 %collective-permute-start.9 = (bf16[256,2304]{1,0:T(8,128)(2,1)}, bf16[256,2304]{1,0:T(8,128)(2,1)}, u32[]{:S(2)}, u32[]{:S(2)}) collective-permute-start(bf16[256,2304]{1,0:T(8,128)(2,1)} %dynamic-slice_bitcast_fusion.3), channel_id=1, source_target_pairs={{0,8},{8,0},{16,24},{24,16},{1,9},{9,1},{17,25},{25,17},{2,10},{10... | collective-permute-start | bytes 3538952 | tf_op jit(solution)/shard_map/ppermute | solution.py:634
  6.6 30.2 %collective-permute-start.2 = (bf16[2,256,2304]{2,1,0:T(8,128)(2,1)S(1)}, bf16[2,256,2304]{2,1,0:T(8,128)(2,1)}, u32[]{:S(2)}, u32[]{:S(2)}) collective-permute-start(bf16[2,256,2304]{2,1,0:T(8,128)(2,1)S(1)} %bitcast.212), channel_id=1, source_target_pairs={{0,8},{8,0},{16,24},{24,16},{1,9},{9,1},{17,25},{25,17},{2,10},{10... | collective-permute-start | bytes 7077896 | tf_op jit(solution)/shard_map/ppermute | solution.py:634
  8.2 34.6 %collective-permute-start = (bf16[1,256,2304]{2,1,0:T(8,128)(2,1)}, bf16[1,256,2304]{2,1,0:T(8,128)(2,1)}, u32[]{:S(2)}, u32[]{:S(2)}) collective-permute-start(bf16[1,256,2304]{2,1,0:T(8,128)(2,1)} %get-tuple-element.211), channel_id=1, source_target_pairs={{0,16},{8,24},{16,0},{24,8},{1,17},{9,25},{17,1},{25,9},{2,18},{10... | collective-permute-start | bytes 3538952 | tf_op jit(solution)/shard_map/ppermute | solution.py:637
  42.9 27.6 %collective-permute-start.1 = (bf16[1,256,2304]{2,1,0:T(8,128)(2,1)S(1)}, bf16[1,256,2304]{2,1,0:T(8,128)(2,1)}, u32[]{:S(2)}, u32[]{:S(2)}) collective-permute-start(bf16[1,256,2304]{2,1,0:T(8,128)(2,1)S(1)} %copy-done.15), channel_id=1, source_target_pairs={{0,16},{8,24},{16,0},{24,8},{1,17},{9,25},{17,1},{25,9},{2,18},{10... | collective-permute-start | bytes 3538952 | tf_op jit(solution)/shard_map/ppermute | solution.py:637
  43.5 30.2 %collective-permute-start.3 = (bf16[1,256,2304]{2,1,0:T(8,128)(2,1)}, bf16[1,256,2304]{2,1,0:T(8,128)(2,1)}, u32[]{:S(2)}, u32[]{:S(2)}) collective-permute-start(bf16[1,256,2304]{2,1,0:T(8,128)(2,1)} %collective-permute-done), channel_id=1, source_target_pairs={{0,8},{8,0},{16,24},{24,16},{1,9},{9,1},{17,25},{25,17},{2,10},{10... | collective-permute-start | bytes 3538952 | tf_op jit(solution)/shard_map/ppermute | solution.py:634
  70.5 27.6 %collective-permute-start.4 = (bf16[1,256,2304]{2,1,0:T(8,128)(2,1)}, bf16[1,256,2304]{2,1,0:T(8,128)(2,1)}, u32[]{:S(2)}, u32[]{:S(2)}) collective-permute-start(bf16[1,256,2304]{2,1,0:T(8,128)(2,1)} %collective-permute-done.1), channel_id=1, source_target_pairs={{0,8},{8,0},{16,24},{24,16},{1,9},{9,1},{17,25},{25,17},{2,10},{10... | collective-permute-start | bytes 3538952 | tf_op jit(solution)/shard_map/ppermute | solution.py:634
  107.6 28.3 %collective-permute-start.31 = (bf16[288,1152]{1,0:T(8,128)(2,1)}, bf16[288,1152]{1,0:T(8,128)(2,1)}, u32[]{:S(2)}, u32[]{:S(2)}) collective-permute-start(bf16[288,1152]{1,0:T(8,128)(2,1)} %collective-permute-done.27.refs_9_.refs_25_), channel_id=1, source_target_pairs={{0,2},{1,0},{2,4},{3,1},{4,6},{5,3},{6,7},{7,5},{8,9},{9,11},{10,8... | collective-permute-start | bytes 1990664 | tf_op jit(solution)/shard_map/ppermute | solution.py:628
  110.1 29.4 %collective-permute-start.33 = (bf16[288,1152]{1,0:T(8,128)(2,1)}, bf16[288,1152]{1,0:T(8,128)(2,1)}, u32[]{:S(2)}, u32[]{:S(2)}) collective-permute-start(bf16[288,1152]{1,0:T(8,128)(2,1)} %collective-permute-done.29.refs_11_.refs_27_), channel_id=1, source_target_pairs={{0,1},{1,3},{2,0},{3,5},{4,2},{5,7},{6,4},{7,6},{8,10},{9,8},{10,1... | collective-permute-start | bytes 1990664 | tf_op jit(solution)/shard_map/ppermute | solution.py:631
  172.9 62.8 %collective-permute-start.55 = (bf16[2,1024,768]{2,1,0:T(8,128)(2,1)}, bf16[2,1024,768]{2,1,0:T(8,128)(2,1)}, u32[]{:S(2)}, u32[]{:S(2)}) collective-permute-start(bf16[2,1024,768]{2,1,0:T(8,128)(2,1)} %get-tuple-element.116.refs_0_), channel_id=1, source_target_pairs={{0,8},{8,0},{16,24},{24,16},{1,9},{9,1},{17,25},{25,17},{2,10},{10... | collective-permute-start | bytes 9437192 | tf_op jit(solution)/shard_map/ppermute | solution.py:634
  175.2 27.6 %collective-permute-start.45 = (bf16[288,1536]{1,0:T(8,128)(2,1)}, bf16[288,1536]{1,0:T(8,128)(2,1)}, u32[]{:S(2)}, u32[]{:S(2)}) collective-permute-start(bf16[288,1536]{1,0:T(8,128)(2,1)} %collective-permute-done.41.refs_7_.refs_38_), channel_id=1, source_target_pairs={{0,1},{1,3},{2,0},{3,5},{4,2},{5,7},{6,4},{7,6},{8,10},{9,8},{10,1... | collective-permute-start | bytes 2654216 | tf_op jit(solution)/shard_map/ppermute | solution.py:631
  198.3 54.3 %collective-permute-start.56 = (bf16[2,1024,768]{2,1,0:T(8,128)(2,1)}, bf16[2,1024,768]{2,1,0:T(8,128)(2,1)}, u32[]{:S(2)}, u32[]{:S(2)}) collective-permute-start(bf16[2,1024,768]{2,1,0:T(8,128)(2,1)} %get-tuple-element.97.refs_1_), channel_id=1, source_target_pairs={{0,8},{8,0},{16,24},{24,16},{1,9},{9,1},{17,25},{25,17},{2,10},{10... | collective-permute-start | bytes 9437192 | tf_op jit(solution)/shard_map/ppermute | solution.py:634
  201.8 28.9 %collective-permute-start.44 = (bf16[288,1536]{1,0:T(8,128)(2,1)}, bf16[288,1536]{1,0:T(8,128)(2,1)S(1)}, u32[]{:S(2)}, u32[]{:S(2)}) collective-permute-start(bf16[288,1536]{1,0:T(8,128)(2,1)} %collective-permute-done.43.refs_9_.refs_40_), channel_id=1, source_target_pairs={{0,8},{8,0},{16,24},{24,16},{1,9},{9,1},{17,25},{25,17},{2,10},{10... | collective-permute-start | bytes 2654216 | tf_op jit(solution)/shard_map/ppermute | solution.py:634
  218.3 34.3 %collective-permute-start.57 = (bf16[2,1024,384]{2,1,0:T(8,128)(2,1)}, bf16[2,1024,384]{2,1,0:T(8,128)(2,1)}, u32[]{:S(2)}, u32[]{:S(2)}) collective-permute-start(bf16[2,1024,384]{2,1,0:T(8,128)(2,1)} %get-tuple-element.98.refs_2_), channel_id=1, source_target_pairs={{0,8},{8,0},{16,24},{24,16},{1,9},{9,1},{17,25},{25,17},{2,10},{10... | collective-permute-start | bytes 4718600 | tf_op jit(solution)/shard_map/ppermute | solution.py:634
  235.7 52.6 %collective-permute-start.50 = (bf16[288,1536]{1,0:T(8,128)(2,1)}, bf16[288,1536]{1,0:T(8,128)(2,1)}, u32[]{:S(2)}, u32[]{:S(2)}) collective-permute-start(bf16[288,1536]{1,0:T(8,128)(2,1)} %collective-permute-done.49.refs_13_.refs_44_), channel_id=1, source_target_pairs={{0,8},{8,0},{16,24},{24,16},{1,9},{9,1},{17,25},{25,17},{2,10},{10... | collective-permute-start | bytes 2654216 | tf_op jit(solution)/shard_map/ppermute | solution.py:634
  252.1 36.3 %collective-permute-start.52 = (bf16[288,1536]{1,0:T(8,128)(2,1)}, bf16[288,1536]{1,0:T(8,128)(2,1)}, u32[]{:S(2)}, u32[]{:S(2)}) collective-permute-start(bf16[288,1536]{1,0:T(8,128)(2,1)} %collective-permute-done.51.refs_15_.refs_46_), channel_id=1, source_target_pairs={{0,8},{8,0},{16,24},{24,16},{1,9},{9,1},{17,25},{25,17},{2,10},{10... | collective-permute-start | bytes 2654216 | tf_op jit(solution)/shard_map/ppermute | solution.py:634
  252.1 36.3 %collective-permute-start.54 = (bf16[288,1536]{1,0:T(8,128)(2,1)}, bf16[288,1536]{1,0:T(8,128)(2,1)}, u32[]{:S(2)}, u32[]{:S(2)}) collective-permute-start(bf16[288,1536]{1,0:T(8,128)(2,1)} %collective-permute-done.53.refs_17_.refs_48_), channel_id=1, source_target_pairs={{0,8},{8,0},{16,24},{24,16},{1,9},{9,1},{17,25},{25,17},{2,10},{10... | collective-permute-start | bytes 2654216 | tf_op jit(solution)/shard_map/ppermute | solution.py:634
  286.3 27.5 %collective-permute-start.58 = (bf16[288,1920]{1,0:T(8,128)(2,1)}, bf16[288,1920]{1,0:T(8,128)(2,1)}, u32[]{:S(2)}, u32[]{:S(2)}) collective-permute-start(bf16[288,1920]{1,0:T(8,128)(2,1)} %get-tuple-element.154), channel_id=1, source_target_pairs={{0,2},{1,0},{2,4},{3,1},{4,6},{5,3},{6,7},{7,5},{8,9},{9,11},{10,8... | collective-permute-start | bytes 3317768 | tf_op jit(solution)/shard_map/ppermute | solution.py:628
  318.4 55.1 %collective-permute-start.77 = (bf16[288,1920]{1,0:T(8,128)(2,1)}, bf16[288,1920]{1,0:T(8,128)(2,1)}, u32[]{:S(2)}, u32[]{:S(2)}) collective-permute-start(bf16[288,1920]{1,0:T(8,128)(2,1)} %get-tuple-element.103), channel_id=1, source_target_pairs={{0,1},{1,3},{2,0},{3,5},{4,2},{5,7},{6,4},{7,6},{8,10},{9,8},{10,1... | collective-permute-start | bytes 3317768 | tf_op jit(solution)/shard_map/ppermute | solution.py:631
  319.4 55.8 %collective-permute-start.64 = (bf16[288,1920]{1,0:T(8,128)(2,1)}, bf16[288,1920]{1,0:T(8,128)(2,1)}, u32[]{:S(2)}, u32[]{:S(2)}) collective-permute-start(bf16[288,1920]{1,0:T(8,128)(2,1)} %get-tuple-element.102), channel_id=1, source_target_pairs={{0,2},{1,0},{2,4},{3,1},{4,6},{5,3},{6,7},{7,5},{8,9},{9,11},{10,8... | collective-permute-start | bytes 3317768 | tf_op jit(solution)/shard_map/ppermute | solution.py:628
  344.7 35.1 %collective-permute-start.60 = (bf16[512,1152]{1,0:T(8,128)(2,1)}, bf16[512,1152]{1,0:T(8,128)(2,1)S(1)}, u32[]{:S(2)}, u32[]{:S(2)}) collective-permute-start(bf16[512,1152]{1,0:T(8,128)(2,1)} %dynamic-slice_bitcast_fusion.2), channel_id=1, source_target_pairs={{0,16},{8,24},{16,0},{24,8},{1,17},{9,25},{17,1},{25,9},{2,18},{10... | collective-permute-start | bytes 3538952 | tf_op jit(solution)/shard_map/ppermute | solution.py:637
  372.1 38.3 %collective-permute-start.62 = (bf16[2,1024,768]{2,1,0:T(8,128)(2,1)}, bf16[2,1024,768]{2,1,0:T(8,128)(2,1)}, u32[]{:S(2)}, u32[]{:S(2)}) collective-permute-start(bf16[2,1024,768]{2,1,0:T(8,128)(2,1)} %get-tuple-element.106.refs_0_.refs_3_), channel_id=1, source_target_pairs={{0,8},{8,0},{16,24},{24,16},{1,9},{9,1},{17,25},{25,17},{2,10},{10... | collective-permute-start | bytes 9437192 | tf_op jit(solution)/shard_map/ppermute | solution.py:634
  372.7 37.7 %collective-permute-start.63 = (bf16[2,1024,768]{2,1,0:T(8,128)(2,1)}, bf16[2,1024,768]{2,1,0:T(8,128)(2,1)}, u32[]{:S(2)}, u32[]{:S(2)}) collective-permute-start(bf16[2,1024,768]{2,1,0:T(8,128)(2,1)} %get-tuple-element.107.refs_1_.refs_4_), channel_id=1, source_target_pairs={{0,8},{8,0},{16,24},{24,16},{1,9},{9,1},{17,25},{25,17},{2,10},{10... | collective-permute-start | bytes 9437192 | tf_op jit(solution)/shard_map/ppermute | solution.py:634
  380.4 27.5 %collective-permute-start.61 = (bf16[256,2304]{1,0:T(8,128)(2,1)S(1)}, bf16[256,2304]{1,0:T(8,128)(2,1)}, u32[]{:S(2)}, u32[]{:S(2)}) collective-permute-start(bf16[256,2304]{1,0:T(8,128)(2,1)S(1)} %dynamic-slice_bitcast_fusion.1), channel_id=1, source_target_pairs={{0,8},{8,0},{16,24},{24,16},{1,9},{9,1},{17,25},{25,17},{2,10},{10... | collective-permute-start | bytes 3538952 | tf_op jit(solution)/shard_map/ppermute | solution.py:634
  383.5 80.7 %collective-permute-start.78 = (bf16[288,1920]{1,0:T(8,128)(2,1)}, bf16[288,1920]{1,0:T(8,128)(2,1)}, u32[]{:S(2)}, u32[]{:S(2)}) collective-permute-start(bf16[288,1920]{1,0:T(8,128)(2,1)} %get-tuple-element.118), channel_id=1, source_target_pairs={{0,1},{1,3},{2,0},{3,5},{4,2},{5,7},{6,4},{7,6},{8,10},{9,8},{10,1... | collective-permute-start | bytes 3317768 | tf_op jit(solution)/shard_map/ppermute | solution.py:631
  407.9 56.3 %collective-permute-start.76 = (bf16[288,1920]{1,0:T(8,128)(2,1)}, bf16[288,1920]{1,0:T(8,128)(2,1)}, u32[]{:S(2)}, u32[]{:S(2)}) collective-permute-start(bf16[288,1920]{1,0:T(8,128)(2,1)} %fusion.5), channel_id=1, source_target_pairs={{0,2},{1,0},{2,4},{3,1},{4,6},{5,3},{6,7},{7,5},{8,9},{9,11},{10,8... | collective-permute-start | bytes 3317768 | tf_op jit(solution)/shard_map/ppermute | solution.py:628
  435.9 36.0 %collective-permute-start.66 = (bf16[288,1536]{1,0:T(8,128)(2,1)S(1)}, bf16[288,1536]{1,0:T(8,128)(2,1)}, u32[]{:S(2)}, u32[]{:S(2)}) collective-permute-start(bf16[288,1536]{1,0:T(8,128)(2,1)S(1)} %get-tuple-element.111), channel_id=1, source_target_pairs={{0,2},{1,0},{2,4},{3,1},{4,6},{5,3},{6,7},{7,5},{8,9},{9,11},{10,8... | collective-permute-start | bytes 2654216 | tf_op jit(solution)/shard_map/ppermute | solution.py:628
  436.4 64.8 %collective-permute-start.67 = (bf16[288,1536]{1,0:T(8,128)(2,1)}, bf16[288,1536]{1,0:T(8,128)(2,1)}, u32[]{:S(2)}, u32[]{:S(2)}) collective-permute-start(bf16[288,1536]{1,0:T(8,128)(2,1)} %get-tuple-element.112), channel_id=1, source_target_pairs={{0,1},{1,3},{2,0},{3,5},{4,2},{5,7},{6,4},{7,6},{8,10},{9,8},{10,1... | collective-permute-start | bytes 2654216 | tf_op jit(solution)/shard_map/ppermute | solution.py:631
  469.6 28.7 %collective-permute-start.79 = (f16[288,1920]{1,0:T(8,128)(2,1)S(1)}, f16[288,1920]{1,0:T(8,128)(2,1)}, u32[]{:S(2)}, u32[]{:S(2)}) collective-permute-start(f16[288,1920]{1,0:T(8,128)(2,1)S(1)} %divide_convert_fusion), channel_id=1, source_target_pairs={{0,16},{8,24},{16,0},{24,8},{1,17},{9,25},{17,1},{25,9},{2,18},{10... | collective-permute-start | bytes 3317768 | tf_op jit(solution)/shard_map/ppermute | solution.py:637
  476.3 77.3 %collective-permute-start.68 = (bf16[512,2304]{1,0:T(8,128)(2,1)}, bf16[512,2304]{1,0:T(8,128)(2,1)S(1)}, u32[]{:S(2)}, u32[]{:S(2)}) collective-permute-start(bf16[512,2304]{1,0:T(8,128)(2,1)} %grad_in.2), channel_id=1, source_target_pairs={{0,16},{8,24},{16,0},{24,8},{1,17},{9,25},{17,1},{25,9},{2,18},{10... | collective-permute-start | bytes 7077896 | tf_op jit(solution)/shard_map/ppermute | solution.py:637
  535.7 53.3 %collective-permute-start.89 = (f32[288,1920]{1,0:T(8,128)}, f32[288,1920]{1,0:T(8,128)}, u32[]{:S(2)}, u32[]{:S(2)}) collective-permute-start(f32[288,1920]{1,0:T(8,128)} %convert_multiply_fusion.refs_0_), channel_id=1, source_target_pairs={{0,8},{8,0},{16,24},{24,16},{1,9},{9,1},{17,25},{25,17},{2,10},{10... | collective-permute-start | bytes 6635528 | tf_op jit(solution)/shard_map/ppermute | solution.py:634
  535.7 53.3 %collective-permute-start.90 = (f32[288,1920]{1,0:T(8,128)}, f32[288,1920]{1,0:T(8,128)}, u32[]{:S(2)}, u32[]{:S(2)}) collective-permute-start(f32[288,1920]{1,0:T(8,128)} %convert_multiply_fusion.1.refs_1_), channel_id=1, source_target_pairs={{0,8},{8,0},{16,24},{24,16},{1,9},{9,1},{17,25},{25,17},{2,10},{10... | collective-permute-start | bytes 6635528 | tf_op jit(solution)/shard_map/ppermute | solution.py:634
  556.9 40.3 %collective-permute-start.69 = (f32[256,2304]{1,0:T(8,128)}, f32[256,2304]{1,0:T(8,128)}, u32[]{:S(2)}, u32[]{:S(2)}) collective-permute-start(f32[256,2304]{1,0:T(8,128)} %dynamic-slice_bitcast_fusion), channel_id=1, source_target_pairs={{0,8},{8,0},{16,24},{24,16},{1,9},{9,1},{17,25},{25,17},{2,10},{10... | collective-permute-start | bytes 7077896 | tf_op jit(solution)/shard_map/ppermute | solution.py:634
  (132 other events, 1641.6 us)

commit v3 on v2

--- a/solution.py
+++ b/solution.py
@@ -15,7 +15,7 @@
 
 
 def cost(flops):
-    return pl.CostEstimate(flops=int(1.6 * flops), bytes_accessed=10**6, transcendentals=0)
+    return pl.CostEstimate(flops=int(5 * flops), bytes_accessed=10**6, transcendentals=0)
 
 
 def any_spec():
@@ -58,11 +58,9 @@
     time, width = x_buf.shape
     cols = gate_buf.shape[1]
     tile = w_buf.shape[2]
-    batch = ids[at["core"]]
-
     def x_copy(i):
         start = pl.multiple_of(ids[at["time"] + i] * rows, rows)
-        return pltpu.make_async_copy(x_refs[i].at[batch], x_buf.at[pl.ds(start, rows), :], x_sem.at[i])
+        return pltpu.make_async_copy(x_refs[i], x_buf.at[pl.ds(start, rows), :], x_sem.at[i])
 
     def w_copies(col, size, slot):
         copies = []
@@ -252,8 +250,7 @@
 
 
 def gates_call(at, ids, blocks, own, pieces, offset, bias, keep, cot, group):
-    rows = blocks[0].shape[1]
-    width = blocks[0].shape[2]
+    rows, width = blocks[0].shape
     half = own.shape[1]
     cols = 3 * group
     time = keep.shape[0]
@@ -388,16 +385,14 @@
 
 
 def turn_kernel(at, n_blocks, half, ids, *refs):
-    x_refs, out_ref = refs[:n_blocks], refs[n_blocks]
-    x_buf, t_buf, sem = refs[n_blocks + 1 :]
+    x_refs, out_ref = refs[: 2 * n_blocks], refs[2 * n_blocks]
+    x_buf, t_buf, sem = refs[2 * n_blocks + 1 :]
     rows = x_buf.shape[1]
     core = ids[at["core"]]
-    jobs = [(i, m) for i in range(n_blocks) for m in range(2)]
+    jobs = [(i, m) for m in range(2) for i in range(n_blocks)]
 
     def load(n):
-        i, m = jobs[n]
-        batch = core if m == 0 else 1 - core
-        return pltpu.make_async_copy(x_refs[i].at[batch], x_buf.at[n % 2], sem.at[n % 2])
+        return pltpu.make_async_copy(x_refs[n], x_buf.at[n % 2], sem.at[n % 2])
 
     load(0).start()
     for n, (i, m) in enumerate(jobs):
@@ -412,9 +407,9 @@
 
 
 def turn_call(at, ids, blocks, per_tap, half, time):
-    _, rows, width = blocks[0].shape
+    rows, width = blocks[0].shape
     return pl.pallas_call(
-        functools.partial(turn_kernel, at, len(blocks), half),
+        functools.partial(turn_kernel, at, len(blocks) // 2, half),
         out_shape=jax.ShapeDtypeStruct((2, per_tap, half, time), BF),
         in_specs=[smem_spec()] + [any_spec()] * len(blocks),
         out_specs=vmem_spec(),
@@ -429,11 +424,11 @@
     )(ids, *blocks)
 
 
-def weight_kernel(count, x_ref, *refs):
-    mine_refs, other_refs, out_ref = refs[:count], refs[count : 2 * count], refs[2 * count]
-    x_buf, dg_buf, out_buf, x_sem, in_sem, out_sem = refs[2 * count + 1 :]
+def weight_kernel(count, offset, x_ref, *refs):
+    mine_refs, other_refs, out_ref = refs[:count], refs[count : 2 * count], refs[-7]
+    x_buf, dg_buf, out_buf, x_sem, in_sem, out_sem = refs[-6:]
     pieces, half, time = x_ref.shape[1:]
-    jobs, col = [], 0
+    jobs, col = [], offset
     for u in range(count):
         for tap in range(2):
             jobs.append((u, tap, col))
@@ -492,14 +487,16 @@
         out_copy(n).wait()
 
 
-def weight_call(x_t, mine, other):
+def weight_call(x_t, mine, other, out, offset, width):
     _, pieces, half, time = x_t.shape
     cols = sum(d.shape[2] for d in mine)
+    extra = [] if out is None else [out]
     most = max(d.shape[2] for d in mine)
     return pl.pallas_call(
-        functools.partial(weight_kernel, len(mine)),
-        out_shape=jax.ShapeDtypeStruct((2, pieces, half, cols), F32),
-        in_specs=[any_spec()] * (1 + 2 * len(mine)),
+        functools.partial(weight_kernel, len(mine), offset),
+        out_shape=jax.ShapeDtypeStruct((2, pieces, half, width), F32),
+        in_specs=[any_spec()] * (1 + 2 * len(mine) + len(extra)),
+        input_output_aliases={1 + 2 * len(mine): 0} if extra else {},
         out_specs=any_spec(),
         scratch_shapes=[
             pltpu.VMEM(x_t.shape, BF),
@@ -512,7 +509,7 @@
         compiler_params=pltpu.CompilerParams(vmem_limit_bytes=VMEM_BYTES),
         cost_estimate=cost(8 * pieces * half * time * cols),
         name="grad_w",
-    )(x_t, *mine, *other)
+    )(x_t, *mine, *other, *extra)
 
 
 def place_kernel(at_id, count, spans, feats, width, ids, *refs):
@@ -582,8 +579,9 @@
             self.at[name] = total
             total += len(numbers)
         flat = jnp.array(np.array([sum(row.values(), []) for row in table], np.int32))
-        me = lax.axis_index("stretch") * self.n_stream + lax.axis_index("stream")
+        me = (lax.axis_index("stretch") * self.n_stream + lax.axis_index("stream")).astype(jnp.uint32)
         self.ids = lax.dynamic_index_in_dim(flat, me, 0, False)
+        self.unsigned = self.ids.astype(jnp.uint32)
         self.x, self.c, self.p = (self.number(name) for name in ("x", "core", "stream"))
 
     def numbers(self, s, p):
@@ -613,7 +611,7 @@
         }
 
     def number(self, name, i=0):
-        return self.ids[self.at[name] + i]
+        return self.unsigned[self.at[name] + i]
 
     def ring_pairs(self, forward):
         pairs = []
@@ -656,26 +654,28 @@
         self.step = 0
         self.waiting, self.crossed, self.group, self.marks = [], [], [], []
 
-    def cross(self):
+    def cross(self, *deps):
         self.crossed = []
         for piece in self.waiting:
-            self.crossed.append(self.links.to_core(piece))
+            self.crossed.append(self.links.to_core(after(piece, *deps)))
             self.group += [piece, self.crossed[-1]]
         self.waiting = []
 
-    def hop(self, *deps):
+    def hop(self, *deps, cross=True):
         links = self.links
-        deps = tuple(self.crossed) + deps
+        given, deps = deps, tuple(self.crossed) + deps
         self.step += 1
-        forth = links.long(after(self.forth, *deps))
+        forth, back, *_ = lax.optimization_barrier((self.forth, self.back) + deps)
+        forth = links.long(forth)
         arriving = [forth]
         if self.step < links.hops:
-            self.back = links.short(after(self.back, *deps))
+            self.back = links.short(back)
             arriving.append(self.back)
             self.marks = arriving
         self.forth = forth
-        self.cross()
-        self.waiting = arriving
+        if cross:
+            self.cross(*given)
+        self.waiting += arriving
 
     def hops_until(self, last, *deps):
         while self.step < last:
@@ -689,18 +689,22 @@
         self.forth = self.back = None
         self.step = 0
 
-    def part(self, shard, incoming, deps):
+    def part(self, shard, incoming):
         part = lax.dynamic_index_in_dim(self.local, shard, 0, False)
         part = part if incoming is None else part + incoming.astype(F32)
-        return after(part.astype(BF), *deps)
+        return part.astype(BF)
 
     def hop(self, *deps):
         links, t = self.links, self.step
         self.step += 1
-        sent = [self.part(links.number("forth", t), self.forth, deps)]
+        if t:
+            self.forth, self.back, *_ = lax.optimization_barrier((self.forth, self.back) + deps)
+        else:
+            self.local = after(self.local, *deps)
+        sent = [self.part(links.number("forth", t), self.forth)]
         self.forth = links.long(sent[0])
         if t < links.hops - 1:
-            sent.append(self.part(links.number("back", t), self.back, deps))
+            sent.append(self.part(links.number("back", t), self.back))
             self.back = links.short(sent[1])
         return sent
 
@@ -734,8 +738,8 @@
     sizes = [count * LANES for count in counts]
     starts = [sum(sizes[:u]) for u in range(5)]
     reals = [min(size, feats - start) for start, size in zip(starts, sizes)]
-    members = [[0], [1, 2], [3, 4]]
-    place_in_group = [(0, 0), (1, 0), (1, 3 * sizes[1]), (2, 0), (2, 3 * sizes[3])]
+    members = [[0, 1], [2, 3, 4]]
+    place_in_group = [(0, 0), (0, 3 * sizes[0])] + [(1, 3 * (starts[u] - starts[2])) for u in (2, 3, 4)]
     grad_members = [[0, 1, 2], [3, 4]]
 
     def columns(a, u):
@@ -751,8 +755,9 @@
             options.append(jnp.concatenate(parts, axis=-1))
         return links.by_x(options)
 
-    def halves(g):
-        parts = [columns(weight, u) for u in members[g]]
+    def halves(g, *deps):
+        late = after(weight, *deps)
+        parts = [columns(late, u) for u in members[g]]
         return jnp.concatenate(parts, axis=1).reshape(2, half, -1)
 
     def mine_of(own, *deps):
@@ -760,23 +765,30 @@
 
     tokens = inputs.reshape(batches, rows, width)
     cots = cotangent.reshape(batches, rows, width)
-    mid = batches // 2
-
-    own_weights = [halves(0)]
+
+    tok_mine = lax.dynamic_index_in_dim(tokens, c, 0, False)
+    tok_away = lax.dynamic_index_in_dim(tokens, 1 - c, 0, False)
+    x_mine = [links.to_x(tok_mine, k) for k in others_x]
+    tok_pair = links.to_core(tok_away)
+    x_pair = [links.to_x(tok_pair, k) for k in others_x]
+    own_weights = [halves(0, tok_mine)]
     first = Gather(links, mine_of(own_weights[0]))
     first.hop()
-    core_tokens = links.to_core(tokens)
-    x_first = [links.to_x(tokens[:mid], k) for k in others_x]
     cot_mine = lax.dynamic_index_in_dim(cots, c, 0, False)
     cot_other = links.to_core(lax.dynamic_index_in_dim(cots, 1 - c, 0, False))
     reset_mine = reset.reshape(batches, rows).astype(F32)
     reset_pair = jnp.stack(links.by_core(reset_mine, links.to_core(reset_mine)), axis=1)
-    own_weights += [halves(1), halves(2)]
-    first.hop(core_tokens, cot_other, reset_pair)
-    first.hops_until(hops - 1)
-    first.hop(*x_first)
+    first.hop()
+    first.hops_until(hops - 2)
+    first.hop(*x_mine, *x_pair)
+    own_weights += [halves(1, *first.waiting)]
+    blocks = [tok_mine] + x_mine + [tok_pair] + x_pair
+
+    blocks_away = [tok_away] + [links.to_core(a) for a in x_pair]
+    blocks_away += [links.to_core(tok_mine)] + [links.to_core(a) for a in x_mine]
+
+    first.hop()
     second = Gather(links, mine_of(own_weights[1], *first.marks))
-    x_second = [links.to_x(after(tokens[mid:], *x_first), k) for k in others_x]
 
     cot_pair = jnp.concatenate(links.by_core(cot_mine, cot_other), axis=0)
 
@@ -795,29 +807,22 @@
         return jnp.concatenate(links.in_x_order(by_k), axis=0), by_k[1:]
 
     cot_units, cot_marks = [None] * 5, [None] * 5
-    cot_units[0], cot_marks[0] = cot_unit(0, *x_first)
-    reset_parts = [reset_pair] + [links.to_x(after(reset_pair, *x_first), k) for k in others_x]
+    cot_units[0], cot_marks[0] = cot_unit(0)
+    reset_parts = [reset_pair] + [after(links.to_x(reset_pair, k), *x_pair) for k in others_x]
     keep = jnp.stack(links.in_x_order(reset_parts), axis=1)
     keep = 1.0 - lax.dynamic_index_in_dim(keep, c, 0, False).reshape(time, 1)
     second.hop()
     first.cross()
-    core_first = [links.to_core(a) for a in x_first]
-    second.hop(*first.crossed, *core_first)
-    second.hops_until(hops - 1, *x_second, *cot_marks[0], *reset_parts[1:])
-    core_second = [links.to_core(a) for a in x_second]
-    from_x = [jnp.concatenate(pair, axis=0) for pair in zip(x_first, x_second)]
-    from_both = [jnp.concatenate(pair, axis=0) for pair in zip(core_first, core_second)]
-    blocks = [tokens] + from_x + [core_tokens] + from_both
     for u in range(1, 5):
-        cot_units[u], cot_marks[u] = cot_unit(u, *x_second)
-
+        cot_units[u], cot_marks[u] = cot_unit(u, *x_pair)
+
+    bias_units = [columns(bias[None, :], u) for u in range(5)]
     hiddens, dgs, others, biases = [], [], [], []
 
     def gates(u, gather, *deps):
         g, offset = place_in_group[u]
-        bias_u = after(columns(bias[None, :], u), *deps)
         hid, dg, db = gates_call(
-            at, ids, blocks, own_weights[g], gather.group, offset, bias_u, keep, cot_units[u], sizes[u]
+            at, ids, blocks, after(own_weights[g], *deps), gather.group, offset, bias_units[u], keep, cot_units[u], sizes[u]
         )
         hiddens.append(hid[:, : reals[u]])
         dgs.append(dg)
@@ -825,79 +830,83 @@
         biases.append(jnp.sum(db, axis=0).reshape(3, sizes[u])[:, : reals[u]])
         return db
 
-    def local_gradient(units):
-        local = weight_call(x_t, [dgs[u] for u in units], [others[u] for u in units])
-        return local.reshape(links.n_stream, half, -1)
+    def local_gradient(units, out, offset, total, *deps):
+        mine = [dgs[u] for u in units]
+        mine[0] = after(mine[0], *deps)
+        return weight_call(x_t, mine, [others[u] for u in units], out, offset, 3 * total)
 
     done = gates(0, first)
+    arrived = second.waiting
+    second.hop(done, *sum(cot_marks[1:], []), cross=False)
+    done = gates(1, first)
+    second.hops_until(hops - 2)
     second.hop(done)
-    third = Gather(links, mine_of(own_weights[2], done, *second.marks))
-    third.hop(*cot_marks[1], *cot_marks[2])
+
+    blocks_away[0] = after(blocks_away[0], done)
+
+    if half % 16 == 0 and rows % LANES == 0:
+        x_t = turn_call(at, ids, blocks + blocks_away, per_tap, half, time)
+    else:
+        x_t = []
+        for group in (blocks, blocks_away):
+            whole = jnp.zeros((time, width), BF)
+            for i, block in enumerate(group):
+                whole = lax.dynamic_update_slice(whole, block, (links.ids[at["time"] + i] * rows, 0))
+            turned = whole.T.reshape(per_tap, 2, half, time)
+            x_t.append(lax.dynamic_index_in_dim(turned, c, 1, False))
+        x_t = jnp.stack(x_t)
+
+    total = sum(sizes[:3])
+    second.hop(x_t)
     second.cross()
-
-    if half % 16 == 0 and rows % LANES == 0:
-        x_t = turn_call(at, ids, blocks, per_tap, half, time)
-    else:
-        whole = jnp.zeros((batches, time, width), BF)
-        for i, block in enumerate(blocks):
-            whole = lax.dynamic_update_slice(whole, block, (0, links.number("time", i) * rows, 0))
-        x_t = whole.transpose(0, 2, 1).reshape(batches, per_tap, 2, half, time)
-        x_t = lax.dynamic_index_in_dim(x_t, c, 2, False)
-        x_t = jnp.stack(links.by_core(x_t[0], x_t[1]))
-
-    third.hop(x_t, *second.crossed)
-    done = gates(1, second)
-    third.hops_until(hops - 1, done, *cot_marks[3], *cot_marks[4])
-    done = gates(2, second)
-    third.hop(done)
-    third.cross()
-
-    red_first = Reduce(links, local_gradient(grad_members[0]))
+    gates(2, second)
+    done = gates(3, second)
+
+    local = local_gradient([0, 1], None, 0, total, done)
+    local = local_gradient([2], local, 3 * (sizes[0] + sizes[1]), total)
+    red_first = Reduce(links, local.reshape(links.n_stream, half, -1))
     sent = red_first.hop()
-    done = gates(3, third, *sent)
-    sent = red_first.hop(done)
-    done = gates(4, third, *sent)
-    sent = red_first.hops_until(hops - 1, done)
+    done = gates(4, second, *sent)
+    sent = red_first.hops_until(hops - 2, done)
 
     hid = jnp.concatenate(hiddens, axis=1).reshape(n_x, own_rows, feats)
+    pieces = [[own] + gather.group for own, gather in zip(own_weights, (first, second))]
+
+    def d_inputs(k, dtype, *deps):
+        now = [after(dgs[0], *deps)] + dgs[1:]
+        return inputs_call(at, ids, k, now, pieces, place_in_group, own_rows, width, dtype)
+
+    total = sum(sizes[3:])
+    local = local_gradient([3], None, 0, total, *sent)
+    local = local_gradient([4], local, 3 * sizes[3], total).reshape(links.n_stream, half, -1)
+    red_last = Reduce(links, local)
+    hid = after(hid, local)
     hid_by_k = [lax.dynamic_index_in_dim(hid, x, 0, False)]
     for k in others_x:
         hid_by_k.append(links.to_x(lax.dynamic_index_in_dim(hid, links.number("far", k), 0, False), k))
     hid = jnp.concatenate(links.in_x_order(hid_by_k), axis=1).reshape(2, rows, width)
     hid_mine = lax.dynamic_index_in_dim(hid, c, 0, False)
-    hid_other = links.to_core(lax.dynamic_index_in_dim(hid, 1 - c, 0, False))
-    hidden = jnp.stack(links.by_core(hid_mine, hid_other)).reshape(inputs.shape)
-
-    pieces = [[own] + gather.group for own, gather in zip(own_weights, (first, second, third))]
-
-    def d_inputs(k, dtype, *deps):
-        now = [after(dgs[0], *deps)] + dgs[1:]
-        return inputs_call(at, ids, k, now, pieces, place_in_group, own_rows, width, dtype)
-
-    red_last = Reduce(links, local_gradient(grad_members[1]))
-    sent = red_first.hop(red_last.local[0, 0, :1], *hid_by_k[1:])
-    sent = red_last.hop(*sent)
+    hid_away = lax.dynamic_index_in_dim(hid, 1 - c, 0, False)
+
+    sent = red_first.hop(local) + red_last.hop(local)
     d_others = [d_inputs(k, BF, *sent) for k in others_x]
     d_received = [links.to_x(a, k) for a, k in zip(d_others, others_x)]
-
-    bias_part = jnp.concatenate(biases, axis=1)
-    bit = 1
-    while bit < links.n_stream:
-        swaps = [(i, i ^ bit) for i in range(links.n_stream)]
-        bias_part = bias_part + lax.ppermute(bias_part, "stream", swaps)
-        bit *= 2
-    bias_part = bias_part + links.to_core(bias_part)
-    bias_parts = [bias_part] + [links.to_x(bias_part, k) for k in others_x]
-    grad_bias = jnp.stack(links.in_x_order(bias_parts), axis=1).reshape(gate_cols)
+    hid_other = links.to_core(after(hid_away, *d_others))
+    hidden = jnp.stack(links.by_core(hid_mine, hid_other)).reshape(inputs.shape)
+    sent = red_first.hop(*d_others, *hid_by_k[1:]) + red_last.hop(*d_others)
+    d_mine = d_inputs(0, F32, *sent)
 
     aligned = feats % LANES == 0
     parts = [[None] * n_x for _ in sizes]
 
-    def spread(total):
+    def code(total):
         scale = jnp.maximum(jnp.max(jnp.abs(total), axis=0, keepdims=True), 1e-30) * 2.0**-15
         coded, scale = lax.optimization_barrier(((total / scale).astype(jnp.float16), scale))
-        scale = jnp.broadcast_to(scale, (8, scale.shape[1]))
-        got = [(coded, scale)] + [(links.to_x(coded, k), links.to_x(scale, k)) for k in others_x]
+        return coded, jnp.broadcast_to(scale, (8, scale.shape[1]))
+
+    def spread(coded, scale, *deps):
+        got = [(coded, scale)]
+        got += [(after(links.to_x(coded, k), *deps), after(links.to_x(scale, k), *deps)) for k in others_x]
         values = [a.astype(F32) * b[:1] for a, b in got]
         return values, [links.to_core(a) for a in values]
 
@@ -915,19 +924,33 @@
             col += 3 * sizes[u]
         return None
 
-    got, crossed = spread(red_first.total(*d_others))
-    sent = red_last.hop(*d_others)
-    d_mine = d_inputs(0, F32, *sent)
-    red_last.hops_until(hops - 1, d_mine, grad_bias, hidden, *got[1:])
+    red_last.hops_until(hops - 2, d_mine)
+    coded = code(red_first.total(d_mine))
+    sent = red_last.hops_until(hops - 1, *d_received)
+    got, crossed = spread(*coded, red_last.forth, red_last.back)
     red_last.hop()
+
     grad_weight = put(None, grad_members[0], got, crossed)
-    got, crossed = spread(red_last.total(*d_received))
     for a in d_received:
         d_mine = d_mine + a.astype(F32)
     d_mine = d_mine.reshape(2, rows, width)
     d_keep = lax.dynamic_index_in_dim(d_mine, c, 0, False)
     d_other = links.to_core(lax.dynamic_index_in_dim(d_mine, 1 - c, 0, False))
     grad_inputs = jnp.stack(links.by_core(d_keep, d_other)).reshape(inputs.shape)
+    red_last.forth, grad_inputs, hidden = lax.optimization_barrier((red_last.forth, grad_inputs, hidden))
+    coded = code(red_last.total())
+
+    bias_part = after(jnp.concatenate(biases, axis=1), *coded)
+    bias_part = bias_part + links.to_core(bias_part)
+    bit = 1
+    while bit < links.n_stream:
+        swaps = [(i, i ^ bit) for i in range(links.n_stream)]
+        bias_part = bias_part + lax.ppermute(bias_part, "stream", swaps)
+        bit *= 2
+    bias_parts = [bias_part] + [links.to_x(bias_part, k) for k in others_x]
+    grad_bias = jnp.stack(links.in_x_order(bias_parts), axis=1).reshape(gate_cols)
+
+    got, crossed = spread(*coded, grad_bias, *([grad_weight] if aligned else []))
     grad_weight = put(grad_weight, grad_members[1], got, crossed)
     if not aligned:
         grad_weight = jnp.concatenate(

time: 619 us -> 576 us (0.931)
  between operations: 24.4 us -> 3.97 us
  waiting for transfers between devices: 163 us -> 148 us
  starting transfers between devices: 69.7 us -> 55.3 us
  Pallas kernels: 234 us -> 245 us
  local copies, waits for them, and re-layouts: 48.4 us -> 40.6 us
    pallas_call x3 -> x5, Pallas kernels: 62.6 us -> 73.3 us  [the longest x4 63.4 us: weight_call(): pl.pallas_call(functools.partial(weight_kernel, len(mine), offset), out_s...]
    convert_element_type x8 -> x9, other arithmetic: 25.7 us -> 33.8 us  [the longest x6 26.5 us: part(): return part.astype(BF)]
    ppermute x20 -> x16, starting transfers between devices: 18.1 us -> 10.5 us  [long(): return lax.ppermute(a, ('stretch', 'stream'), self.pairs[0])]
    ppermute x15, waiting for transfers between devices: 48.1 us -> 40.9 us  [to_x(): lax.ppermute(a, 'stretch', [(i, i ^ 2 * k) for i in range(self.n_stretch)])]
    ppermute x15 -> x12, waiting for transfers between devices: 16.3 us -> 9.7 us  [short(): return lax.ppermute(a, ('stretch', 'stream'), self.pairs[1])]
    unnamed x157 -> x113, local copies, waits for them, and re-layouts: 14.6 us -> 9.76 us
    ppermute x20 -> x16, waiting for transfers between devices: 90.3 us -> 86.1 us  [long(): return lax.ppermute(a, ('stretch', 'stream'), self.pairs[0])]
    ppermute x15 -> x12, starting transfers between devices: 22 us -> 19.5 us  [short(): return lax.ppermute(a, ('stretch', 'stream'), self.pairs[1])]
  transfers between devices with their start and end apart: 91 -> 78, of which waited for: 20 -> 23; matrix products, arithmetic and copies ran while one was open for 17% -> 17% of each run, Pallas kernels for 37% -> 42%
where the time goes in v3:
time: 576 us; the launch traced here: 567 us
  Pallas kernels  245 us (43%)
  waiting for transfers between devices  148 us (26%)
  other arithmetic  73.2 us (13%)
  starting transfers between devices  55.3 us (10%)
  local copies, waits for them, and re-layouts  40.6 us (7%)
    pallas_call x5, Pallas kernels, gates_call(): pl.pallas_call(kernel, out_shape=(jax.ShapeDtypeStruct((time, group), BF)...  104 us
    ppermute x16, waiting for transfers between devices, long(): return lax.ppermute(a, ('stretch', 'stream'), self.pairs[0])  86.1 us
    pallas_call x4, Pallas kernels, weight_call(): pl.pallas_call(functools.partial(weight_kernel, len(mine), offset), out_s...  63.4 us
    pallas_call x2, Pallas kernels, inputs_call(): pl.pallas_call(functools.partial(inputs_kernel, at, k, half, n_pieces, ch...  53.2 us
    ppermute x15, waiting for transfers between devices, to_x(): lax.ppermute(a, 'stretch', [(i, i ^ 2 * k) for i in range(self.n_stretch)])  40.9 us
    convert_element_type x6, other arithmetic, part(): return part.astype(BF)  26.5 us
    ppermute x12, starting transfers between devices, short(): return lax.ppermute(a, ('stretch', 'stream'), self.pairs[1])  19.5 us
    pallas_call x2, Pallas kernels, place_call(): pl.pallas_call(functools.partial(place_kernel, at, len(parts), spans, fea...  14.9 us
  transfers between devices with their start and end apart: 78, of which 23 were waited for; matrix products, arithmetic and copies ran while one was open for 17% of the time, Pallas kernels for 42%

profile of v3, /device:TPU:0, one launch (start us, length us, event | category | flops | bytes accessed | tf_op | source)
XLA Modules:
  0.0 566.6 jit_solution(14945769978280718164)
XLA Ops:
  20.5 18.0 %collective-permute-done.3.refs_5_.refs_6_ = bf16[288,1536]{1,0:T(8,128)(2,1)S(1)} collective-permute-done((bf16[288,1536]{1,0:T(8,128)(2,1)}, bf16[288,1536]{1,0:T(8,128)(2,1)S(1)}, u32[]{:S(2)}, u32[]{:S(2)}) %collective-permute-start.3) | collective-permute-done | bytes 884768 | tf_op jit(solution)/shard_map/ppermute | solution.py:626
  46.7 16.7 %collective-permute-done.7.refs_9_.refs_10_ = bf16[288,1536]{1,0:T(8,128)(2,1)} collective-permute-done((bf16[288,1536]{1,0:T(8,128)(2,1)}, bf16[288,1536]{1,0:T(8,128)(2,1)}, u32[]{:S(2)}, u32[]{:S(2)}) %collective-permute-start.7) | collective-permute-done | bytes 884768 | tf_op jit(solution)/shard_map/ppermute | solution.py:626
  63.4 8.9 %collective-permute-done.2.refs_3_ = bf16[256,2304]{1,0:T(8,128)(2,1)S(1)} collective-permute-done((bf16[256,2304]{1,0:T(8,128)(2,1)}, bf16[256,2304]{1,0:T(8,128)(2,1)S(1)}, u32[]{:S(2)}, u32[]{:S(2)}) %collective-permute-start.2) | collective-permute-done | bytes 1179680 | tf_op jit(solution)/shard_map/ppermute | solution.py:635
  84.7 10.8 %collective-permute-done.11.refs_13_.refs_14_ = bf16[288,1536]{1,0:T(8,128)(2,1)} collective-permute-done((bf16[288,1536]{1,0:T(8,128)(2,1)}, bf16[288,1536]{1,0:T(8,128)(2,1)}, u32[]{:S(2)}, u32[]{:S(2)}) %collective-permute-start.11) | collective-permute-done | bytes 884768 | tf_op jit(solution)/shard_map/ppermute | solution.py:626
  101.4 7.3 %collective-permute-done.15.refs_17_.refs_18_ = bf16[288,1536]{1,0:T(8,128)(2,1)S(1)} collective-permute-done((bf16[288,1536]{1,0:T(8,128)(2,1)}, bf16[288,1536]{1,0:T(8,128)(2,1)S(1)}, u32[]{:S(2)}, u32[]{:S(2)}) %collective-permute-start.15) | collective-permute-done | bytes 884768 | tf_op jit(solution)/shard_map/ppermute | solution.py:626
  114.3 22.1 %gates.6 = (bf16[1024,256]{1,0:T(8,128)(2,1)}, bf16[2,1024,768]{2,1,0:T(8,128)(2,1)}, f32[8,768]{1,0:T(8,128)}) custom-call(s32[39]{0:T(128)} %get-tuple-element.289.ids, bf16[256,2304]{1,0:T(8,128)(2,1)} %copy-done.6, bf16[256,2304]{1,0:T(8,128)(2,1)} %collective-permute-done.refs_1_, bf16[256,2304]{1,0:T(8,128)(2,1)} %collective-permute-done.1.refs_2_, ...), custom_call_target="tpu_custom_call" | custom-call | flops 54358179840 | bytes 1000000 | tf_op jit(solution)/shard_map/gates/pallas_call | solution.py:259
  141.5 22.0 %gates.5 = (bf16[1024,256]{1,0:T(8,128)(2,1)}, bf16[2,1024,768]{2,1,0:T(8,128)(2,1)}, f32[8,768]{1,0:T(8,128)}) custom-call(s32[39]{0:T(128)} %get-tuple-element.289.ids, bf16[256,2304]{1,0:T(8,128)(2,1)} %copy-done.6, bf16[256,2304]{1,0:T(8,128)(2,1)} %collective-permute-done.refs_1_, bf16[256,2304]{1,0:T(8,128)(2,1)} %collective-permute-done.1.refs_2_, ...), custom_call_target="tpu_custom_call" | custom-call | flops 54358179840 | bytes 1000000 | tf_op jit(solution)/shard_map/gates/pallas_call | solution.py:259
  172.3 9.8 %turn.1.x_ref = bf16[2,4,288,1024]{3,2,1,0:T(8,128)(2,1)} custom-call(s32[39]{0:T(128)} %get-tuple-element.289.ids, bf16[256,2304]{1,0:T(8,128)(2,1)} %copy-done.6, bf16[256,2304]{1,0:T(8,128)(2,1)} %collective-permute-done.refs_1_, bf16[256,2304]{1,0:T(8,128)(2,1)} %collective-permute-done.1.refs_2_, bf16[256,2304]{1,0:T(8,128)(2,1)} %copy-done.42, ...), custom_call_target="tpu_custom_call" | custom-call | flops 35000000512 | bytes 1000000 | tf_op jit(solution)/shard_map/turn/pallas_call | solution.py:411
  182.1 11.7 %collective-permute-done.36.refs_13_.refs_29_ = bf16[288,1920]{1,0:T(8,128)(2,1)} collective-permute-done((bf16[288,1920]{1,0:T(8,128)(2,1)}, bf16[288,1920]{1,0:T(8,128)(2,1)}, u32[]{:S(2)}, u32[]{:S(2)}) %collective-permute-start.36) | collective-permute-done | bytes 1105952 | tf_op jit(solution)/shard_map/ppermute | solution.py:626
  199.4 11.0 %collective-permute-done.40.refs_17_.refs_33_ = bf16[288,1920]{1,0:T(8,128)(2,1)} collective-permute-done((bf16[288,1920]{1,0:T(8,128)(2,1)}, bf16[288,1920]{1,0:T(8,128)(2,1)}, u32[]{:S(2)}, u32[]{:S(2)}) %collective-permute-start.40) | collective-permute-done | bytes 1105952 | tf_op jit(solution)/shard_map/ppermute | solution.py:626
  215.4 15.9 %gates.7 = (bf16[1024,128]{1,0:T(8,128)(2,1)}, bf16[2,1024,384]{2,1,0:T(8,128)(2,1)}, f32[8,384]{1,0:T(8,128)}) custom-call(s32[39]{0:T(128)} %get-tuple-element.289.ids, bf16[256,2304]{1,0:T(8,128)(2,1)} %copy-done.6, bf16[256,2304]{1,0:T(8,128)(2,1)} %collective-permute-done.refs_1_, bf16[256,2304]{1,0:T(8,128)(2,1)} %collective-permute-done.1.refs_2_, ...), custom_call_target="tpu_custom_call" | custom-call | flops 27179089920 | bytes 1000000 | tf_op jit(solution)/shard_map/gates/pallas_call | solution.py:259
  231.8 21.9 %gates.8 = (bf16[1024,256]{1,0:T(8,128)(2,1)}, bf16[2,1024,768]{2,1,0:T(8,128)(2,1)}, f32[8,768]{1,0:T(8,128)}) custom-call(s32[39]{0:T(128)} %get-tuple-element.289.ids, bf16[256,2304]{1,0:T(8,128)(2,1)} %copy-done.6, bf16[256,2304]{1,0:T(8,128)(2,1)} %collective-permute-done.refs_1_, bf16[256,2304]{1,0:T(8,128)(2,1)} %collective-permute-done.1.refs_2_, ...), custom_call_target="tpu_custom_call" | custom-call | flops 54358179840 | bytes 1000000 | tf_op jit(solution)/shard_map/gates/pallas_call | solution.py:259
  253.9 22.6 %grad_w.4.refs_2_ = f32[2,4,288,1920]{3,2,1,0:T(8,128)} custom-call(bf16[2,4,288,1024]{3,2,1,0:T(8,128)(2,1)} %turn.1.x_ref, bf16[2,1024,768]{2,1,0:T(8,128)(2,1)} %get-tuple-element.144.refs_0_, bf16[2,1024,768]{2,1,0:T(8,128)(2,1)} %get-tuple-element.120.refs_1_, bf16[2,1024,768]{2,1,0:T(8,128)(2,1)} %collective-permute-done.43.refs_2_, ...), custom_call_target="tpu_custom_call" | custom-call | flops 72477573120 | bytes 1000000 | tf_op jit(solution)/shard_map/grad_w/pallas_call | solution.py:495
  280.4 12.8 %grad_w.5 = f32[2,4,288,1920]{3,2,1,0:T(8,128)} custom-call(bf16[2,4,288,1024]{3,2,1,0:T(8,128)(2,1)} %turn.1.x_ref, bf16[2,1024,384]{2,1,0:T(8,128)(2,1)} %get-tuple-element.116.refs_0_.refs_2_, bf16[2,1024,384]{2,1,0:T(8,128)(2,1)} %copy-done.41, f32[2,4,288,1920]{3,2,1,0:T(8,128)} %grad_w.4.refs_2_), custom_call_target="tpu_custom_call", output_to_operand_aliasing={{}: (3, {})} | custom-call | flops 18119393280 | bytes 1000000 | tf_op jit(solution)/shard_map/grad_w/pallas_call | solution.py:495
  293.2 3.8 fusion.17
  299.1 22.2 %gates.9 = (bf16[1024,256]{1,0:T(8,128)(2,1)}, bf16[2,1024,768]{2,1,0:T(8,128)(2,1)}, f32[8,768]{1,0:T(8,128)}) custom-call(s32[39]{0:T(128)} %get-tuple-element.289.ids, bf16[256,2304]{1,0:T(8,128)(2,1)} %copy-done.6, bf16[256,2304]{1,0:T(8,128)(2,1)} %collective-permute-done.refs_1_, bf16[256,2304]{1,0:T(8,128)(2,1)} %collective-permute-done.1.refs_2_, ...), custom_call_target="tpu_custom_call" | custom-call | flops 54358179840 | bytes 1000000 | tf_op jit(solution)/shard_map/gates/pallas_call | solution.py:259
  324.8 5.2 fusion.6
  332.0 14.0 %grad_w.6.refs_2_ = f32[2,4,288,1536]{3,2,1,0:T(8,128)} custom-call(bf16[2,4,288,1024]{3,2,1,0:T(8,128)(2,1)} %turn.1.x_ref, bf16[2,1024,768]{2,1,0:T(8,128)(2,1)} %get-tuple-element.127.refs_0_.refs_3_, bf16[2,1024,768]{2,1,0:T(8,128)(2,1)} %collective-permute-done.48.refs_1_), custom_call_target="tpu_custom_call" | custom-call | flops 36238786560 | bytes 1000000 | tf_op jit(solution)/shard_map/grad_w/pallas_call | solution.py:495
  346.1 14.0 %grad_w.7 = f32[2,4,288,1536]{3,2,1,0:T(8,128)} custom-call(bf16[2,4,288,1024]{3,2,1,0:T(8,128)(2,1)} %turn.1.x_ref, bf16[2,1024,768]{2,1,0:T(8,128)(2,1)} %get-tuple-element.122.refs_0_.refs_4_, bf16[2,1024,768]{2,1,0:T(8,128)(2,1)} %collective-permute-done.45.refs_1_, f32[2,4,288,1536]{3,2,1,0:T(8,128)} %grad_w.6.refs_2_), custom_call_target="tpu_custom_call", output_to_operand_aliasing={{}: (3, {})} | custom-call | flops 36238786560 | bytes 1000000 | tf_op jit(solution)/shard_map/grad_w/pallas_call | solution.py:495
  360.1 5.2 fusion.4
  367.4 4.8 fusion.19
  377.7 26.1 %grad_in.2 = bf16[512,2304]{1,0:T(8,128)(2,1)} custom-call(s32[39]{0:T(128)} %get-tuple-element.289.ids, bf16[2,1024,768]{2,1,0:T(8,128)(2,1)} %get-tuple-element.144.refs_0_, bf16[2,1024,768]{2,1,0:T(8,128)(2,1)} %get-tuple-element.120.refs_1_, bf16[2,1024,384]{2,1,0:T(8,128)(2,1)} %get-tuple-element.116.refs_0_.refs_2_, ...), custom_call_target="tpu_custom_call" | custom-call | flops 81537269760 | bytes 1000000 | tf_op jit(solution)/shard_map/grad_in/pallas_call | solution.py:369
  403.8 7.3 %collective-permute-done.50 = bf16[288,1536]{1,0:T(8,128)(2,1)} collective-permute-done((bf16[288,1536]{1,0:T(8,128)(2,1)}, bf16[288,1536]{1,0:T(8,128)(2,1)}, u32[]{:S(2)}, u32[]{:S(2)}) %collective-permute-start.50) | collective-permute-done | bytes 884768 | tf_op jit(solution)/shard_map/ppermute | solution.py:629
  412.8 5.6 fusion.10
  420.4 3.9 fusion.3
  428.0 27.1 %grad_in.3 = f32[512,2304]{1,0:T(8,128)} custom-call(s32[39]{0:T(128)} %get-tuple-element.289.ids, bf16[2,1024,768]{2,1,0:T(8,128)(2,1)} %get-tuple-element.144.refs_0_, bf16[2,1024,768]{2,1,0:T(8,128)(2,1)} %get-tuple-element.120.refs_1_, bf16[2,1024,384]{2,1,0:T(8,128)(2,1)} %get-tuple-element.116.refs_0_.refs_2_, ...), custom_call_target="tpu_custom_call" | custom-call | flops 81537269760 | bytes 1000000 | tf_op jit(solution)/shard_map/grad_in/pallas_call | solution.py:369
  465.2 4.2 fusion.9
  478.9 10.7 %collective-permute-done.72 = f32[8,1920]{1,0:T(8,128)S(1)} collective-permute-done((f32[8,1920]{1,0:T(8,128)S(1)}, f32[8,1920]{1,0:T(8,128)S(1)}, u32[]{:S(2)}, u32[]{:S(2)}) %collective-permute-start.72) | collective-permute-done | bytes 61472 | tf_op jit(solution)/shard_map/ppermute | solution.py:635
  501.2 6.0 %collective-permute-done.58 = bf16[288,1536]{1,0:T(8,128)(2,1)S(1)} collective-permute-done((bf16[288,1536]{1,0:T(8,128)(2,1)S(1)}, bf16[288,1536]{1,0:T(8,128)(2,1)S(1)}, u32[]{:S(2)}, u32[]{:S(2)}) %collective-permute-start.58) | collective-permute-done | bytes 884768 | tf_op jit(solution)/shard_map/ppermute | solution.py:626
  526.7 17.4 %collective-permute-done.69 = f32[3,1152]{1,0:T(4,128)S(1)} collective-permute-done((f32[3,1152]{1,0:T(4,128)S(1)}, f32[3,1152]{1,0:T(4,128)S(1)}, u32[]{:S(2)}, u32[]{:S(2)}) %collective-permute-start.69) | collective-permute-done | bytes 13856 | tf_op jit(solution)/shard_map/ppermute | solution.py:635
  546.2 8.3 %place.2.refs_4_ = f32[576,6912]{1,0:T(8,128)} custom-call(s32[39]{0:T(128)} %get-tuple-element.289.ids, f32[288,1920]{1,0:T(8,128)} %convert_multiply_fusion.1.refs_0_, f32[288,1920]{1,0:T(8,128)} %convert_multiply_fusion.refs_1_, f32[288,1920]{1,0:T(8,128)} %collective-permute-done.73.refs_2_, f32[288,1920]{1,0:T(8,128)} %collective-permute-done.74.refs_3_), custom_call_target="tpu_custom_call" | custom-call | flops 24999999488 | bytes 1000000 | tf_op jit(solution)/shard_map/place/pallas_call | solution.py:546
  559.6 6.7 %place.3 = f32[576,6912]{1,0:T(8,128)} custom-call(s32[39]{0:T(128)} %get-tuple-element.289.ids, f32[288,1536]{1,0:T(8,128)} %copy-done.4, f32[288,1536]{1,0:T(8,128)} %copy-done.5, f32[288,1536]{1,0:T(8,128)} %collective-permute-done.76.refs_2_, f32[288,1536]{1,0:T(8,128)} %collective-permute-done.77.refs_3_, ...), custom_call_target="tpu_custom_call", output_to_operand_aliasing={{}: (5, {})} | custom-call | flops 24999999488 | bytes 1000000 | tf_op jit(solution)/shard_map/place/pallas_call | solution.py:546
  (347 shorter events, 158.7 us)
Async XLA Ops:
  5.7 37.1 %collective-permute-start.19 = (bf16[256,2304]{1,0:T(8,128)(2,1)}, bf16[256,2304]{1,0:T(8,128)(2,1)}, u32[]{:S(2)}, u32[]{:S(2)}) collective-permute-start(bf16[256,2304]{1,0:T(8,128)(2,1)} %dynamic-slice_bitcast_fusion.3), channel_id=1, source_target_pairs={{0,8},{8,0},{16,24},{24,16},{1,9},{9,1},{17,25},{25,17},{2,10},{10... | collective-permute-start | bytes 3538952 | tf_op jit(solution)/shard_map/ppermute | solution.py:632
  7.9 34.8 %collective-permute-start.1 = (bf16[256,2304]{1,0:T(8,128)(2,1)}, bf16[256,2304]{1,0:T(8,128)(2,1)}, u32[]{:S(2)}, u32[]{:S(2)}) collective-permute-start(bf16[256,2304]{1,0:T(8,128)(2,1)} %get-tuple-element.96.refs_4_), channel_id=1, source_target_pairs={{0,8},{8,0},{16,24},{24,16},{1,9},{9,1},{17,25},{25,17},{2,10},{10... | collective-permute-start | bytes 3538952 | tf_op jit(solution)/shard_map/ppermute | solution.py:632
  8.0 35.3 %collective-permute-start = (bf16[256,2304]{1,0:T(8,128)(2,1)S(1)}, bf16[256,2304]{1,0:T(8,128)(2,1)}, u32[]{:S(2)}, u32[]{:S(2)}) collective-permute-start(bf16[256,2304]{1,0:T(8,128)(2,1)S(1)} %get-tuple-element.245.refs_0_), channel_id=1, source_target_pairs={{0,16},{8,24},{16,0},{24,8},{1,17},{9,25},{17,1},{25,9},{2,18},{10... | collective-permute-start | bytes 3538952 | tf_op jit(solution)/shard_map/ppermute | solution.py:635
  41.2 31.1 %collective-permute-start.9 = (bf16[288,1536]{1,0:T(8,128)(2,1)}, bf16[288,1536]{1,0:T(8,128)(2,1)}, u32[]{:S(2)}, u32[]{:S(2)}) collective-permute-start(bf16[288,1536]{1,0:T(8,128)(2,1)} %collective-permute-done.5.refs_7_.refs_8_), channel_id=1, source_target_pairs={{0,1},{1,3},{2,0},{3,5},{4,2},{5,7},{6,4},{7,6},{8,10},{9,8},{10,1... | collective-permute-start | bytes 2654216 | tf_op jit(solution)/shard_map/ppermute | solution.py:629
  42.7 30.1 %collective-permute-start.4 = (bf16[288,1536]{1,0:T(8,128)(2,1)}, bf16[288,1536]{1,0:T(8,128)(2,1)S(1)}, u32[]{:S(2)}, u32[]{:S(2)}) collective-permute-start(bf16[288,1536]{1,0:T(8,128)(2,1)} %copy-done.44), channel_id=1, source_target_pairs={{0,8},{8,0},{16,24},{24,16},{1,9},{9,1},{17,25},{25,17},{2,10},{10... | collective-permute-start | bytes 2654216 | tf_op jit(solution)/shard_map/ppermute | solution.py:632
  42.8 30.1 %collective-permute-start.6 = (bf16[288,1536]{1,0:T(8,128)(2,1)}, bf16[288,1536]{1,0:T(8,128)(2,1)S(1)}, u32[]{:S(2)}, u32[]{:S(2)}) collective-permute-start(bf16[288,1536]{1,0:T(8,128)(2,1)} %collective-permute-done.5.refs_7_.refs_8_), channel_id=1, source_target_pairs={{0,8},{8,0},{16,24},{24,16},{1,9},{9,1},{17,25},{25,17},{2,10},{10... | collective-permute-start | bytes 2654216 | tf_op jit(solution)/shard_map/ppermute | solution.py:632
  43.3 29.0 %collective-permute-start.2 = (bf16[256,2304]{1,0:T(8,128)(2,1)}, bf16[256,2304]{1,0:T(8,128)(2,1)S(1)}, u32[]{:S(2)}, u32[]{:S(2)}) collective-permute-start(bf16[256,2304]{1,0:T(8,128)(2,1)} %collective-permute-done.1.refs_2_), channel_id=1, source_target_pairs={{0,16},{8,24},{16,0},{24,8},{1,17},{9,25},{17,1},{25,9},{2,18},{10... | collective-permute-start | bytes 3538952 | tf_op jit(solution)/shard_map/ppermute | solution.py:635
  82.6 53.7 %collective-permute-start.29 = (bf16[512,128]{1,0:T(8,128)(2,1)S(1)}, bf16[512,128]{1,0:T(8,128)(2,1)S(1)}, u32[]{:S(2)}, u32[]{:S(2)}) collective-permute-start(bf16[512,128]{1,0:T(8,128)(2,1)S(1)} %get-tuple-element.104), channel_id=1, source_target_pairs={{0,16},{8,24},{16,0},{24,8},{1,17},{9,25},{17,1},{25,9},{2,18},{10... | collective-permute-start | bytes 393224 | tf_op jit(solution)/shard_map/ppermute | solution.py:635
  84.4 52.3 %collective-permute-start.30 = (bf16[512,256]{1,0:T(8,128)(2,1)S(1)}, bf16[512,256]{1,0:T(8,128)(2,1)S(1)}, u32[]{:S(2)}, u32[]{:S(2)}) collective-permute-start(bf16[512,256]{1,0:T(8,128)(2,1)S(1)} %get-tuple-element.105), channel_id=1, source_target_pairs={{0,16},{8,24},{16,0},{24,8},{1,17},{9,25},{17,1},{25,9},{2,18},{10... | collective-permute-start | bytes 786440 | tf_op jit(solution)/shard_map/ppermute | solution.py:635
  136.4 30.5 %collective-permute-start.22 = (bf16[256,2304]{1,0:T(8,128)(2,1)S(1)}, bf16[256,2304]{1,0:T(8,128)(2,1)}, u32[]{:S(2)}, u32[]{:S(2)}) collective-permute-start(bf16[256,2304]{1,0:T(8,128)(2,1)S(1)} %copy-done.7), channel_id=1, source_target_pairs={{0,8},{8,0},{16,24},{24,16},{1,9},{9,1},{17,25},{25,17},{2,10},{10... | collective-permute-start | bytes 3538952 | tf_op jit(solution)/shard_map/ppermute | solution.py:632
  136.6 30.2 %collective-permute-start.23 = (bf16[256,2304]{1,0:T(8,128)(2,1)}, bf16[256,2304]{1,0:T(8,128)(2,1)}, u32[]{:S(2)}, u32[]{:S(2)}) collective-permute-start(bf16[256,2304]{1,0:T(8,128)(2,1)} %collective-permute-done.refs_1_), channel_id=1, source_target_pairs={{0,8},{8,0},{16,24},{24,16},{1,9},{9,1},{17,25},{25,17},{2,10},{10... | collective-permute-start | bytes 3538952 | tf_op jit(solution)/shard_map/ppermute | solution.py:632
  137.0 30.4 %collective-permute-start.21 = (bf16[256,2304]{1,0:T(8,128)(2,1)}, bf16[256,2304]{1,0:T(8,128)(2,1)}, u32[]{:S(2)}, u32[]{:S(2)}) collective-permute-start(bf16[256,2304]{1,0:T(8,128)(2,1)} %copy-done.42), channel_id=1, source_target_pairs={{0,8},{8,0},{16,24},{24,16},{1,9},{9,1},{17,25},{25,17},{2,10},{10... | collective-permute-start | bytes 3538952 | tf_op jit(solution)/shard_map/ppermute | solution.py:632
  213.0 40.8 %collective-permute-start.43 = (bf16[2,1024,768]{2,1,0:T(8,128)(2,1)}, bf16[2,1024,768]{2,1,0:T(8,128)(2,1)}, u32[]{:S(2)}, u32[]{:S(2)}) collective-permute-start(bf16[2,1024,768]{2,1,0:T(8,128)(2,1)} %get-tuple-element.144.refs_0_), channel_id=1, source_target_pairs={{0,8},{8,0},{16,24},{24,16},{1,9},{9,1},{17,25},{25,17},{2,10},{10... | collective-permute-start | bytes 9437192 | tf_op jit(solution)/shard_map/ppermute | solution.py:632
  213.6 40.2 %collective-permute-start.44 = (bf16[2,1024,768]{2,1,0:T(8,128)(2,1)}, bf16[2,1024,768]{2,1,0:T(8,128)(2,1)}, u32[]{:S(2)}, u32[]{:S(2)}) collective-permute-start(bf16[2,1024,768]{2,1,0:T(8,128)(2,1)} %get-tuple-element.120.refs_1_), channel_id=1, source_target_pairs={{0,8},{8,0},{16,24},{24,16},{1,9},{9,1},{17,25},{25,17},{2,10},{10... | collective-permute-start | bytes 9437192 | tf_op jit(solution)/shard_map/ppermute | solution.py:632
  231.3 48.0 %collective-permute-start.42 = (bf16[2,1024,384]{2,1,0:T(8,128)(2,1)}, bf16[2,1024,384]{2,1,0:T(8,128)(2,1)S(1)}, u32[]{:S(2)}, u32[]{:S(2)}) collective-permute-start(bf16[2,1024,384]{2,1,0:T(8,128)(2,1)} %get-tuple-element.116.refs_0_.refs_2_), channel_id=1, source_target_pairs={{0,8},{8,0},{16,24},{24,16},{1,9},{9,1},{17,25},{25,17},{2,10},{10... | collective-permute-start | bytes 4718600 | tf_op jit(solution)/shard_map/ppermute | solution.py:632
  253.7 78.3 %collective-permute-start.48 = (bf16[2,1024,768]{2,1,0:T(8,128)(2,1)}, bf16[2,1024,768]{2,1,0:T(8,128)(2,1)}, u32[]{:S(2)}, u32[]{:S(2)}) collective-permute-start(bf16[2,1024,768]{2,1,0:T(8,128)(2,1)} %get-tuple-element.127.refs_0_.refs_3_), channel_id=1, source_target_pairs={{0,8},{8,0},{16,24},{24,16},{1,9},{9,1},{17,25},{25,17},{2,10},{10... | collective-permute-start | bytes 9437192 | tf_op jit(solution)/shard_map/ppermute | solution.py:632
  330.0 30.1 %collective-permute-start.52 = (bf16[288,1920]{1,0:T(8,128)(2,1)}, bf16[288,1920]{1,0:T(8,128)(2,1)S(1)}, u32[]{:S(2)}, u32[]{:S(2)}) collective-permute-start(bf16[288,1920]{1,0:T(8,128)(2,1)} %get-tuple-element.187), channel_id=1, source_target_pairs={{0,1},{1,3},{2,0},{3,5},{4,2},{5,7},{6,4},{7,6},{8,10},{9,8},{10,1... | collective-permute-start | bytes 3317768 | tf_op jit(solution)/shard_map/ppermute | solution.py:629
  365.3 54.5 %collective-permute-start.60 = (bf16[288,1920]{1,0:T(8,128)(2,1)}, bf16[288,1920]{1,0:T(8,128)(2,1)S(1)}, u32[]{:S(2)}, u32[]{:S(2)}) collective-permute-start(bf16[288,1920]{1,0:T(8,128)(2,1)} %get-tuple-element.185), channel_id=1, source_target_pairs={{0,1},{1,3},{2,0},{3,5},{4,2},{5,7},{6,4},{7,6},{8,10},{9,8},{10,1... | collective-permute-start | bytes 3317768 | tf_op jit(solution)/shard_map/ppermute | solution.py:629
  367.2 53.2 %collective-permute-start.59 = (bf16[288,1920]{1,0:T(8,128)(2,1)}, bf16[288,1920]{1,0:T(8,128)(2,1)}, u32[]{:S(2)}, u32[]{:S(2)}) collective-permute-start(bf16[288,1920]{1,0:T(8,128)(2,1)} %get-tuple-element.186), channel_id=1, source_target_pairs={{0,2},{1,0},{2,4},{3,1},{4,6},{5,3},{6,7},{7,5},{8,9},{9,11},{10,8... | collective-permute-start | bytes 3317768 | tf_op jit(solution)/shard_map/ppermute | solution.py:626
  372.1 39.0 %collective-permute-start.50 = (bf16[288,1536]{1,0:T(8,128)(2,1)}, bf16[288,1536]{1,0:T(8,128)(2,1)}, u32[]{:S(2)}, u32[]{:S(2)}) collective-permute-start(bf16[288,1536]{1,0:T(8,128)(2,1)} %get-tuple-element.195), channel_id=1, source_target_pairs={{0,1},{1,3},{2,0},{3,5},{4,2},{5,7},{6,4},{7,6},{8,10},{9,8},{10,1... | collective-permute-start | bytes 2654216 | tf_op jit(solution)/shard_map/ppermute | solution.py:629
  374.0 38.8 %collective-permute-start.49 = (bf16[288,1536]{1,0:T(8,128)(2,1)}, bf16[288,1536]{1,0:T(8,128)(2,1)}, u32[]{:S(2)}, u32[]{:S(2)}) collective-permute-start(bf16[288,1536]{1,0:T(8,128)(2,1)} %get-tuple-element.196), channel_id=1, source_target_pairs={{0,2},{1,0},{2,4},{3,1},{4,6},{5,3},{6,7},{7,5},{8,9},{9,11},{10,8... | collective-permute-start | bytes 2654216 | tf_op jit(solution)/shard_map/ppermute | solution.py:626
  376.1 44.3 %collective-permute-start.61 = (bf16[512,1152]{1,0:T(8,128)(2,1)S(1)}, bf16[512,1152]{1,0:T(8,128)(2,1)S(1)}, u32[]{:S(2)}, u32[]{:S(2)}) collective-permute-start(bf16[512,1152]{1,0:T(8,128)(2,1)S(1)} %dynamic-slice_bitcast_fusion.2), channel_id=1, source_target_pairs={{0,16},{8,24},{16,0},{24,8},{1,17},{9,25},{17,1},{25,9},{2,18},{10... | collective-permute-start | bytes 3538952 | tf_op jit(solution)/shard_map/ppermute | solution.py:635
  411.1 54.1 %collective-permute-start.55 = (bf16[512,2304]{1,0:T(8,128)(2,1)}, bf16[512,2304]{1,0:T(8,128)(2,1)}, u32[]{:S(2)}, u32[]{:S(2)}) collective-permute-start(bf16[512,2304]{1,0:T(8,128)(2,1)} %grad_in.2), channel_id=1, source_target_pairs={{0,16},{8,24},{16,0},{24,8},{1,17},{9,25},{17,1},{25,9},{2,18},{10... | collective-permute-start | bytes 7077896 | tf_op jit(solution)/shard_map/ppermute | solution.py:635
  418.4 45.5 %collective-permute-start.54 = (bf16[288,1536]{1,0:T(8,128)(2,1)}, bf16[288,1536]{1,0:T(8,128)(2,1)}, u32[]{:S(2)}, u32[]{:S(2)}) collective-permute-start(bf16[288,1536]{1,0:T(8,128)(2,1)} %get-tuple-element.193), channel_id=1, source_target_pairs={{0,1},{1,3},{2,0},{3,5},{4,2},{5,7},{6,4},{7,6},{8,10},{9,8},{10,1... | collective-permute-start | bytes 2654216 | tf_op jit(solution)/shard_map/ppermute | solution.py:629
  419.8 45.4 %collective-permute-start.53 = (bf16[288,1536]{1,0:T(8,128)(2,1)}, bf16[288,1536]{1,0:T(8,128)(2,1)}, u32[]{:S(2)}, u32[]{:S(2)}) collective-permute-start(bf16[288,1536]{1,0:T(8,128)(2,1)} %get-tuple-element.194), channel_id=1, source_target_pairs={{0,2},{1,0},{2,4},{3,1},{4,6},{5,3},{6,7},{7,5},{8,9},{9,11},{10,8... | collective-permute-start | bytes 2654216 | tf_op jit(solution)/shard_map/ppermute | solution.py:626
  424.3 30.8 %collective-permute-start.70 = (bf16[288,1920]{1,0:T(8,128)(2,1)}, bf16[288,1920]{1,0:T(8,128)(2,1)}, u32[]{:S(2)}, u32[]{:S(2)}) collective-permute-start(bf16[288,1920]{1,0:T(8,128)(2,1)} %fusion.3), channel_id=1, source_target_pairs={{0,2},{1,0},{2,4},{3,1},{4,6},{5,3},{6,7},{7,5},{8,9},{9,11},{10,8... | collective-permute-start | bytes 3317768 | tf_op jit(solution)/shard_map/ppermute | solution.py:626
  428.0 47.2 %collective-permute-start.63 = (bf16[256,2304]{1,0:T(8,128)(2,1)}, bf16[256,2304]{1,0:T(8,128)(2,1)}, u32[]{:S(2)}, u32[]{:S(2)}) collective-permute-start(bf16[256,2304]{1,0:T(8,128)(2,1)} %dynamic-slice_bitcast_fusion.1), channel_id=1, source_target_pairs={{0,8},{8,0},{16,24},{24,16},{1,9},{9,1},{17,25},{25,17},{2,10},{10... | collective-permute-start | bytes 3538952 | tf_op jit(solution)/shard_map/ppermute | solution.py:632
  461.5 33.4 %collective-permute-start.71 = (f16[288,1920]{1,0:T(8,128)(2,1)S(1)}, f16[288,1920]{1,0:T(8,128)(2,1)}, u32[]{:S(2)}, u32[]{:S(2)}) collective-permute-start(f16[288,1920]{1,0:T(8,128)(2,1)S(1)} %divide_convert_fusion), channel_id=1, source_target_pairs={{0,16},{8,24},{16,0},{24,8},{1,17},{9,25},{17,1},{25,9},{2,18},{10... | collective-permute-start | bytes 3317768 | tf_op jit(solution)/shard_map/ppermute | solution.py:635
  489.7 56.5 %collective-permute-start.73 = (f32[288,1920]{1,0:T(8,128)}, f32[288,1920]{1,0:T(8,128)}, u32[]{:S(2)}, u32[]{:S(2)}) collective-permute-start(f32[288,1920]{1,0:T(8,128)} %convert_multiply_fusion.1.refs_0_), channel_id=1, source_target_pairs={{0,8},{8,0},{16,24},{24,16},{1,9},{9,1},{17,25},{25,17},{2,10},{10... | collective-permute-start | bytes 6635528 | tf_op jit(solution)/shard_map/ppermute | solution.py:632
  497.8 48.4 %collective-permute-start.74 = (f32[288,1920]{1,0:T(8,128)}, f32[288,1920]{1,0:T(8,128)}, u32[]{:S(2)}, u32[]{:S(2)}) collective-permute-start(f32[288,1920]{1,0:T(8,128)} %convert_multiply_fusion.refs_1_), channel_id=1, source_target_pairs={{0,8},{8,0},{16,24},{24,16},{1,9},{9,1},{17,25},{25,17},{2,10},{10... | collective-permute-start | bytes 6635528 | tf_op jit(solution)/shard_map/ppermute | solution.py:632
  523.0 31.4 %collective-permute-start.75 = (f32[8,1536]{1,0:T(8,128)}, f32[8,1536]{1,0:T(8,128)}, u32[]{:S(2)}, u32[]{:S(2)}) collective-permute-start(f32[8,1536]{1,0:T(8,128)} %broadcast_in_dim.12), channel_id=1, source_target_pairs={{0,16},{8,24},{16,0},{24,8},{1,17},{9,25},{17,1},{25,9},{2,18},{10... | collective-permute-start | bytes 147464 | tf_op jit(solution)/shard_map/ppermute | solution.py:635
  523.5 31.8 %collective-permute-start.64 = (f16[288,1536]{1,0:T(8,128)(2,1)S(1)}, f16[288,1536]{1,0:T(8,128)(2,1)S(1)}, u32[]{:S(2)}, u32[]{:S(2)}) collective-permute-start(f16[288,1536]{1,0:T(8,128)(2,1)S(1)} %divide_convert_fusion.1), channel_id=1, source_target_pairs={{0,16},{8,24},{16,0},{24,8},{1,17},{9,25},{17,1},{25,9},{2,18},{10... | collective-permute-start | bytes 2654216 | tf_op jit(solution)/shard_map/ppermute | solution.py:635
  (98 other events, 1788.5 us)

commit v4 on v3

--- a/solution.py
+++ b/solution.py
@@ -780,14 +780,14 @@
     reset_pair = jnp.stack(links.by_core(reset_mine, links.to_core(reset_mine)), axis=1)
     first.hop()
     first.hops_until(hops - 2)
-    first.hop(*x_mine, *x_pair)
+    first.hop(*x_mine)
     own_weights += [halves(1, *first.waiting)]
     blocks = [tok_mine] + x_mine + [tok_pair] + x_pair
 
     blocks_away = [tok_away] + [links.to_core(a) for a in x_pair]
     blocks_away += [links.to_core(tok_mine)] + [links.to_core(a) for a in x_mine]
 
-    first.hop()
+    first.hop(*x_pair)
     second = Gather(links, mine_of(own_weights[1], *first.marks))
 
     cot_pair = jnp.concatenate(links.by_core(cot_mine, cot_other), axis=0)

time: 576 us -> 571 us (level)
  waiting for transfers between devices: 148 us -> 141 us
    ppermute x16, waiting for transfers between devices: 86.1 us -> 73.8 us  [long(): return lax.ppermute(a, ('stretch', 'stream'), self.pairs[0])]
  transfers between devices with their start and end apart: 78 -> 78, of which waited for: 23 -> 23; matrix products, arithmetic and copies ran while one was open for 17% -> 18% of each run, Pallas kernels for 42% -> 43%
where the time goes in v4:
time: 571 us; the launch traced here: 561 us
  Pallas kernels  245 us (43%)
  waiting for transfers between devices  141 us (25%)
  other arithmetic  74 us (13%)
  starting transfers between devices  55.6 us (10%)
  local copies, waits for them, and re-layouts  40.3 us (7%)
    pallas_call x5, Pallas kernels, gates_call(): pl.pallas_call(kernel, out_shape=(jax.ShapeDtypeStruct((time, group), BF)...  104 us
    ppermute x16, waiting for transfers between devices, long(): return lax.ppermute(a, ('stretch', 'stream'), self.pairs[0])  73.8 us
    pallas_call x4, Pallas kernels, weight_call(): pl.pallas_call(functools.partial(weight_kernel, len(mine), offset), out_s...  63.3 us
    pallas_call x2, Pallas kernels, inputs_call(): pl.pallas_call(functools.partial(inputs_kernel, at, k, half, n_pieces, ch...  53.2 us
    ppermute x15, waiting for transfers between devices, to_x(): lax.ppermute(a, 'stretch', [(i, i ^ 2 * k) for i in range(self.n_stretch)])  42.9 us
    convert_element_type x6, other arithmetic, part(): return part.astype(BF)  26.4 us
    ppermute x12, starting transfers between devices, short(): return lax.ppermute(a, ('stretch', 'stream'), self.pairs[1])  19.3 us
    pallas_call x2, Pallas kernels, place_call(): pl.pallas_call(functools.partial(place_kernel, at, len(parts), spans, fea...  14.9 us
  transfers between devices with their start and end apart: 78, of which 23 were waited for; matrix products, arithmetic and copies ran while one was open for 18% of the time, Pallas kernels for 43%

profile of v4, /device:TPU:0, one launch (start us, length us, event | category | flops | bytes accessed | tf_op | source)
XLA Modules:
  0.0 560.8 jit_solution(14231355728189378554)
XLA Ops:
  20.7 18.1 %collective-permute-done.3.refs_5_.refs_6_ = bf16[288,1536]{1,0:T(8,128)(2,1)} collective-permute-done((bf16[288,1536]{1,0:T(8,128)(2,1)}, bf16[288,1536]{1,0:T(8,128)(2,1)}, u32[]{:S(2)}, u32[]{:S(2)}) %collective-permute-start.3) | collective-permute-done | bytes 884768 | tf_op jit(solution)/shard_map/ppermute | solution.py:626
  46.3 16.0 %collective-permute-done.7.refs_9_.refs_10_ = bf16[288,1536]{1,0:T(8,128)(2,1)} collective-permute-done((bf16[288,1536]{1,0:T(8,128)(2,1)}, bf16[288,1536]{1,0:T(8,128)(2,1)}, u32[]{:S(2)}, u32[]{:S(2)}) %collective-permute-start.7) | collective-permute-done | bytes 884768 | tf_op jit(solution)/shard_map/ppermute | solution.py:626
  65.2 11.3 %collective-permute-done.28 = bf16[512,256]{1,0:T(8,128)(2,1)S(1)} collective-permute-done((bf16[512,256]{1,0:T(8,128)(2,1)S(1)}, bf16[512,256]{1,0:T(8,128)(2,1)S(1)}, u32[]{:S(2)}, u32[]{:S(2)}) %collective-permute-start.28) | collective-permute-done | bytes 262176 | tf_op jit(solution)/shard_map/ppermute | solution.py:635
  96.7 6.4 %collective-permute-done.15.refs_17_.refs_18_ = bf16[288,1536]{1,0:T(8,128)(2,1)S(1)} collective-permute-done((bf16[288,1536]{1,0:T(8,128)(2,1)}, bf16[288,1536]{1,0:T(8,128)(2,1)S(1)}, u32[]{:S(2)}, u32[]{:S(2)}) %collective-permute-start.15) | collective-permute-done | bytes 884768 | tf_op jit(solution)/shard_map/ppermute | solution.py:626
  108.9 22.1 %gates.6 = (bf16[1024,256]{1,0:T(8,128)(2,1)}, bf16[2,1024,768]{2,1,0:T(8,128)(2,1)}, f32[8,768]{1,0:T(8,128)}) custom-call(s32[39]{0:T(128)} %get-tuple-element.293.ids, bf16[256,2304]{1,0:T(8,128)(2,1)} %copy-done.6, bf16[256,2304]{1,0:T(8,128)(2,1)} %collective-permute-done.refs_1_, bf16[256,2304]{1,0:T(8,128)(2,1)} %collective-permute-done.1.refs_2_, ...), custom_call_target="tpu_custom_call" | custom-call | flops 54358179840 | bytes 1000000 | tf_op jit(solution)/shard_map/gates/pallas_call | solution.py:259
  136.2 22.0 %gates.5 = (bf16[1024,256]{1,0:T(8,128)(2,1)}, bf16[2,1024,768]{2,1,0:T(8,128)(2,1)}, f32[8,768]{1,0:T(8,128)}) custom-call(s32[39]{0:T(128)} %get-tuple-element.293.ids, bf16[256,2304]{1,0:T(8,128)(2,1)} %copy-done.6, bf16[256,2304]{1,0:T(8,128)(2,1)} %collective-permute-done.refs_1_, bf16[256,2304]{1,0:T(8,128)(2,1)} %collective-permute-done.1.refs_2_, ...), custom_call_target="tpu_custom_call" | custom-call | flops 54358179840 | bytes 1000000 | tf_op jit(solution)/shard_map/gates/pallas_call | solution.py:259
  166.5 9.8 %turn.1.x_ref = bf16[2,4,288,1024]{3,2,1,0:T(8,128)(2,1)} custom-call(s32[39]{0:T(128)} %get-tuple-element.293.ids, bf16[256,2304]{1,0:T(8,128)(2,1)} %copy-done.6, bf16[256,2304]{1,0:T(8,128)(2,1)} %collective-permute-done.refs_1_, bf16[256,2304]{1,0:T(8,128)(2,1)} %collective-permute-done.1.refs_2_, bf16[256,2304]{1,0:T(8,128)(2,1)} %copy-done.51, ...), custom_call_target="tpu_custom_call" | custom-call | flops 35000000512 | bytes 1000000 | tf_op jit(solution)/shard_map/turn/pallas_call | solution.py:411
  176.4 11.6 %collective-permute-done.36.refs_13_.refs_29_ = bf16[288,1920]{1,0:T(8,128)(2,1)} collective-permute-done((bf16[288,1920]{1,0:T(8,128)(2,1)}, bf16[288,1920]{1,0:T(8,128)(2,1)}, u32[]{:S(2)}, u32[]{:S(2)}) %collective-permute-start.36) | collective-permute-done | bytes 1105952 | tf_op jit(solution)/shard_map/ppermute | solution.py:626
  193.5 11.1 %collective-permute-done.40.refs_17_.refs_33_ = bf16[288,1920]{1,0:T(8,128)(2,1)} collective-permute-done((bf16[288,1920]{1,0:T(8,128)(2,1)}, bf16[288,1920]{1,0:T(8,128)(2,1)}, u32[]{:S(2)}, u32[]{:S(2)}) %collective-permute-start.40) | collective-permute-done | bytes 1105952 | tf_op jit(solution)/shard_map/ppermute | solution.py:626
  209.5 15.8 %gates.7 = (bf16[1024,128]{1,0:T(8,128)(2,1)}, bf16[2,1024,384]{2,1,0:T(8,128)(2,1)}, f32[8,384]{1,0:T(8,128)}) custom-call(s32[39]{0:T(128)} %get-tuple-element.293.ids, bf16[256,2304]{1,0:T(8,128)(2,1)} %copy-done.6, bf16[256,2304]{1,0:T(8,128)(2,1)} %collective-permute-done.refs_1_, bf16[256,2304]{1,0:T(8,128)(2,1)} %collective-permute-done.1.refs_2_, ...), custom_call_target="tpu_custom_call" | custom-call | flops 27179089920 | bytes 1000000 | tf_op jit(solution)/shard_map/gates/pallas_call | solution.py:259
  225.9 22.0 %gates.8 = (bf16[1024,256]{1,0:T(8,128)(2,1)}, bf16[2,1024,768]{2,1,0:T(8,128)(2,1)}, f32[8,768]{1,0:T(8,128)}) custom-call(s32[39]{0:T(128)} %get-tuple-element.293.ids, bf16[256,2304]{1,0:T(8,128)(2,1)} %copy-done.6, bf16[256,2304]{1,0:T(8,128)(2,1)} %collective-permute-done.refs_1_, bf16[256,2304]{1,0:T(8,128)(2,1)} %collective-permute-done.1.refs_2_, ...), custom_call_target="tpu_custom_call" | custom-call | flops 54358179840 | bytes 1000000 | tf_op jit(solution)/shard_map/gates/pallas_call | solution.py:259
  248.1 22.5 %grad_w.4.refs_2_ = f32[2,4,288,1920]{3,2,1,0:T(8,128)} custom-call(bf16[2,4,288,1024]{3,2,1,0:T(8,128)(2,1)} %turn.1.x_ref, bf16[2,1024,768]{2,1,0:T(8,128)(2,1)} %get-tuple-element.148.refs_0_, bf16[2,1024,768]{2,1,0:T(8,128)(2,1)} %get-tuple-element.124.refs_1_, bf16[2,1024,768]{2,1,0:T(8,128)(2,1)} %collective-permute-done.43.refs_2_, ...), custom_call_target="tpu_custom_call" | custom-call | flops 72477573120 | bytes 1000000 | tf_op jit(solution)/shard_map/grad_w/pallas_call | solution.py:495
  274.5 12.8 %grad_w.5 = f32[2,4,288,1920]{3,2,1,0:T(8,128)} custom-call(bf16[2,4,288,1024]{3,2,1,0:T(8,128)(2,1)} %turn.1.x_ref, bf16[2,1024,384]{2,1,0:T(8,128)(2,1)} %get-tuple-element.120.refs_0_.refs_2_, bf16[2,1024,384]{2,1,0:T(8,128)(2,1)} %copy-done.50, f32[2,4,288,1920]{3,2,1,0:T(8,128)} %grad_w.4.refs_2_), custom_call_target="tpu_custom_call", output_to_operand_aliasing={{}: (3, {})} | custom-call | flops 18119393280 | bytes 1000000 | tf_op jit(solution)/shard_map/grad_w/pallas_call | solution.py:495
  287.4 3.7 fusion.17
  293.1 22.1 %gates.9 = (bf16[1024,256]{1,0:T(8,128)(2,1)}, bf16[2,1024,768]{2,1,0:T(8,128)(2,1)}, f32[8,768]{1,0:T(8,128)}) custom-call(s32[39]{0:T(128)} %get-tuple-element.293.ids, bf16[256,2304]{1,0:T(8,128)(2,1)} %copy-done.6, bf16[256,2304]{1,0:T(8,128)(2,1)} %collective-permute-done.refs_1_, bf16[256,2304]{1,0:T(8,128)(2,1)} %collective-permute-done.1.refs_2_, ...), custom_call_target="tpu_custom_call" | custom-call | flops 54358179840 | bytes 1000000 | tf_op jit(solution)/shard_map/gates/pallas_call | solution.py:259
  318.8 5.2 fusion.6
  326.0 14.0 %grad_w.6.refs_2_ = f32[2,4,288,1536]{3,2,1,0:T(8,128)} custom-call(bf16[2,4,288,1024]{3,2,1,0:T(8,128)(2,1)} %turn.1.x_ref, bf16[2,1024,768]{2,1,0:T(8,128)(2,1)} %get-tuple-element.131.refs_0_.refs_3_, bf16[2,1024,768]{2,1,0:T(8,128)(2,1)} %collective-permute-done.48.refs_1_), custom_call_target="tpu_custom_call" | custom-call | flops 36238786560 | bytes 1000000 | tf_op jit(solution)/shard_map/grad_w/pallas_call | solution.py:495
  340.0 14.0 %grad_w.7 = f32[2,4,288,1536]{3,2,1,0:T(8,128)} custom-call(bf16[2,4,288,1024]{3,2,1,0:T(8,128)(2,1)} %turn.1.x_ref, bf16[2,1024,768]{2,1,0:T(8,128)(2,1)} %get-tuple-element.126.refs_0_.refs_4_, bf16[2,1024,768]{2,1,0:T(8,128)(2,1)} %collective-permute-done.45.refs_1_, f32[2,4,288,1536]{3,2,1,0:T(8,128)} %grad_w.6.refs_2_), custom_call_target="tpu_custom_call", output_to_operand_aliasing={{}: (3, {})} | custom-call | flops 36238786560 | bytes 1000000 | tf_op jit(solution)/shard_map/grad_w/pallas_call | solution.py:495
  354.0 5.3 fusion.4
  361.4 4.6 fusion.19
  372.1 26.1 %grad_in.2 = bf16[512,2304]{1,0:T(8,128)(2,1)} custom-call(s32[39]{0:T(128)} %get-tuple-element.293.ids, bf16[2,1024,768]{2,1,0:T(8,128)(2,1)} %get-tuple-element.148.refs_0_, bf16[2,1024,768]{2,1,0:T(8,128)(2,1)} %get-tuple-element.124.refs_1_, bf16[2,1024,384]{2,1,0:T(8,128)(2,1)} %get-tuple-element.120.refs_0_.refs_2_, ...), custom_call_target="tpu_custom_call" | custom-call | flops 81537269760 | bytes 1000000 | tf_op jit(solution)/shard_map/grad_in/pallas_call | solution.py:369
  398.2 7.2 %collective-permute-done.50 = bf16[288,1536]{1,0:T(8,128)(2,1)} collective-permute-done((bf16[288,1536]{1,0:T(8,128)(2,1)}, bf16[288,1536]{1,0:T(8,128)(2,1)}, u32[]{:S(2)}, u32[]{:S(2)}) %collective-permute-start.50) | collective-permute-done | bytes 884768 | tf_op jit(solution)/shard_map/ppermute | solution.py:629
  407.1 5.5 fusion.10
  414.7 3.7 fusion.3
  422.3 27.1 %grad_in.3 = f32[512,2304]{1,0:T(8,128)} custom-call(s32[39]{0:T(128)} %get-tuple-element.293.ids, bf16[2,1024,768]{2,1,0:T(8,128)(2,1)} %get-tuple-element.148.refs_0_, bf16[2,1024,768]{2,1,0:T(8,128)(2,1)} %get-tuple-element.124.refs_1_, bf16[2,1024,384]{2,1,0:T(8,128)(2,1)} %get-tuple-element.120.refs_0_.refs_2_, ...), custom_call_target="tpu_custom_call" | custom-call | flops 81537269760 | bytes 1000000 | tf_op jit(solution)/shard_map/grad_in/pallas_call | solution.py:369
  459.4 4.3 fusion.9
  465.9 3.5 convert_add_fusion
  473.3 10.6 %collective-permute-done.72 = f32[8,1920]{1,0:T(8,128)S(1)} collective-permute-done((f32[8,1920]{1,0:T(8,128)S(1)}, f32[8,1920]{1,0:T(8,128)S(1)}, u32[]{:S(2)}, u32[]{:S(2)}) %collective-permute-start.72) | collective-permute-done | bytes 61472 | tf_op jit(solution)/shard_map/ppermute | solution.py:635
  495.8 5.6 collective-permute-done.58
  520.9 17.4 %collective-permute-done.69 = f32[3,1152]{1,0:T(4,128)S(1)} collective-permute-done((f32[3,1152]{1,0:T(4,128)S(1)}, f32[3,1152]{1,0:T(4,128)S(1)}, u32[]{:S(2)}, u32[]{:S(2)}) %collective-permute-start.69) | collective-permute-done | bytes 13856 | tf_op jit(solution)/shard_map/ppermute | solution.py:635
  540.4 8.3 %place.2.refs_4_ = f32[576,6912]{1,0:T(8,128)} custom-call(s32[39]{0:T(128)} %get-tuple-element.293.ids, f32[288,1920]{1,0:T(8,128)} %convert_multiply_fusion.1.refs_0_, f32[288,1920]{1,0:T(8,128)} %convert_multiply_fusion.refs_1_, f32[288,1920]{1,0:T(8,128)} %collective-permute-done.73.refs_2_, f32[288,1920]{1,0:T(8,128)} %collective-permute-done.74.refs_3_), custom_call_target="tpu_custom_call" | custom-call | flops 24999999488 | bytes 1000000 | tf_op jit(solution)/shard_map/place/pallas_call | solution.py:546
  553.7 6.7 %place.3 = f32[576,6912]{1,0:T(8,128)} custom-call(s32[39]{0:T(128)} %get-tuple-element.293.ids, f32[288,1536]{1,0:T(8,128)} %copy-done.4, f32[288,1536]{1,0:T(8,128)} %copy-done.5, f32[288,1536]{1,0:T(8,128)} %collective-permute-done.76.refs_2_, f32[288,1536]{1,0:T(8,128)} %collective-permute-done.77.refs_3_, ...), custom_call_target="tpu_custom_call", output_to_operand_aliasing={{}: (5, {})} | custom-call | flops 24999999488 | bytes 1000000 | tf_op jit(solution)/shard_map/place/pallas_call | solution.py:546
  (363 shorter events, 160.1 us)
Async XLA Ops:
  5.7 36.5 %collective-permute-start.19 = (bf16[256,2304]{1,0:T(8,128)(2,1)}, bf16[256,2304]{1,0:T(8,128)(2,1)}, u32[]{:S(2)}, u32[]{:S(2)}) collective-permute-start(bf16[256,2304]{1,0:T(8,128)(2,1)} %dynamic-slice_bitcast_fusion.3), channel_id=1, source_target_pairs={{0,8},{8,0},{16,24},{24,16},{1,9},{9,1},{17,25},{25,17},{2,10},{10... | collective-permute-start | bytes 3538952 | tf_op jit(solution)/shard_map/ppermute | solution.py:632
  8.0 34.2 %collective-permute-start.1 = (bf16[256,2304]{1,0:T(8,128)(2,1)}, bf16[256,2304]{1,0:T(8,128)(2,1)}, u32[]{:S(2)}, u32[]{:S(2)}) collective-permute-start(bf16[256,2304]{1,0:T(8,128)(2,1)} %get-tuple-element.100.refs_4_), channel_id=1, source_target_pairs={{0,8},{8,0},{16,24},{24,16},{1,9},{9,1},{17,25},{25,17},{2,10},{10... | collective-permute-start | bytes 3538952 | tf_op jit(solution)/shard_map/ppermute | solution.py:632
  8.0 34.7 %collective-permute-start = (bf16[256,2304]{1,0:T(8,128)(2,1)S(1)}, bf16[256,2304]{1,0:T(8,128)(2,1)}, u32[]{:S(2)}, u32[]{:S(2)}) collective-permute-start(bf16[256,2304]{1,0:T(8,128)(2,1)S(1)} %get-tuple-element.249.refs_0_), channel_id=1, source_target_pairs={{0,16},{8,24},{16,0},{24,8},{1,17},{9,25},{17,1},{25,9},{2,18},{10... | collective-permute-start | bytes 3538952 | tf_op jit(solution)/shard_map/ppermute | solution.py:635
  42.7 36.1 %collective-permute-start.2 = (bf16[256,2304]{1,0:T(8,128)(2,1)}, bf16[256,2304]{1,0:T(8,128)(2,1)S(1)}, u32[]{:S(2)}, u32[]{:S(2)}) collective-permute-start(bf16[256,2304]{1,0:T(8,128)(2,1)} %collective-permute-done.1.refs_2_), channel_id=1, source_target_pairs={{0,16},{8,24},{16,0},{24,8},{1,17},{9,25},{17,1},{25,9},{2,18},{10... | collective-permute-start | bytes 3538952 | tf_op jit(solution)/shard_map/ppermute | solution.py:635
  84.7 46.3 %collective-permute-start.29 = (bf16[512,128]{1,0:T(8,128)(2,1)S(1)}, bf16[512,128]{1,0:T(8,128)(2,1)S(1)}, u32[]{:S(2)}, u32[]{:S(2)}) collective-permute-start(bf16[512,128]{1,0:T(8,128)(2,1)S(1)} %get-tuple-element.108), channel_id=1, source_target_pairs={{0,16},{8,24},{16,0},{24,8},{1,17},{9,25},{17,1},{25,9},{2,18},{10... | collective-permute-start | bytes 393224 | tf_op jit(solution)/shard_map/ppermute | solution.py:635
  86.2 44.9 %collective-permute-start.30 = (bf16[512,256]{1,0:T(8,128)(2,1)S(1)}, bf16[512,256]{1,0:T(8,128)(2,1)S(1)}, u32[]{:S(2)}, u32[]{:S(2)}) collective-permute-start(bf16[512,256]{1,0:T(8,128)(2,1)S(1)} %get-tuple-element.109), channel_id=1, source_target_pairs={{0,16},{8,24},{16,0},{24,8},{1,17},{9,25},{17,1},{25,9},{2,18},{10... | collective-permute-start | bytes 786440 | tf_op jit(solution)/shard_map/ppermute | solution.py:635
  106.9 27.2 %collective-permute-start.24 = (bf16[288,1920]{1,0:T(8,128)(2,1)S(1)}, bf16[288,1920]{1,0:T(8,128)(2,1)}, u32[]{:S(2)}, u32[]{:S(2)}) collective-permute-start(bf16[288,1920]{1,0:T(8,128)(2,1)S(1)} %dynamic-slice_bitcast_fusion.6), channel_id=1, source_target_pairs={{0,2},{1,0},{2,4},{3,1},{4,6},{5,3},{6,7},{7,5},{8,9},{9,11},{10,8... | collective-permute-start | bytes 3317768 | tf_op jit(solution)/shard_map/ppermute | solution.py:626
  131.0 30.5 %collective-permute-start.22 = (bf16[256,2304]{1,0:T(8,128)(2,1)S(1)}, bf16[256,2304]{1,0:T(8,128)(2,1)}, u32[]{:S(2)}, u32[]{:S(2)}) collective-permute-start(bf16[256,2304]{1,0:T(8,128)(2,1)S(1)} %copy-done.7), channel_id=1, source_target_pairs={{0,8},{8,0},{16,24},{24,16},{1,9},{9,1},{17,25},{25,17},{2,10},{10... | collective-permute-start | bytes 3538952 | tf_op jit(solution)/shard_map/ppermute | solution.py:632
  131.1 30.5 %collective-permute-start.23 = (bf16[256,2304]{1,0:T(8,128)(2,1)}, bf16[256,2304]{1,0:T(8,128)(2,1)}, u32[]{:S(2)}, u32[]{:S(2)}) collective-permute-start(bf16[256,2304]{1,0:T(8,128)(2,1)} %collective-permute-done.refs_1_), channel_id=1, source_target_pairs={{0,8},{8,0},{16,24},{24,16},{1,9},{9,1},{17,25},{25,17},{2,10},{10... | collective-permute-start | bytes 3538952 | tf_op jit(solution)/shard_map/ppermute | solution.py:632
  131.6 30.5 %collective-permute-start.21 = (bf16[256,2304]{1,0:T(8,128)(2,1)}, bf16[256,2304]{1,0:T(8,128)(2,1)}, u32[]{:S(2)}, u32[]{:S(2)}) collective-permute-start(bf16[256,2304]{1,0:T(8,128)(2,1)} %copy-done.51), channel_id=1, source_target_pairs={{0,8},{8,0},{16,24},{24,16},{1,9},{9,1},{17,25},{25,17},{2,10},{10... | collective-permute-start | bytes 3538952 | tf_op jit(solution)/shard_map/ppermute | solution.py:632
  207.2 40.9 %collective-permute-start.43 = (bf16[2,1024,768]{2,1,0:T(8,128)(2,1)}, bf16[2,1024,768]{2,1,0:T(8,128)(2,1)}, u32[]{:S(2)}, u32[]{:S(2)}) collective-permute-start(bf16[2,1024,768]{2,1,0:T(8,128)(2,1)} %get-tuple-element.148.refs_0_), channel_id=1, source_target_pairs={{0,8},{8,0},{16,24},{24,16},{1,9},{9,1},{17,25},{25,17},{2,10},{10... | collective-permute-start | bytes 9437192 | tf_op jit(solution)/shard_map/ppermute | solution.py:632
  207.8 40.3 %collective-permute-start.44 = (bf16[2,1024,768]{2,1,0:T(8,128)(2,1)}, bf16[2,1024,768]{2,1,0:T(8,128)(2,1)}, u32[]{:S(2)}, u32[]{:S(2)}) collective-permute-start(bf16[2,1024,768]{2,1,0:T(8,128)(2,1)} %get-tuple-element.124.refs_1_), channel_id=1, source_target_pairs={{0,8},{8,0},{16,24},{24,16},{1,9},{9,1},{17,25},{25,17},{2,10},{10... | collective-permute-start | bytes 9437192 | tf_op jit(solution)/shard_map/ppermute | solution.py:632
  225.4 48.0 %collective-permute-start.42 = (bf16[2,1024,384]{2,1,0:T(8,128)(2,1)}, bf16[2,1024,384]{2,1,0:T(8,128)(2,1)S(1)}, u32[]{:S(2)}, u32[]{:S(2)}) collective-permute-start(bf16[2,1024,384]{2,1,0:T(8,128)(2,1)} %get-tuple-element.120.refs_0_.refs_2_), channel_id=1, source_target_pairs={{0,8},{8,0},{16,24},{24,16},{1,9},{9,1},{17,25},{25,17},{2,10},{10... | collective-permute-start | bytes 4718600 | tf_op jit(solution)/shard_map/ppermute | solution.py:632
  247.9 78.1 %collective-permute-start.48 = (bf16[2,1024,768]{2,1,0:T(8,128)(2,1)}, bf16[2,1024,768]{2,1,0:T(8,128)(2,1)}, u32[]{:S(2)}, u32[]{:S(2)}) collective-permute-start(bf16[2,1024,768]{2,1,0:T(8,128)(2,1)} %get-tuple-element.131.refs_0_.refs_3_), channel_id=1, source_target_pairs={{0,8},{8,0},{16,24},{24,16},{1,9},{9,1},{17,25},{25,17},{2,10},{10... | collective-permute-start | bytes 9437192 | tf_op jit(solution)/shard_map/ppermute | solution.py:632
  291.1 27.7 %collective-permute-start.47 = (bf16[288,1920]{1,0:T(8,128)(2,1)S(1)}, bf16[288,1920]{1,0:T(8,128)(2,1)S(1)}, u32[]{:S(2)}, u32[]{:S(2)}) collective-permute-start(bf16[288,1920]{1,0:T(8,128)(2,1)S(1)} %get-tuple-element.193), channel_id=1, source_target_pairs={{0,1},{1,3},{2,0},{3,5},{4,2},{5,7},{6,4},{7,6},{8,10},{9,8},{10,1... | collective-permute-start | bytes 3317768 | tf_op jit(solution)/shard_map/ppermute | solution.py:629
  323.9 30.1 %collective-permute-start.52 = (bf16[288,1920]{1,0:T(8,128)(2,1)}, bf16[288,1920]{1,0:T(8,128)(2,1)S(1)}, u32[]{:S(2)}, u32[]{:S(2)}) collective-permute-start(bf16[288,1920]{1,0:T(8,128)(2,1)} %get-tuple-element.191), channel_id=1, source_target_pairs={{0,1},{1,3},{2,0},{3,5},{4,2},{5,7},{6,4},{7,6},{8,10},{9,8},{10,1... | collective-permute-start | bytes 3317768 | tf_op jit(solution)/shard_map/ppermute | solution.py:629
  325.8 28.2 %collective-permute-start.51 = (bf16[288,1920]{1,0:T(8,128)(2,1)S(1)}, bf16[288,1920]{1,0:T(8,128)(2,1)S(1)}, u32[]{:S(2)}, u32[]{:S(2)}) collective-permute-start(bf16[288,1920]{1,0:T(8,128)(2,1)S(1)} %get-tuple-element.192), channel_id=1, source_target_pairs={{0,2},{1,0},{2,4},{3,1},{4,6},{5,3},{6,7},{7,5},{8,9},{9,11},{10,8... | collective-permute-start | bytes 3317768 | tf_op jit(solution)/shard_map/ppermute | solution.py:626
  359.4 54.7 %collective-permute-start.60 = (bf16[288,1920]{1,0:T(8,128)(2,1)}, bf16[288,1920]{1,0:T(8,128)(2,1)S(1)}, u32[]{:S(2)}, u32[]{:S(2)}) collective-permute-start(bf16[288,1920]{1,0:T(8,128)(2,1)} %get-tuple-element.189), channel_id=1, source_target_pairs={{0,1},{1,3},{2,0},{3,5},{4,2},{5,7},{6,4},{7,6},{8,10},{9,8},{10,1... | collective-permute-start | bytes 3317768 | tf_op jit(solution)/shard_map/ppermute | solution.py:629
  361.3 53.4 %collective-permute-start.59 = (bf16[288,1920]{1,0:T(8,128)(2,1)}, bf16[288,1920]{1,0:T(8,128)(2,1)}, u32[]{:S(2)}, u32[]{:S(2)}) collective-permute-start(bf16[288,1920]{1,0:T(8,128)(2,1)} %get-tuple-element.190), channel_id=1, source_target_pairs={{0,2},{1,0},{2,4},{3,1},{4,6},{5,3},{6,7},{7,5},{8,9},{9,11},{10,8... | collective-permute-start | bytes 3317768 | tf_op jit(solution)/shard_map/ppermute | solution.py:626
  366.0 39.4 %collective-permute-start.50 = (bf16[288,1536]{1,0:T(8,128)(2,1)}, bf16[288,1536]{1,0:T(8,128)(2,1)}, u32[]{:S(2)}, u32[]{:S(2)}) collective-permute-start(bf16[288,1536]{1,0:T(8,128)(2,1)} %get-tuple-element.199), channel_id=1, source_target_pairs={{0,1},{1,3},{2,0},{3,5},{4,2},{5,7},{6,4},{7,6},{8,10},{9,8},{10,1... | collective-permute-start | bytes 2654216 | tf_op jit(solution)/shard_map/ppermute | solution.py:629
  367.9 39.2 %collective-permute-start.49 = (bf16[288,1536]{1,0:T(8,128)(2,1)}, bf16[288,1536]{1,0:T(8,128)(2,1)}, u32[]{:S(2)}, u32[]{:S(2)}) collective-permute-start(bf16[288,1536]{1,0:T(8,128)(2,1)} %get-tuple-element.200), channel_id=1, source_target_pairs={{0,2},{1,0},{2,4},{3,1},{4,6},{5,3},{6,7},{7,5},{8,9},{9,11},{10,8... | collective-permute-start | bytes 2654216 | tf_op jit(solution)/shard_map/ppermute | solution.py:626
  370.1 44.6 %collective-permute-start.61 = (bf16[512,1152]{1,0:T(8,128)(2,1)S(1)}, bf16[512,1152]{1,0:T(8,128)(2,1)S(1)}, u32[]{:S(2)}, u32[]{:S(2)}) collective-permute-start(bf16[512,1152]{1,0:T(8,128)(2,1)S(1)} %dynamic-slice_bitcast_fusion.2), channel_id=1, source_target_pairs={{0,16},{8,24},{16,0},{24,8},{1,17},{9,25},{17,1},{25,9},{2,18},{10... | collective-permute-start | bytes 3538952 | tf_op jit(solution)/shard_map/ppermute | solution.py:635
  405.4 54.0 %collective-permute-start.55 = (bf16[512,2304]{1,0:T(8,128)(2,1)}, bf16[512,2304]{1,0:T(8,128)(2,1)}, u32[]{:S(2)}, u32[]{:S(2)}) collective-permute-start(bf16[512,2304]{1,0:T(8,128)(2,1)} %grad_in.2), channel_id=1, source_target_pairs={{0,16},{8,24},{16,0},{24,8},{1,17},{9,25},{17,1},{25,9},{2,18},{10... | collective-permute-start | bytes 7077896 | tf_op jit(solution)/shard_map/ppermute | solution.py:635
  412.6 45.3 %collective-permute-start.54 = (bf16[288,1536]{1,0:T(8,128)(2,1)}, bf16[288,1536]{1,0:T(8,128)(2,1)}, u32[]{:S(2)}, u32[]{:S(2)}) collective-permute-start(bf16[288,1536]{1,0:T(8,128)(2,1)} %get-tuple-element.197), channel_id=1, source_target_pairs={{0,1},{1,3},{2,0},{3,5},{4,2},{5,7},{6,4},{7,6},{8,10},{9,8},{10,1... | collective-permute-start | bytes 2654216 | tf_op jit(solution)/shard_map/ppermute | solution.py:629
  414.0 45.4 %collective-permute-start.53 = (bf16[288,1536]{1,0:T(8,128)(2,1)}, bf16[288,1536]{1,0:T(8,128)(2,1)}, u32[]{:S(2)}, u32[]{:S(2)}) collective-permute-start(bf16[288,1536]{1,0:T(8,128)(2,1)} %get-tuple-element.198), channel_id=1, source_target_pairs={{0,2},{1,0},{2,4},{3,1},{4,6},{5,3},{6,7},{7,5},{8,9},{9,11},{10,8... | collective-permute-start | bytes 2654216 | tf_op jit(solution)/shard_map/ppermute | solution.py:626
  418.4 30.9 %collective-permute-start.70 = (bf16[288,1920]{1,0:T(8,128)(2,1)}, bf16[288,1920]{1,0:T(8,128)(2,1)}, u32[]{:S(2)}, u32[]{:S(2)}) collective-permute-start(bf16[288,1920]{1,0:T(8,128)(2,1)} %fusion.3), channel_id=1, source_target_pairs={{0,2},{1,0},{2,4},{3,1},{4,6},{5,3},{6,7},{7,5},{8,9},{9,11},{10,8... | collective-permute-start | bytes 3317768 | tf_op jit(solution)/shard_map/ppermute | solution.py:626
  422.3 47.3 %collective-permute-start.63 = (bf16[256,2304]{1,0:T(8,128)(2,1)}, bf16[256,2304]{1,0:T(8,128)(2,1)}, u32[]{:S(2)}, u32[]{:S(2)}) collective-permute-start(bf16[256,2304]{1,0:T(8,128)(2,1)} %dynamic-slice_bitcast_fusion.1), channel_id=1, source_target_pairs={{0,8},{8,0},{16,24},{24,16},{1,9},{9,1},{17,25},{25,17},{2,10},{10... | collective-permute-start | bytes 3538952 | tf_op jit(solution)/shard_map/ppermute | solution.py:632
  455.7 33.8 %collective-permute-start.71 = (f16[288,1920]{1,0:T(8,128)(2,1)S(1)}, f16[288,1920]{1,0:T(8,128)(2,1)}, u32[]{:S(2)}, u32[]{:S(2)}) collective-permute-start(f16[288,1920]{1,0:T(8,128)(2,1)S(1)} %divide_convert_fusion), channel_id=1, source_target_pairs={{0,16},{8,24},{16,0},{24,8},{1,17},{9,25},{17,1},{25,9},{2,18},{10... | collective-permute-start | bytes 3317768 | tf_op jit(solution)/shard_map/ppermute | solution.py:635
  483.9 56.4 %collective-permute-start.73 = (f32[288,1920]{1,0:T(8,128)}, f32[288,1920]{1,0:T(8,128)}, u32[]{:S(2)}, u32[]{:S(2)}) collective-permute-start(f32[288,1920]{1,0:T(8,128)} %convert_multiply_fusion.1.refs_0_), channel_id=1, source_target_pairs={{0,8},{8,0},{16,24},{24,16},{1,9},{9,1},{17,25},{25,17},{2,10},{10... | collective-permute-start | bytes 6635528 | tf_op jit(solution)/shard_map/ppermute | solution.py:632
  492.4 48.0 %collective-permute-start.74 = (f32[288,1920]{1,0:T(8,128)}, f32[288,1920]{1,0:T(8,128)}, u32[]{:S(2)}, u32[]{:S(2)}) collective-permute-start(f32[288,1920]{1,0:T(8,128)} %convert_multiply_fusion.refs_1_), channel_id=1, source_target_pairs={{0,8},{8,0},{16,24},{24,16},{1,9},{9,1},{17,25},{25,17},{2,10},{10... | collective-permute-start | bytes 6635528 | tf_op jit(solution)/shard_map/ppermute | solution.py:632
  517.3 31.4 %collective-permute-start.75 = (f32[8,1536]{1,0:T(8,128)}, f32[8,1536]{1,0:T(8,128)}, u32[]{:S(2)}, u32[]{:S(2)}) collective-permute-start(f32[8,1536]{1,0:T(8,128)} %broadcast_in_dim.12), channel_id=1, source_target_pairs={{0,16},{8,24},{16,0},{24,8},{1,17},{9,25},{17,1},{25,9},{2,18},{10... | collective-permute-start | bytes 147464 | tf_op jit(solution)/shard_map/ppermute | solution.py:635
  517.9 31.6 %collective-permute-start.64 = (f16[288,1536]{1,0:T(8,128)(2,1)S(1)}, f16[288,1536]{1,0:T(8,128)(2,1)S(1)}, u32[]{:S(2)}, u32[]{:S(2)}) collective-permute-start(f16[288,1536]{1,0:T(8,128)(2,1)S(1)} %divide_convert_fusion.1), channel_id=1, source_target_pairs={{0,16},{8,24},{16,0},{24,8},{1,17},{9,25},{17,1},{25,9},{2,18},{10... | collective-permute-start | bytes 2654216 | tf_op jit(solution)/shard_map/ppermute | solution.py:635
  (106 other events, 1957.0 us)

commit v5 on v4

--- a/solution.py
+++ b/solution.py
@@ -941,14 +941,15 @@
     coded = code(red_last.total())
 
     bias_part = after(jnp.concatenate(biases, axis=1), *coded)
+    bias_parts = [bias_part] + [links.to_x(bias_part, k) for k in others_x]
+    bias_part = jnp.stack(links.in_x_order(bias_parts), axis=1)
     bias_part = bias_part + links.to_core(bias_part)
     bit = 1
     while bit < links.n_stream:
         swaps = [(i, i ^ bit) for i in range(links.n_stream)]
         bias_part = bias_part + lax.ppermute(bias_part, "stream", swaps)
         bit *= 2
-    bias_parts = [bias_part] + [links.to_x(bias_part, k) for k in others_x]
-    grad_bias = jnp.stack(links.in_x_order(bias_parts), axis=1).reshape(gate_cols)
+    grad_bias = bias_part.reshape(gate_cols)
 
     got, crossed = spread(*coded, grad_bias, *([grad_weight] if aligned else []))
     grad_weight = put(grad_weight, grad_members[1], got, crossed)

time: 571 us -> 568 us (level)
    ppermute x15, waiting for transfers between devices: 42.9 us -> 32.4 us  [to_x(): lax.ppermute(a, 'stretch', [(i, i ^ 2 * k) for i in range(self.n_stretch)])]
  transfers between devices with their start and end apart: 78 -> 78, of which waited for: 23 -> 24; matrix products, arithmetic and copies ran while one was open for 18% -> 18% of each run, Pallas kernels for 43% -> 43%
where the time goes in v5:
time: 568 us; the launch traced here: 558 us
  Pallas kernels  245 us (43%)
  waiting for transfers between devices  139 us (24%)
  other arithmetic  74.8 us (13%)
  starting transfers between devices  55.3 us (10%)
  local copies, waits for them, and re-layouts  38.9 us (7%)
    pallas_call x5, Pallas kernels, gates_call(): pl.pallas_call(kernel, out_shape=(jax.ShapeDtypeStruct((time, group), BF)...  104 us
    ppermute x16, waiting for transfers between devices, long(): return lax.ppermute(a, ('stretch', 'stream'), self.pairs[0])  76.8 us
    pallas_call x4, Pallas kernels, weight_call(): pl.pallas_call(functools.partial(weight_kernel, len(mine), offset), out_s...  63.2 us
    pallas_call x2, Pallas kernels, inputs_call(): pl.pallas_call(functools.partial(inputs_kernel, at, k, half, n_pieces, ch...  53.2 us
    ppermute x15, waiting for transfers between devices, to_x(): lax.ppermute(a, 'stretch', [(i, i ^ 2 * k) for i in range(self.n_stretch)])  32.4 us
    convert_element_type x6, other arithmetic, part(): return part.astype(BF)  26.4 us
    ppermute x12, starting transfers between devices, short(): return lax.ppermute(a, ('stretch', 'stream'), self.pairs[1])  19.3 us
    ppermute x12, waiting for transfers between devices, short(): return lax.ppermute(a, ('stretch', 'stream'), self.pairs[1])  17.1 us
  transfers between devices with their start and end apart: 78, of which 24 were waited for; matrix products, arithmetic and copies ran while one was open for 18% of the time, Pallas kernels for 43%

profile of v5, /device:TPU:0, one launch (start us, length us, event | category | flops | bytes accessed | tf_op | source)
XLA Modules:
  0.0 558.0 jit_solution(16911066214017731528)
XLA Ops:
  20.8 18.1 %collective-permute-done.3.refs_5_.refs_6_ = bf16[288,1536]{1,0:T(8,128)(2,1)} collective-permute-done((bf16[288,1536]{1,0:T(8,128)(2,1)}, bf16[288,1536]{1,0:T(8,128)(2,1)}, u32[]{:S(2)}, u32[]{:S(2)}) %collective-permute-start.3) | collective-permute-done | bytes 884768 | tf_op jit(solution)/shard_map/ppermute | solution.py:626
  46.5 16.0 %collective-permute-done.7.refs_9_.refs_10_ = bf16[288,1536]{1,0:T(8,128)(2,1)} collective-permute-done((bf16[288,1536]{1,0:T(8,128)(2,1)}, bf16[288,1536]{1,0:T(8,128)(2,1)}, u32[]{:S(2)}, u32[]{:S(2)}) %collective-permute-start.7) | collective-permute-done | bytes 884768 | tf_op jit(solution)/shard_map/ppermute | solution.py:626
  65.4 11.3 %collective-permute-done.28 = bf16[512,256]{1,0:T(8,128)(2,1)S(1)} collective-permute-done((bf16[512,256]{1,0:T(8,128)(2,1)S(1)}, bf16[512,256]{1,0:T(8,128)(2,1)S(1)}, u32[]{:S(2)}, u32[]{:S(2)}) %collective-permute-start.28) | collective-permute-done | bytes 262176 | tf_op jit(solution)/shard_map/ppermute | solution.py:635
  96.9 6.4 %collective-permute-done.15.refs_17_.refs_18_ = bf16[288,1536]{1,0:T(8,128)(2,1)S(1)} collective-permute-done((bf16[288,1536]{1,0:T(8,128)(2,1)}, bf16[288,1536]{1,0:T(8,128)(2,1)S(1)}, u32[]{:S(2)}, u32[]{:S(2)}) %collective-permute-start.15) | collective-permute-done | bytes 884768 | tf_op jit(solution)/shard_map/ppermute | solution.py:626
  109.1 22.1 %gates.6 = (bf16[1024,256]{1,0:T(8,128)(2,1)}, bf16[2,1024,768]{2,1,0:T(8,128)(2,1)}, f32[8,768]{1,0:T(8,128)}) custom-call(s32[39]{0:T(128)} %get-tuple-element.293.ids, bf16[256,2304]{1,0:T(8,128)(2,1)} %copy-done.6, bf16[256,2304]{1,0:T(8,128)(2,1)} %collective-permute-done.refs_1_, bf16[256,2304]{1,0:T(8,128)(2,1)} %collective-permute-done.1.refs_2_, ...), custom_call_target="tpu_custom_call" | custom-call | flops 54358179840 | bytes 1000000 | tf_op jit(solution)/shard_map/gates/pallas_call | solution.py:259
  136.3 22.0 %gates.5 = (bf16[1024,256]{1,0:T(8,128)(2,1)}, bf16[2,1024,768]{2,1,0:T(8,128)(2,1)}, f32[8,768]{1,0:T(8,128)}) custom-call(s32[39]{0:T(128)} %get-tuple-element.293.ids, bf16[256,2304]{1,0:T(8,128)(2,1)} %copy-done.6, bf16[256,2304]{1,0:T(8,128)(2,1)} %collective-permute-done.refs_1_, bf16[256,2304]{1,0:T(8,128)(2,1)} %collective-permute-done.1.refs_2_, ...), custom_call_target="tpu_custom_call" | custom-call | flops 54358179840 | bytes 1000000 | tf_op jit(solution)/shard_map/gates/pallas_call | solution.py:259
  166.7 9.8 %turn.1.x_ref = bf16[2,4,288,1024]{3,2,1,0:T(8,128)(2,1)} custom-call(s32[39]{0:T(128)} %get-tuple-element.293.ids, bf16[256,2304]{1,0:T(8,128)(2,1)} %copy-done.6, bf16[256,2304]{1,0:T(8,128)(2,1)} %collective-permute-done.refs_1_, bf16[256,2304]{1,0:T(8,128)(2,1)} %collective-permute-done.1.refs_2_, bf16[256,2304]{1,0:T(8,128)(2,1)} %copy-done.52, ...), custom_call_target="tpu_custom_call" | custom-call | flops 35000000512 | bytes 1000000 | tf_op jit(solution)/shard_map/turn/pallas_call | solution.py:411
  176.5 11.6 %collective-permute-done.36.refs_13_.refs_29_ = bf16[288,1920]{1,0:T(8,128)(2,1)} collective-permute-done((bf16[288,1920]{1,0:T(8,128)(2,1)}, bf16[288,1920]{1,0:T(8,128)(2,1)}, u32[]{:S(2)}, u32[]{:S(2)}) %collective-permute-start.36) | collective-permute-done | bytes 1105952 | tf_op jit(solution)/shard_map/ppermute | solution.py:626
  193.7 11.1 %collective-permute-done.40.refs_17_.refs_33_ = bf16[288,1920]{1,0:T(8,128)(2,1)} collective-permute-done((bf16[288,1920]{1,0:T(8,128)(2,1)}, bf16[288,1920]{1,0:T(8,128)(2,1)}, u32[]{:S(2)}, u32[]{:S(2)}) %collective-permute-start.40) | collective-permute-done | bytes 1105952 | tf_op jit(solution)/shard_map/ppermute | solution.py:626
  209.7 15.8 %gates.7 = (bf16[1024,128]{1,0:T(8,128)(2,1)}, bf16[2,1024,384]{2,1,0:T(8,128)(2,1)}, f32[8,384]{1,0:T(8,128)}) custom-call(s32[39]{0:T(128)} %get-tuple-element.293.ids, bf16[256,2304]{1,0:T(8,128)(2,1)} %copy-done.6, bf16[256,2304]{1,0:T(8,128)(2,1)} %collective-permute-done.refs_1_, bf16[256,2304]{1,0:T(8,128)(2,1)} %collective-permute-done.1.refs_2_, ...), custom_call_target="tpu_custom_call" | custom-call | flops 27179089920 | bytes 1000000 | tf_op jit(solution)/shard_map/gates/pallas_call | solution.py:259
  226.1 22.0 %gates.8 = (bf16[1024,256]{1,0:T(8,128)(2,1)}, bf16[2,1024,768]{2,1,0:T(8,128)(2,1)}, f32[8,768]{1,0:T(8,128)}) custom-call(s32[39]{0:T(128)} %get-tuple-element.293.ids, bf16[256,2304]{1,0:T(8,128)(2,1)} %copy-done.6, bf16[256,2304]{1,0:T(8,128)(2,1)} %collective-permute-done.refs_1_, bf16[256,2304]{1,0:T(8,128)(2,1)} %collective-permute-done.1.refs_2_, ...), custom_call_target="tpu_custom_call" | custom-call | flops 54358179840 | bytes 1000000 | tf_op jit(solution)/shard_map/gates/pallas_call | solution.py:259
  248.3 22.5 %grad_w.4.refs_2_ = f32[2,4,288,1920]{3,2,1,0:T(8,128)} custom-call(bf16[2,4,288,1024]{3,2,1,0:T(8,128)(2,1)} %turn.1.x_ref, bf16[2,1024,768]{2,1,0:T(8,128)(2,1)} %get-tuple-element.148.refs_0_, bf16[2,1024,768]{2,1,0:T(8,128)(2,1)} %get-tuple-element.124.refs_1_, bf16[2,1024,768]{2,1,0:T(8,128)(2,1)} %collective-permute-done.43.refs_2_, ...), custom_call_target="tpu_custom_call" | custom-call | flops 72477573120 | bytes 1000000 | tf_op jit(solution)/shard_map/grad_w/pallas_call | solution.py:495
  274.7 12.8 %grad_w.5 = f32[2,4,288,1920]{3,2,1,0:T(8,128)} custom-call(bf16[2,4,288,1024]{3,2,1,0:T(8,128)(2,1)} %turn.1.x_ref, bf16[2,1024,384]{2,1,0:T(8,128)(2,1)} %get-tuple-element.120.refs_0_.refs_2_, bf16[2,1024,384]{2,1,0:T(8,128)(2,1)} %copy-done.51, f32[2,4,288,1920]{3,2,1,0:T(8,128)} %grad_w.4.refs_2_), custom_call_target="tpu_custom_call", output_to_operand_aliasing={{}: (3, {})} | custom-call | flops 18119393280 | bytes 1000000 | tf_op jit(solution)/shard_map/grad_w/pallas_call | solution.py:495
  287.5 3.8 fusion.17
  293.3 22.1 %gates.9 = (bf16[1024,256]{1,0:T(8,128)(2,1)}, bf16[2,1024,768]{2,1,0:T(8,128)(2,1)}, f32[8,768]{1,0:T(8,128)}) custom-call(s32[39]{0:T(128)} %get-tuple-element.293.ids, bf16[256,2304]{1,0:T(8,128)(2,1)} %copy-done.6, bf16[256,2304]{1,0:T(8,128)(2,1)} %collective-permute-done.refs_1_, bf16[256,2304]{1,0:T(8,128)(2,1)} %collective-permute-done.1.refs_2_, ...), custom_call_target="tpu_custom_call" | custom-call | flops 54358179840 | bytes 1000000 | tf_op jit(solution)/shard_map/gates/pallas_call | solution.py:259
  318.9 5.2 fusion.6
  326.2 14.0 %grad_w.6.refs_2_ = f32[2,4,288,1536]{3,2,1,0:T(8,128)} custom-call(bf16[2,4,288,1024]{3,2,1,0:T(8,128)(2,1)} %turn.1.x_ref, bf16[2,1024,768]{2,1,0:T(8,128)(2,1)} %get-tuple-element.131.refs_0_.refs_3_, bf16[2,1024,768]{2,1,0:T(8,128)(2,1)} %collective-permute-done.48.refs_1_), custom_call_target="tpu_custom_call" | custom-call | flops 36238786560 | bytes 1000000 | tf_op jit(solution)/shard_map/grad_w/pallas_call | solution.py:495
  340.2 14.0 %grad_w.7 = f32[2,4,288,1536]{3,2,1,0:T(8,128)} custom-call(bf16[2,4,288,1024]{3,2,1,0:T(8,128)(2,1)} %turn.1.x_ref, bf16[2,1024,768]{2,1,0:T(8,128)(2,1)} %get-tuple-element.126.refs_0_.refs_4_, bf16[2,1024,768]{2,1,0:T(8,128)(2,1)} %collective-permute-done.45.refs_1_, f32[2,4,288,1536]{3,2,1,0:T(8,128)} %grad_w.6.refs_2_), custom_call_target="tpu_custom_call", output_to_operand_aliasing={{}: (3, {})} | custom-call | flops 36238786560 | bytes 1000000 | tf_op jit(solution)/shard_map/grad_w/pallas_call | solution.py:495
  354.2 5.3 fusion.4
  361.6 4.7 fusion.19
  372.3 26.1 %grad_in.2 = bf16[512,2304]{1,0:T(8,128)(2,1)} custom-call(s32[39]{0:T(128)} %get-tuple-element.293.ids, bf16[2,1024,768]{2,1,0:T(8,128)(2,1)} %get-tuple-element.148.refs_0_, bf16[2,1024,768]{2,1,0:T(8,128)(2,1)} %get-tuple-element.124.refs_1_, bf16[2,1024,384]{2,1,0:T(8,128)(2,1)} %get-tuple-element.120.refs_0_.refs_2_, ...), custom_call_target="tpu_custom_call" | custom-call | flops 81537269760 | bytes 1000000 | tf_op jit(solution)/shard_map/grad_in/pallas_call | solution.py:369
  398.4 7.3 %collective-permute-done.50 = bf16[288,1536]{1,0:T(8,128)(2,1)} collective-permute-done((bf16[288,1536]{1,0:T(8,128)(2,1)}, bf16[288,1536]{1,0:T(8,128)(2,1)}, u32[]{:S(2)}, u32[]{:S(2)}) %collective-permute-start.50) | collective-permute-done | bytes 884768 | tf_op jit(solution)/shard_map/ppermute | solution.py:629
  407.3 5.6 fusion.10
  414.9 3.7 fusion.3
  422.5 27.1 %grad_in.3 = f32[512,2304]{1,0:T(8,128)} custom-call(s32[39]{0:T(128)} %get-tuple-element.293.ids, bf16[2,1024,768]{2,1,0:T(8,128)(2,1)} %get-tuple-element.148.refs_0_, bf16[2,1024,768]{2,1,0:T(8,128)(2,1)} %get-tuple-element.124.refs_1_, bf16[2,1024,384]{2,1,0:T(8,128)(2,1)} %get-tuple-element.120.refs_0_.refs_2_, ...), custom_call_target="tpu_custom_call" | custom-call | flops 81537269760 | bytes 1000000 | tf_op jit(solution)/shard_map/grad_in/pallas_call | solution.py:369
  463.5 4.3 fusion.9
  473.6 10.5 %collective-permute-done.72 = f32[8,1920]{1,0:T(8,128)S(1)} collective-permute-done((f32[8,1920]{1,0:T(8,128)S(1)}, f32[8,1920]{1,0:T(8,128)S(1)}, u32[]{:S(2)}, u32[]{:S(2)}) %collective-permute-start.72) | collective-permute-done | bytes 61472 | tf_op jit(solution)/shard_map/ppermute | solution.py:635
  484.2 6.0 %collective-permute-done.57 = bf16[288,1536]{1,0:T(8,128)(2,1)S(1)} collective-permute-done((bf16[288,1536]{1,0:T(8,128)(2,1)S(1)}, bf16[288,1536]{1,0:T(8,128)(2,1)S(1)}, u32[]{:S(2)}, u32[]{:S(2)}) %collective-permute-start.57) | collective-permute-done | bytes 884768 | tf_op jit(solution)/shard_map/ppermute | solution.py:629
  496.9 8.6 %collective-permute-done.58 = bf16[288,1536]{1,0:T(8,128)(2,1)S(1)} collective-permute-done((bf16[288,1536]{1,0:T(8,128)(2,1)S(1)}, bf16[288,1536]{1,0:T(8,128)(2,1)S(1)}, u32[]{:S(2)}, u32[]{:S(2)}) %collective-permute-start.58) | collective-permute-done | bytes 884768 | tf_op jit(solution)/shard_map/ppermute | solution.py:626
  530.9 8.3 %place.2.refs_4_ = f32[576,6912]{1,0:T(8,128)} custom-call(s32[39]{0:T(128)} %get-tuple-element.293.ids, f32[288,1920]{1,0:T(8,128)} %convert_multiply_fusion.1.refs_0_, f32[288,1920]{1,0:T(8,128)} %copy-done.4, f32[288,1920]{1,0:T(8,128)} %collective-permute-done.73.refs_2_, f32[288,1920]{1,0:T(8,128)} %collective-permute-done.74.refs_3_), custom_call_target="tpu_custom_call" | custom-call | flops 24999999488 | bytes 1000000 | tf_op jit(solution)/shard_map/place/pallas_call | solution.py:546
  539.2 5.3 collective-permute-done.64
  550.9 6.7 %place.3 = f32[576,6912]{1,0:T(8,128)} custom-call(s32[39]{0:T(128)} %get-tuple-element.293.ids, f32[288,1536]{1,0:T(8,128)} %convert_multiply_fusion.3.refs_0_, f32[288,1536]{1,0:T(8,128)} %copy-done.5, f32[288,1536]{1,0:T(8,128)} %collective-permute-done.76.refs_2_, f32[288,1536]{1,0:T(8,128)} %copy-done.50, ...), custom_call_target="tpu_custom_call", output_to_operand_aliasing={{}: (5, {})} | custom-call | flops 24999999488 | bytes 1000000 | tf_op jit(solution)/shard_map/place/pallas_call | solution.py:546
  (365 shorter events, 163.6 us)
Async XLA Ops:
  5.8 36.6 %collective-permute-start.19 = (bf16[256,2304]{1,0:T(8,128)(2,1)}, bf16[256,2304]{1,0:T(8,128)(2,1)}, u32[]{:S(2)}, u32[]{:S(2)}) collective-permute-start(bf16[256,2304]{1,0:T(8,128)(2,1)} %dynamic-slice_bitcast_fusion.3), channel_id=1, source_target_pairs={{0,8},{8,0},{16,24},{24,16},{1,9},{9,1},{17,25},{25,17},{2,10},{10... | collective-permute-start | bytes 3538952 | tf_op jit(solution)/shard_map/ppermute | solution.py:632
  8.1 34.3 %collective-permute-start.1 = (bf16[256,2304]{1,0:T(8,128)(2,1)}, bf16[256,2304]{1,0:T(8,128)(2,1)}, u32[]{:S(2)}, u32[]{:S(2)}) collective-permute-start(bf16[256,2304]{1,0:T(8,128)(2,1)} %get-tuple-element.100.refs_4_), channel_id=1, source_target_pairs={{0,8},{8,0},{16,24},{24,16},{1,9},{9,1},{17,25},{25,17},{2,10},{10... | collective-permute-start | bytes 3538952 | tf_op jit(solution)/shard_map/ppermute | solution.py:632
  8.1 34.7 %collective-permute-start = (bf16[256,2304]{1,0:T(8,128)(2,1)S(1)}, bf16[256,2304]{1,0:T(8,128)(2,1)}, u32[]{:S(2)}, u32[]{:S(2)}) collective-permute-start(bf16[256,2304]{1,0:T(8,128)(2,1)S(1)} %get-tuple-element.249.refs_0_), channel_id=1, source_target_pairs={{0,16},{8,24},{16,0},{24,8},{1,17},{9,25},{17,1},{25,9},{2,18},{10... | collective-permute-start | bytes 3538952 | tf_op jit(solution)/shard_map/ppermute | solution.py:635
  42.9 36.1 %collective-permute-start.2 = (bf16[256,2304]{1,0:T(8,128)(2,1)}, bf16[256,2304]{1,0:T(8,128)(2,1)S(1)}, u32[]{:S(2)}, u32[]{:S(2)}) collective-permute-start(bf16[256,2304]{1,0:T(8,128)(2,1)} %collective-permute-done.1.refs_2_), channel_id=1, source_target_pairs={{0,16},{8,24},{16,0},{24,8},{1,17},{9,25},{17,1},{25,9},{2,18},{10... | collective-permute-start | bytes 3538952 | tf_op jit(solution)/shard_map/ppermute | solution.py:635
  84.9 46.3 %collective-permute-start.29 = (bf16[512,128]{1,0:T(8,128)(2,1)S(1)}, bf16[512,128]{1,0:T(8,128)(2,1)S(1)}, u32[]{:S(2)}, u32[]{:S(2)}) collective-permute-start(bf16[512,128]{1,0:T(8,128)(2,1)S(1)} %get-tuple-element.108), channel_id=1, source_target_pairs={{0,16},{8,24},{16,0},{24,8},{1,17},{9,25},{17,1},{25,9},{2,18},{10... | collective-permute-start | bytes 393224 | tf_op jit(solution)/shard_map/ppermute | solution.py:635
  86.4 44.9 %collective-permute-start.30 = (bf16[512,256]{1,0:T(8,128)(2,1)S(1)}, bf16[512,256]{1,0:T(8,128)(2,1)S(1)}, u32[]{:S(2)}, u32[]{:S(2)}) collective-permute-start(bf16[512,256]{1,0:T(8,128)(2,1)S(1)} %get-tuple-element.109), channel_id=1, source_target_pairs={{0,16},{8,24},{16,0},{24,8},{1,17},{9,25},{17,1},{25,9},{2,18},{10... | collective-permute-start | bytes 786440 | tf_op jit(solution)/shard_map/ppermute | solution.py:635
  107.1 27.2 %collective-permute-start.24 = (bf16[288,1920]{1,0:T(8,128)(2,1)S(1)}, bf16[288,1920]{1,0:T(8,128)(2,1)}, u32[]{:S(2)}, u32[]{:S(2)}) collective-permute-start(bf16[288,1920]{1,0:T(8,128)(2,1)S(1)} %dynamic-slice_bitcast_fusion.6), channel_id=1, source_target_pairs={{0,2},{1,0},{2,4},{3,1},{4,6},{5,3},{6,7},{7,5},{8,9},{9,11},{10,8... | collective-permute-start | bytes 3317768 | tf_op jit(solution)/shard_map/ppermute | solution.py:626
  107.7 26.6 %collective-permute-start.26 = (bf16[288,1920]{1,0:T(8,128)(2,1)S(1)}, bf16[288,1920]{1,0:T(8,128)(2,1)}, u32[]{:S(2)}, u32[]{:S(2)}) collective-permute-start(bf16[288,1920]{1,0:T(8,128)(2,1)S(1)} %dynamic-slice_bitcast_fusion.6), channel_id=1, source_target_pairs={{0,1},{1,3},{2,0},{3,5},{4,2},{5,7},{6,4},{7,6},{8,10},{9,8},{10,1... | collective-permute-start | bytes 3317768 | tf_op jit(solution)/shard_map/ppermute | solution.py:629
  131.2 30.5 %collective-permute-start.22 = (bf16[256,2304]{1,0:T(8,128)(2,1)S(1)}, bf16[256,2304]{1,0:T(8,128)(2,1)}, u32[]{:S(2)}, u32[]{:S(2)}) collective-permute-start(bf16[256,2304]{1,0:T(8,128)(2,1)S(1)} %copy-done.7), channel_id=1, source_target_pairs={{0,8},{8,0},{16,24},{24,16},{1,9},{9,1},{17,25},{25,17},{2,10},{10... | collective-permute-start | bytes 3538952 | tf_op jit(solution)/shard_map/ppermute | solution.py:632
  131.3 30.5 %collective-permute-start.23 = (bf16[256,2304]{1,0:T(8,128)(2,1)}, bf16[256,2304]{1,0:T(8,128)(2,1)}, u32[]{:S(2)}, u32[]{:S(2)}) collective-permute-start(bf16[256,2304]{1,0:T(8,128)(2,1)} %collective-permute-done.refs_1_), channel_id=1, source_target_pairs={{0,8},{8,0},{16,24},{24,16},{1,9},{9,1},{17,25},{25,17},{2,10},{10... | collective-permute-start | bytes 3538952 | tf_op jit(solution)/shard_map/ppermute | solution.py:632
  131.8 30.5 %collective-permute-start.21 = (bf16[256,2304]{1,0:T(8,128)(2,1)}, bf16[256,2304]{1,0:T(8,128)(2,1)}, u32[]{:S(2)}, u32[]{:S(2)}) collective-permute-start(bf16[256,2304]{1,0:T(8,128)(2,1)} %copy-done.52), channel_id=1, source_target_pairs={{0,8},{8,0},{16,24},{24,16},{1,9},{9,1},{17,25},{25,17},{2,10},{10... | collective-permute-start | bytes 3538952 | tf_op jit(solution)/shard_map/ppermute | solution.py:632
  134.3 26.9 %collective-permute-start.32 = (bf16[288,1920]{1,0:T(8,128)(2,1)}, bf16[288,1920]{1,0:T(8,128)(2,1)}, u32[]{:S(2)}, u32[]{:S(2)}) collective-permute-start(bf16[288,1920]{1,0:T(8,128)(2,1)} %collective-permute-done.24.refs_5_.refs_21_), channel_id=1, source_target_pairs={{0,2},{1,0},{2,4},{3,1},{4,6},{5,3},{6,7},{7,5},{8,9},{9,11},{10,8... | collective-permute-start | bytes 3317768 | tf_op jit(solution)/shard_map/ppermute | solution.py:626
  207.4 40.9 %collective-permute-start.43 = (bf16[2,1024,768]{2,1,0:T(8,128)(2,1)}, bf16[2,1024,768]{2,1,0:T(8,128)(2,1)}, u32[]{:S(2)}, u32[]{:S(2)}) collective-permute-start(bf16[2,1024,768]{2,1,0:T(8,128)(2,1)} %get-tuple-element.148.refs_0_), channel_id=1, source_target_pairs={{0,8},{8,0},{16,24},{24,16},{1,9},{9,1},{17,25},{25,17},{2,10},{10... | collective-permute-start | bytes 9437192 | tf_op jit(solution)/shard_map/ppermute | solution.py:632
  208.0 40.3 %collective-permute-start.44 = (bf16[2,1024,768]{2,1,0:T(8,128)(2,1)}, bf16[2,1024,768]{2,1,0:T(8,128)(2,1)}, u32[]{:S(2)}, u32[]{:S(2)}) collective-permute-start(bf16[2,1024,768]{2,1,0:T(8,128)(2,1)} %get-tuple-element.124.refs_1_), channel_id=1, source_target_pairs={{0,8},{8,0},{16,24},{24,16},{1,9},{9,1},{17,25},{25,17},{2,10},{10... | collective-permute-start | bytes 9437192 | tf_op jit(solution)/shard_map/ppermute | solution.py:632
  225.6 47.9 %collective-permute-start.42 = (bf16[2,1024,384]{2,1,0:T(8,128)(2,1)}, bf16[2,1024,384]{2,1,0:T(8,128)(2,1)S(1)}, u32[]{:S(2)}, u32[]{:S(2)}) collective-permute-start(bf16[2,1024,384]{2,1,0:T(8,128)(2,1)} %get-tuple-element.120.refs_0_.refs_2_), channel_id=1, source_target_pairs={{0,8},{8,0},{16,24},{24,16},{1,9},{9,1},{17,25},{25,17},{2,10},{10... | collective-permute-start | bytes 4718600 | tf_op jit(solution)/shard_map/ppermute | solution.py:632
  248.1 78.0 %collective-permute-start.48 = (bf16[2,1024,768]{2,1,0:T(8,128)(2,1)}, bf16[2,1024,768]{2,1,0:T(8,128)(2,1)}, u32[]{:S(2)}, u32[]{:S(2)}) collective-permute-start(bf16[2,1024,768]{2,1,0:T(8,128)(2,1)} %get-tuple-element.131.refs_0_.refs_3_), channel_id=1, source_target_pairs={{0,8},{8,0},{16,24},{24,16},{1,9},{9,1},{17,25},{25,17},{2,10},{10... | collective-permute-start | bytes 9437192 | tf_op jit(solution)/shard_map/ppermute | solution.py:632
  291.3 27.6 %collective-permute-start.47 = (bf16[288,1920]{1,0:T(8,128)(2,1)S(1)}, bf16[288,1920]{1,0:T(8,128)(2,1)S(1)}, u32[]{:S(2)}, u32[]{:S(2)}) collective-permute-start(bf16[288,1920]{1,0:T(8,128)(2,1)S(1)} %get-tuple-element.193), channel_id=1, source_target_pairs={{0,1},{1,3},{2,0},{3,5},{4,2},{5,7},{6,4},{7,6},{8,10},{9,8},{10,1... | collective-permute-start | bytes 3317768 | tf_op jit(solution)/shard_map/ppermute | solution.py:629
  324.1 30.1 %collective-permute-start.52 = (bf16[288,1920]{1,0:T(8,128)(2,1)}, bf16[288,1920]{1,0:T(8,128)(2,1)S(1)}, u32[]{:S(2)}, u32[]{:S(2)}) collective-permute-start(bf16[288,1920]{1,0:T(8,128)(2,1)} %get-tuple-element.191), channel_id=1, source_target_pairs={{0,1},{1,3},{2,0},{3,5},{4,2},{5,7},{6,4},{7,6},{8,10},{9,8},{10,1... | collective-permute-start | bytes 3317768 | tf_op jit(solution)/shard_map/ppermute | solution.py:629
  326.0 28.2 %collective-permute-start.51 = (bf16[288,1920]{1,0:T(8,128)(2,1)S(1)}, bf16[288,1920]{1,0:T(8,128)(2,1)S(1)}, u32[]{:S(2)}, u32[]{:S(2)}) collective-permute-start(bf16[288,1920]{1,0:T(8,128)(2,1)S(1)} %get-tuple-element.192), channel_id=1, source_target_pairs={{0,2},{1,0},{2,4},{3,1},{4,6},{5,3},{6,7},{7,5},{8,9},{9,11},{10,8... | collective-permute-start | bytes 3317768 | tf_op jit(solution)/shard_map/ppermute | solution.py:626
  359.6 54.8 %collective-permute-start.60 = (bf16[288,1920]{1,0:T(8,128)(2,1)}, bf16[288,1920]{1,0:T(8,128)(2,1)S(1)}, u32[]{:S(2)}, u32[]{:S(2)}) collective-permute-start(bf16[288,1920]{1,0:T(8,128)(2,1)} %get-tuple-element.189), channel_id=1, source_target_pairs={{0,1},{1,3},{2,0},{3,5},{4,2},{5,7},{6,4},{7,6},{8,10},{9,8},{10,1... | collective-permute-start | bytes 3317768 | tf_op jit(solution)/shard_map/ppermute | solution.py:629
  361.4 53.5 %collective-permute-start.59 = (bf16[288,1920]{1,0:T(8,128)(2,1)}, bf16[288,1920]{1,0:T(8,128)(2,1)}, u32[]{:S(2)}, u32[]{:S(2)}) collective-permute-start(bf16[288,1920]{1,0:T(8,128)(2,1)} %get-tuple-element.190), channel_id=1, source_target_pairs={{0,2},{1,0},{2,4},{3,1},{4,6},{5,3},{6,7},{7,5},{8,9},{9,11},{10,8... | collective-permute-start | bytes 3317768 | tf_op jit(solution)/shard_map/ppermute | solution.py:626
  366.3 39.4 %collective-permute-start.50 = (bf16[288,1536]{1,0:T(8,128)(2,1)}, bf16[288,1536]{1,0:T(8,128)(2,1)}, u32[]{:S(2)}, u32[]{:S(2)}) collective-permute-start(bf16[288,1536]{1,0:T(8,128)(2,1)} %get-tuple-element.199), channel_id=1, source_target_pairs={{0,1},{1,3},{2,0},{3,5},{4,2},{5,7},{6,4},{7,6},{8,10},{9,8},{10,1... | collective-permute-start | bytes 2654216 | tf_op jit(solution)/shard_map/ppermute | solution.py:629
  368.2 39.2 %collective-permute-start.49 = (bf16[288,1536]{1,0:T(8,128)(2,1)}, bf16[288,1536]{1,0:T(8,128)(2,1)}, u32[]{:S(2)}, u32[]{:S(2)}) collective-permute-start(bf16[288,1536]{1,0:T(8,128)(2,1)} %get-tuple-element.200), channel_id=1, source_target_pairs={{0,2},{1,0},{2,4},{3,1},{4,6},{5,3},{6,7},{7,5},{8,9},{9,11},{10,8... | collective-permute-start | bytes 2654216 | tf_op jit(solution)/shard_map/ppermute | solution.py:626
  370.3 44.6 %collective-permute-start.61 = (bf16[512,1152]{1,0:T(8,128)(2,1)S(1)}, bf16[512,1152]{1,0:T(8,128)(2,1)S(1)}, u32[]{:S(2)}, u32[]{:S(2)}) collective-permute-start(bf16[512,1152]{1,0:T(8,128)(2,1)S(1)} %dynamic-slice_bitcast_fusion.2), channel_id=1, source_target_pairs={{0,16},{8,24},{16,0},{24,8},{1,17},{9,25},{17,1},{25,9},{2,18},{10... | collective-permute-start | bytes 3538952 | tf_op jit(solution)/shard_map/ppermute | solution.py:635
  405.6 52.5 %collective-permute-start.55 = (bf16[512,2304]{1,0:T(8,128)(2,1)}, bf16[512,2304]{1,0:T(8,128)(2,1)}, u32[]{:S(2)}, u32[]{:S(2)}) collective-permute-start(bf16[512,2304]{1,0:T(8,128)(2,1)} %grad_in.2), channel_id=1, source_target_pairs={{0,16},{8,24},{16,0},{24,8},{1,17},{9,25},{17,1},{25,9},{2,18},{10... | collective-permute-start | bytes 7077896 | tf_op jit(solution)/shard_map/ppermute | solution.py:635
  412.9 50.3 %collective-permute-start.54 = (bf16[288,1536]{1,0:T(8,128)(2,1)}, bf16[288,1536]{1,0:T(8,128)(2,1)}, u32[]{:S(2)}, u32[]{:S(2)}) collective-permute-start(bf16[288,1536]{1,0:T(8,128)(2,1)} %get-tuple-element.197), channel_id=1, source_target_pairs={{0,1},{1,3},{2,0},{3,5},{4,2},{5,7},{6,4},{7,6},{8,10},{9,8},{10,1... | collective-permute-start | bytes 2654216 | tf_op jit(solution)/shard_map/ppermute | solution.py:629
  414.3 48.9 %collective-permute-start.53 = (bf16[288,1536]{1,0:T(8,128)(2,1)}, bf16[288,1536]{1,0:T(8,128)(2,1)}, u32[]{:S(2)}, u32[]{:S(2)}) collective-permute-start(bf16[288,1536]{1,0:T(8,128)(2,1)} %get-tuple-element.198), channel_id=1, source_target_pairs={{0,2},{1,0},{2,4},{3,1},{4,6},{5,3},{6,7},{7,5},{8,9},{9,11},{10,8... | collective-permute-start | bytes 2654216 | tf_op jit(solution)/shard_map/ppermute | solution.py:626
  418.7 30.9 %collective-permute-start.70 = (bf16[288,1920]{1,0:T(8,128)(2,1)}, bf16[288,1920]{1,0:T(8,128)(2,1)}, u32[]{:S(2)}, u32[]{:S(2)}) collective-permute-start(bf16[288,1920]{1,0:T(8,128)(2,1)} %fusion.3), channel_id=1, source_target_pairs={{0,2},{1,0},{2,4},{3,1},{4,6},{5,3},{6,7},{7,5},{8,9},{9,11},{10,8... | collective-permute-start | bytes 3317768 | tf_op jit(solution)/shard_map/ppermute | solution.py:626
  422.5 47.0 %collective-permute-start.63 = (bf16[256,2304]{1,0:T(8,128)(2,1)}, bf16[256,2304]{1,0:T(8,128)(2,1)}, u32[]{:S(2)}, u32[]{:S(2)}) collective-permute-start(bf16[256,2304]{1,0:T(8,128)(2,1)} %dynamic-slice_bitcast_fusion.1), channel_id=1, source_target_pairs={{0,8},{8,0},{16,24},{24,16},{1,9},{9,1},{17,25},{25,17},{2,10},{10... | collective-permute-start | bytes 3538952 | tf_op jit(solution)/shard_map/ppermute | solution.py:632
  456.0 37.4 %collective-permute-start.71 = (f16[288,1920]{1,0:T(8,128)(2,1)S(1)}, f16[288,1920]{1,0:T(8,128)(2,1)}, u32[]{:S(2)}, u32[]{:S(2)}) collective-permute-start(f16[288,1920]{1,0:T(8,128)(2,1)S(1)} %divide_convert_fusion), channel_id=1, source_target_pairs={{0,16},{8,24},{16,0},{24,8},{1,17},{9,25},{17,1},{25,9},{2,18},{10... | collective-permute-start | bytes 3317768 | tf_op jit(solution)/shard_map/ppermute | solution.py:635
  463.4 30.0 %collective-permute-start.62 = (f32[256,2304]{1,0:T(8,128)S(1)}, f32[256,2304]{1,0:T(8,128)S(1)}, u32[]{:S(2)}, u32[]{:S(2)}) collective-permute-start(f32[256,2304]{1,0:T(8,128)S(1)} %dynamic-slice_bitcast_fusion), channel_id=1, source_target_pairs={{0,8},{8,0},{16,24},{24,16},{1,9},{9,1},{17,25},{25,17},{2,10},{10... | collective-permute-start | bytes 7077896 | tf_op jit(solution)/shard_map/ppermute | solution.py:632
  484.2 46.7 %collective-permute-start.73 = (f32[288,1920]{1,0:T(8,128)}, f32[288,1920]{1,0:T(8,128)}, u32[]{:S(2)}, u32[]{:S(2)}) collective-permute-start(f32[288,1920]{1,0:T(8,128)} %convert_multiply_fusion.1.refs_0_), channel_id=1, source_target_pairs={{0,8},{8,0},{16,24},{24,16},{1,9},{9,1},{17,25},{25,17},{2,10},{10... | collective-permute-start | bytes 6635528 | tf_op jit(solution)/shard_map/ppermute | solution.py:632
  (107 other events, 1922.9 us)
